TPU v7x, 256 devices: a whole 4x4x8 slice. The times are simulated.
256 devices in a mesh: row: 8 (over z), col: 32 (over x, y, core).
Axes of the slice: x: 4, y: 4, z: 8, core: 2. Of those that a mesh axis runs over, the one named last changes fastest.
Arguments:
- activations: bfloat16 [131072, 8192], P(('row', 'col')), may hold values from -24 to 24
- kv_grads: bfloat16 [131072, 512], P(('row', 'col')), may hold values from -24 to 24
- row_state: float32 [512], P('row'), may hold values from 0.01 to 1
- col_state: float32 [2, 8192], P(None, 'col'), may hold values from 0.01 to 1
Outputs:
- direction: float32 [512, 8192], P('row', 'col')
- row_new: float32 [512], P('row')
- col_new: float32 [2, 8192], P(None, 'col')
All inputs are finite; a program needn't handle non-finite values.
Results may differ from a plain program's by a relative error of at most 0.0003.
Values sent between devices are 32-bit elements; how exact they have to be, the bound alone decides.
No kernel may reach another device: no remote copies, remote signals or barrier semaphores. Data moves between devices by JAX's collectives and lax.ppermute only.
A program may use at most 256 MiB of HBM per device.

v0:
```python
import jax
import jax.numpy as jnp
from jax import lax
from jax.sharding import PartitionSpec as P

D = 8192
HEAD_DIM = 256


DECAY_RATE = 1.0 - 8.0 ** (-0.8)
EPSILON = 1e-30
CLIP_LIMIT = 1.0
HIGHEST = lax.Precision.HIGHEST


def on_device(activations, kv_grads, row_state, col_state):
    tok_rows = activations.shape[0]
    row_width = row_state.shape[0]
    row_count = lax.axis_size("row")
    col_count = lax.axis_size("col")
    contract = (((0,), (0,)), ((), ()))
    partial_value = lax.psum_scatter(
        lax.dot_general(activations, kv_grads, contract, preferred_element_type=jnp.float32),
        "col",
        scatter_dimension=0,
        tiled=True,
    )
    grad_tile = lax.psum_scatter(partial_value, "row", scatter_dimension=1, tiled=True).T
    grad = grad_tile * (tok_rows * row_count * col_count) ** (-0.5)
    squares = grad * grad + EPSILON
    global_rows = lax.axis_index("row") * row_width + jnp.arange(row_width, dtype=jnp.int32)
    members = global_rows % 2
    onehot = (members[:, None] == jnp.arange(2, dtype=jnp.int32)[None, :]).astype(jnp.float32)
    col_squares = jnp.dot(onehot.T, squares, precision=HIGHEST)
    row_sum = lax.psum(jnp.sum(squares, axis=1), "col")
    col_sum = lax.psum(col_squares, "row")
    row_new = DECAY_RATE * row_state + (1.0 - DECAY_RATE) * (row_sum / D)
    col_new = DECAY_RATE * col_state + (1.0 - DECAY_RATE) * (col_sum / HEAD_DIM)
    second_moment = row_new[:, None] * jnp.dot(onehot, col_new, precision=HIGHEST)
    raw_step = grad / jnp.sqrt(second_moment)
    clip_terms = jnp.dot(jnp.sum(raw_step * raw_step, axis=1), onehot, precision=HIGHEST)
    clip_total = lax.psum(clip_terms, ("row", "col"))
    root_mean = jnp.sqrt(clip_total / (HEAD_DIM * D))
    limiter = jnp.maximum(1.0, root_mean / CLIP_LIMIT)
    direction = raw_step / jnp.dot(onehot, limiter, precision=HIGHEST)[:, None]
    return (direction, row_new, col_new)


def solution(mesh):
    placed = (P(("row", "col"), None), P(("row", "col"), None), P("row"), P(None, "col"))
    return jax.shard_map(
        on_device,
        mesh=mesh,
        in_specs=placed,
        out_specs=(P("row", "col"), P("row"), P(None, "col")),
        check_vma=False,
    )
```

profile of v0, /device:TPU:1, one launch (start us, length us, event | category | flops | bytes accessed | tf_op | source)
XLA Modules:
  0.0 348.1 jit_solution(7802952189324154153)
XLA Ops:
  7.2 0.0 copy-start
  7.2 0.0 reduce-scatter.5.cloned.1.call-start
  7.2 1.0 copy-done
  8.2 11.7 %fusion.21 = f32[8192,512]{1,0:T(8,128)} fusion(bf16[512,8192]{1,0:T(8,128)(2,1)} %param.4, bf16[512,512]{1,0:T(8,128)(2,1)S(1)} %copy-done), kind=kOutput, calls=%fused_computation.35 | convolution fusion | flops 4294967296 | bytes 25690112 | tf_op jit(solution)/shard_map/dot_general | solution.py:23
  19.9 0.0 copy-start.2
  19.9 0.0 copy-start.4
  19.9 0.0 reduce-scatter.5.cloned.1.call-update
  19.9 0.0 reduce-scatter.7.cloned.1.call-start
  20.0 125.6 %reduce-scatter.5.cloned.1.call-done = f32[256,512]{1,0:T(8,128)} async-done(((f32[8192,512]{1,0:T(8,128)}), f32[256,512]{1,0:T(8,128)}) %reduce-scatter.5.cloned.1.call-update) | async-done | bytes 524304 | tf_op jit(solution)/shard_map/reduce_scatter | solution.py:22
  145.5 2.0 copy.10
  147.5 0.0 reduce-scatter.7.cloned.1.call-update
  147.6 33.7 %reduce-scatter.7.cloned.1.call-done = f32[64,256]{1,0:T(8,128)} async-done(((f32[512,256]{1,0:T(8,128)}), f32[64,256]{1,0:T(8,128)}) %reduce-scatter.7.cloned.1.call-update) | async-done | bytes 65552
  181.3 1.1 fusion.3
  182.4 12.0 %psum.22 = f32[2,256]{1,0:T(2,128)S(1)} all-reduce(f32[2,256]{1,0:T(2,128)S(1)} %fusion.3), channel_id=1, replica_groups=mesh['row'=8,'col'=32] {'row'}, use_global_device_ids=true, to_apply=%region_4.5 | all-reduce | flops 512 | bytes 4096 | tf_op jit(solution)/shard_map/psum | solution.py:36
  194.3 0.9 fusion.4
  195.3 71.0 %psum.21 = f32[64]{0:T(128)S(1)} all-reduce(f32[64]{0:T(128)S(1)} %fusion.4), channel_id=1, replica_groups=mesh['row'=8,'col'=32] {'col'}, use_global_device_ids=true, to_apply=%region_3.4 | all-reduce | flops 64 | bytes 512 | tf_op jit(solution)/shard_map/psum | solution.py:35
  266.3 0.0 copy-done.2
  266.3 0.0 copy-done.4
  266.3 0.0 copy-start.1
  266.3 0.0 copy-start.3
  266.3 1.2 multiply_reduce_fusion
  267.5 0.2 convolution_bitcast_fusion.1
  267.7 72.6 %psum.23 = f32[2]{0:T(128)S(1)} all-reduce(f32[2]{0:T(128)S(1)} %convolution_bitcast_fusion.1), channel_id=1, replica_groups=mesh['row'=8,'col'=32] {'row','col'}, use_global_device_ids=true, to_apply=%region_6.7 | all-reduce | flops 2 | bytes 16 | tf_op jit(solution)/shard_map/psum | solution.py:42
  340.3 0.2 convolution_bitcast_fusion
  340.5 0.8 broadcast_divide_fusion
  341.3 0.0 copy-done.1
  341.3 0.0 copy-done.3
  (3 shorter events, 0.0 us)
Async XLA Ops:
  7.2 1.0 copy-start
  7.2 138.3 %reduce-scatter.5.cloned.1.call-start = ((), (), s32[]{:S(2)}) async-start(), calls=%async_computation.2 | async-start | bytes 17301504 | tf_op jit(solution)/shard_map/reduce_scatter | solution.py:22
  19.9 246.4 %copy-start.2 = (f32[2,256]{1,0:T(2,128)S(1)}, f32[2,256]{1,0:T(2,128)}, u32[]{:S(2)}) copy-start(f32[2,256]{1,0:T(2,128)} %param.7) | copy-start | bytes 6148
  19.9 246.4 %copy-start.4 = (f32[64]{0:T(128)S(1)}, f32[64]{0:T(128)}, u32[]{:S(2)}) copy-start(f32[64]{0:T(128)} %param.6) | copy-start | bytes 772
  19.9 161.4 %reduce-scatter.7.cloned.1.call-start = ((), (), s32[]{:S(2)}) async-start(), calls=%async_computation.3 | async-start | bytes 589824
  266.3 75.0 %copy-start.1 = (f32[2,256]{1,0:T(2,128)}, f32[2,256]{1,0:T(2,128)S(1)}, u32[]{:S(2)}) copy-start(f32[2,256]{1,0:T(2,128)S(1)} %multiply_add_fusion.2) | copy-start | bytes 6148
  266.3 75.0 %copy-start.3 = (f32[64]{0:T(128)}, f32[64]{0:T(128)S(1)}, u32[]{:S(2)}) copy-start(f32[64]{0:T(128)S(1)} %multiply_add_fusion.3) | copy-start | bytes 772
Sparse Core Ops, SparseCore 0:
  20.0 125.4 reduce-scatter.4
  148.0 33.2 reduce-scatter.6
where the time goes:
time: 349 us; the launch traced here: 348 us
  waiting for transfers between devices  159 us (46%)
  blocking collectives  156 us (45%)
  matrix products  14.3 us (4%)
  between operations  14.1 us (4%)
    reduce_scatter x1, waiting for transfers between devices, on_device(): lax.psum_scatter(lax.dot_general(activations, kv_grads, contract, preferr...  126 us
    psum x1, blocking collectives, on_device(): clip_total = lax.psum(clip_terms, ('row', 'col'))  72.6 us
    psum x1, blocking collectives, on_device(): row_sum = lax.psum(jnp.sum(squares, axis=1), 'col')  71 us
    unnamed x3, waiting for transfers between devices  33.7 us
    psum x1, blocking collectives, on_device(): col_sum = lax.psum(col_squares, 'row')  12 us
    dot_general x1, matrix products, on_device(): lax.dot_general(activations, kv_grads, contract, preferred_element_type=j...  11.7 us
  transfers between devices with their start and end apart: 2, of which 2 were waited for; matrix products, arithmetic and copies ran while one was open for 0% of the time, Pallas kernels for 0%

commit v1 on v0

v1 whole, which is shorter than its diff:
```python
import functools
import jax
import jax.numpy as jnp
import numpy as np
from jax import lax
from jax.experimental import pallas as pl
from jax.experimental.pallas import tpu as pltpu
from jax.sharding import PartitionSpec as P

D = 8192
HEAD_DIM = 256
DECAY_RATE = 1.0 - 8.0 ** (-0.8)
EPSILON = 1e-30
CLIP_LIMIT = 1.0

RING4 = ((1, 3), (3, 1))
RING8 = (1, 2, 6)
XYZ = "xyzxyzz"
YZX = "yzxyzxz"
ZXY = "zxyzxyz"
PARTS = (
    (0, 8, 0, 384, 0, XYZ),
    (8, 8, 0, 384, 1, XYZ),
    (16, 8, 0, 384, 0, YZX),
    (24, 8, 0, 384, 1, YZX),
    (0, 16, 384, 128, 0, ZXY),
    (16, 16, 384, 128, 1, ZXY),
)


def masks4(kind):
    first, second = RING4[kind]
    return [0, second, first, first ^ second]


def masks8():
    a, b, c = RING8
    return [i * a ^ j * b ^ k * c for i in (0, 1) for j in (0, 1) for k in (0, 1)]


def col_perm(axis, mask):
    if axis == "c":
        return [(i, i ^ 1) for i in range(32)]
    shift = 3 if axis == "x" else 1
    return [(i, i ^ (mask << shift)) for i in range(32)]


def row_perm(mask, kind):
    return [(i, (((i + kind) % 8) ^ mask) + 8 * kind - kind) for i in range(8)]


def row_pairs(mask, kind):
    return [(a, b % 8) for a, b in row_perm(mask, kind)]


def partial_kernel(count, places, x_ref, y_ref, *refs):
    got, out, acc = refs[:count], refs[count:-1], refs[-1]
    acc[...] = lax.dot_general(
        x_ref[...], y_ref[...], (((0,), (0,)), ((), ())), preferred_element_type=jnp.float32
    )
    for p, (row, rows, lane, lanes, kind, _) in enumerate(PARTS):
        for slot in range(8):
            start = pl.multiple_of(places[32 + kind * 8 + slot] * 32 + row, 8)
            value = acc[pl.ds(start, rows), lane : lane + lanes]
            if count:
                value = value + got[p][0, slot]
            out[p][0, slot] = value


def partial(places, x, y, got):
    shapes = [(16, 8, rows, lanes) for _, rows, _, lanes, _, _ in PARTS]
    blocks = []

    def spec(part):
        shape = shapes[part]
        kind = PARTS[part][4]
        return pl.BlockSpec((1,) + shape[1:], lambda s, places: (places[48 + 16 * kind + s], 0, 0, 0))

    specs = [spec(p) for p in range(len(PARTS))]
    return pl.pallas_call(
        functools.partial(partial_kernel, len(got)),
        grid_spec=pltpu.PrefetchScalarGridSpec(
            num_scalar_prefetch=1,
            grid=(16,),
            in_specs=[
                pl.BlockSpec((512, 256), lambda s, places: (0, places[s])),
                pl.BlockSpec((512, 512), lambda s, places: (0, 0)),
            ]
            + (specs if got else []),
            out_specs=specs,
            scratch_shapes=[pltpu.VMEM((256, 512), jnp.float32)],
        ),
        out_shape=[jax.ShapeDtypeStruct(s, jnp.float32) for s in shapes],
        compiler_params=pltpu.CompilerParams(vmem_limit_bytes=24 * 1024 * 1024),
        cost_estimate=pl.CostEstimate(
            flops=2 * 512 * 512 * 4096, bytes_accessed=13_000_000 + 8_400_000 * (len(got) > 0), transcendentals=0
        ),
    )(places, x, y, *got)


def reduce_parts(parts):
    values = []
    dims = []
    for part, (_, rows, _, lanes, _, _) in zip(parts, PARTS):
        values.append(part.reshape((2, 2, 2, 2, 2, 2, 2, rows, lanes)))
        dims.append([("x", 0), ("x", 1), ("y", 0), ("y", 1), ("z", 0), ("z", 1), ("z", 2)])
    done = [{"x": 0, "y": 0, "z": 0} for _ in PARTS]
    for step in range(7):
        sent = []
        for p, (_, _, _, _, kind, order) in enumerate(PARTS):
            axis = order[step]
            at = dims[p].index((axis, done[p][axis]))
            send = lax.index_in_dim(values[p], 1, at, keepdims=False)
            if axis == "z":
                got = lax.ppermute(send, "row", row_pairs(RING8[done[p][axis]], kind))
            else:
                got = lax.ppermute(send, "col", col_perm(axis, RING4[kind][done[p][axis]]))
            sent.append((at, got))
        for p, (at, got) in enumerate(sent):
            axis = PARTS[p][5][step]
            values[p] = lax.index_in_dim(values[p], 0, at, keepdims=False) + got
            dims[p].pop(at)
            done[p][axis] += 1
    return values


def col_total(value):
    value = value + lax.ppermute(value, "col", col_perm("c", 1))
    for axis in "xy":
        value = value + sum(lax.ppermute(value, "col", col_perm(axis, m)) for m in (1, 2, 3))
    return value


def on_device(activations, kv_grads, row_state, col_state):
    z = lax.axis_index("row").astype(jnp.int32)
    col = lax.axis_index("col").astype(jnp.int32)
    xi, yi, ci = col // 8, (col // 2) % 4, col % 2

    step_masks = [(a, b) for a in range(4) for b in range(4)]
    mx = jnp.asarray(np.array([a for a, _ in step_masks], np.int32))
    my = jnp.asarray(np.array([b for _, b in step_masks], np.int32))
    z0 = z ^ jnp.asarray(np.array(masks8(), np.int32))
    z1 = ((((z + 1) % 8) ^ jnp.asarray(np.array(masks8(), np.int32))) + 7) % 8
    slots = [
        np.array([masks4(kind).index(a) * 4 + masks4(kind).index(b) for a, b in step_masks], np.int32)
        for kind in (0, 1)
    ]
    blocks = ((xi ^ mx) * 4 + (yi ^ my)) * 2
    rest = [jnp.zeros((16,), jnp.int32), z0, z1, jnp.asarray(slots[0]), jnp.asarray(slots[1])]
    far = jnp.concatenate([blocks + (1 - ci)] + rest)
    near = jnp.concatenate([blocks + ci] + rest)

    away = partial(far, activations, kv_grads, [])
    came = [lax.ppermute(a, "col", col_perm("c", 1)) for a in away]
    parts = reduce_parts(partial(near, activations, kv_grads, came))
    wide = jnp.concatenate(parts[:4], axis=0)
    narrow = jnp.concatenate(parts[4:], axis=0)
    grad = jnp.concatenate([wide, narrow], axis=1) * (512 * 256) ** (-0.5)

    square = grad * grad
    squares = square + EPSILON
    even = lax.broadcasted_iota(jnp.int32, (1, 512), 1) % 2 == 0
    col_sum = jnp.stack(
        [jnp.sum(jnp.where(even, squares, 0.0), axis=1), jnp.sum(jnp.where(even, 0.0, squares), axis=1)]
    )
    col_old = lax.dynamic_slice_in_dim(col_state, z * 32, 32, axis=1)
    col_part = DECAY_RATE * col_old + (1.0 - DECAY_RATE) * (col_sum / HEAD_DIM)
    of_row = jnp.where(even, col_part[0][:, None], col_part[1][:, None])
    stats = jnp.stack([jnp.sum(squares, axis=0), jnp.sum(square / of_row, axis=0)])
    stats = col_total(stats.reshape(8, 128))

    tile = grad.reshape(2, 16, 8, 64).transpose(2, 1, 0, 3).reshape(8, 16, 128)
    small = jnp.concatenate([col_part.reshape(64), row_state, jnp.zeros((7 * 128,), jnp.float32)]).reshape(8, 128)
    common = jnp.concatenate([stats, small], axis=0)
    load = jnp.concatenate([tile, jnp.broadcast_to(common, (8, 16, 128))], axis=1)
    load = lax.all_to_all(load, "row", 0, 0, tiled=True)

    grad = load[:, :16].reshape(8, 16, 2, 64).transpose(3, 0, 2, 1).reshape(64, 256)
    total = jnp.sum(load[:, 16:24], axis=0).reshape(2, 512)
    col_new = load[:, 24, :64].reshape(8, 2, 32).transpose(1, 0, 2).reshape(2, 256)
    row_old = load[:, 24, 64:].reshape(512)
    row_all = DECAY_RATE * row_old + (1.0 - DECAY_RATE) * (total[0] / D)
    per_row = total[1] / row_all
    clip = jnp.sum(per_row.reshape(256, 2), axis=0)
    limiter = jnp.maximum(1.0, jnp.sqrt(clip / (HEAD_DIM * D)) / CLIP_LIMIT)
    row_new = lax.dynamic_slice_in_dim(row_all, z * 64, 64)
    key_row = lax.broadcasted_iota(jnp.int32, (64, 1), 0) % 2 == 0
    moment = row_new[:, None] * jnp.where(key_row, col_new[0][None, :], col_new[1][None, :])
    direction = grad / jnp.sqrt(moment) / jnp.where(key_row, limiter[0], limiter[1])
    return (direction, row_new, col_new)


def solution(mesh):
    placed = (P(("row", "col"), None), P(("row", "col"), None), P("row"), P(None, "col"))
    return jax.shard_map(
        on_device,
        mesh=mesh,
        in_specs=placed,
        out_specs=(P("row", "col"), P("row"), P(None, "col")),
        check_vma=False,
    )
```

time: 349 us -> 211 us (0.60)
  blocking collectives: 156 us -> 0 us
  starting transfers between devices: 0.08 us -> 86.2 us
  waiting for transfers between devices: 159 us -> 78 us
  Pallas kernels: 0 us -> 23.3 us
  matrix products: 14.3 us -> 0 us
  between operations: 14.1 us -> 1.53 us
  local copies, waits for them, and re-layouts: 3.05 us -> 13.4 us
    psum x3 -> x0, blocking collectives: 156 us -> none  [the longest x1 72.6 us: on_device(): clip_total = lax.psum(clip_terms, ('row', 'col'))]
    reduce_scatter x1 -> x0, waiting for transfers between devices: 126 us -> none  [on_device(): lax.psum_scatter(lax.dot_general(activations, kv_grads, contract, preferr...]
    ppermute x0 -> x55, starting transfers between devices: none -> 82.8 us  [the longest x18 28.8 us: reduce_parts(): got = lax.ppermute(send, 'row', row_pairs(RING8[done[p][axis]], kind))]
    ppermute x0 -> x55, waiting for transfers between devices: none -> 70.2 us  [the longest x18 30.7 us: reduce_parts(): got = lax.ppermute(send, 'row', row_pairs(RING8[done[p][axis]], kind))]
    unnamed x3 -> x0, waiting for transfers between devices: 33.7 us -> none
    pallas_call x0 -> x2, Pallas kernels: none -> 23.3 us  [partial(): pl.pallas_call(functools.partial(partial_kernel, len(got)), grid_spec=plt...]
    dot_general x5 -> x0, matrix products: 14.3 us -> none  [the longest x1 11.7 us: on_device(): lax.dot_general(activations, kv_grads, contract, preferred_element_type=j...]
    all_to_all x0 -> x1, waiting for transfers between devices: none -> 7.82 us  [on_device(): load = lax.all_to_all(load, 'row', 0, 0, tiled=True)]
  transfers between devices with their start and end apart: 2 -> 56, of which waited for: 2 -> 28; matrix products, arithmetic and copies ran while one was open for 0% -> 1% of each run, Pallas kernels for 0% -> 0%
where the time goes in v1:
time: 211 us; the launch traced here: 208 us
  starting transfers between devices  86.2 us (41%)
  waiting for transfers between devices  78 us (37%)
  Pallas kernels  23.3 us (11%)
  local copies, waits for them, and re-layouts  13.4 us (6%)
  other arithmetic  5.19 us (2%)
    ppermute x18, waiting for transfers between devices, reduce_parts(): got = lax.ppermute(send, 'row', row_pairs(RING8[done[p][axis]], kind))  30.7 us
    ppermute x18, starting transfers between devices, reduce_parts(): got = lax.ppermute(send, 'row', row_pairs(RING8[done[p][axis]], kind))  28.8 us
    ppermute x24, waiting for transfers between devices, reduce_parts(): got = lax.ppermute(send, 'col', col_perm(axis, RING4[kind][done[p][axis]]))  23.4 us
    pallas_call x2, Pallas kernels, partial(): pl.pallas_call(functools.partial(partial_kernel, len(got)), grid_spec=plt...  23.3 us
    ppermute x1, starting transfers between devices, col_total(): value = value + lax.ppermute(value, 'col', col_perm('c', 1))  21.3 us
    ppermute x24, starting transfers between devices, reduce_parts(): got = lax.ppermute(send, 'col', col_perm(axis, RING4[kind][done[p][axis]]))  20.4 us
    ppermute x6, waiting for transfers between devices, on_device(): came = [lax.ppermute(a, 'col', col_perm('c', 1)) for a in away]  11.7 us
    unnamed x23, local copies, waits for them, and re-layouts  8.78 us
  transfers between devices with their start and end apart: 56, of which 28 were waited for; matrix products, arithmetic and copies ran while one was open for 1% of the time, Pallas kernels for 0%

profile of v1, /device:TPU:1, one launch (start us, length us, event | category | flops | bytes accessed | tf_op | source)
XLA Modules:
  0.0 207.6 jit_solution(13291930709119315470)
XLA Ops:
  2.8 3.4 %copy-done = bf16[512,8192]{1,0:T(8,128)(2,1)S(1)} copy-done((bf16[512,8192]{1,0:T(8,128)(2,1)S(1)}, bf16[512,8192]{1,0:T(8,128)(2,1)}, u32[]{:S(2)}) %copy-start) | copy-done | bytes 8388632
  7.2 10.3 %shard_map.121 = (f32[16,8,8,384]{3,2,1,0:T(8,128)}, f32[16,8,8,384]{3,2,1,0:T(8,128)}, f32[16,8,8,384]{3,2,1,0:T(8,128)}, f32[16,8,8,384]{3,2,1,0:T(8,128)}, f3...) custom-call(s32[80]{0:T(128)S(1)} %concatenate.25.places, bf16[512,8192]{1,0:T(8,128)(2,1)S(1)} %copy-done, ...), custom_call_target="tpu_custom_call" | custom-call | flops 2147483648 | bytes 13000000 | tf_op jit(solution)/shard_map/pallas_call | solution.py:80
  17.6 3.2 %collective-permute-start.4 = (f32[16,8,16,128]{3,2,1,0:T(8,128)S(1)}, f32[16,8,16,128]{3,2,1,0:T(8,128)S(1)}, u32[]{:S(2)}, u32[]{:S(2)}) collective-permute-start(f32[16,8,16,128]{3,2,1,0:T(8,128)S(1)} %get-tuple-element.19), channel_id=1, source_target_pairs={{0,1},{1,0},{2,3},{3,2},{4,5},{5,4},{6,7},{7,6},{8,9},{9,8},{10,11... | collective-permute-start | bytes 3145736 | tf_op jit(solution)/shard_map/ppermute | solution.py:154
  21.8 2.0 collective-permute-done.4.refs_4_
  24.3 9.6 %collective-permute-done.5.refs_5_ = f32[16,8,16,128]{3,2,1,0:T(8,128)} collective-permute-done((f32[16,8,16,128]{3,2,1,0:T(8,128)}, f32[16,8,16,128]{3,2,1,0:T(8,128)}, u32[]{:S(2)}, u32[]{:S(2)}) %collective-permute-start.5) | collective-permute-done | bytes 1048608 | tf_op jit(solution)/shard_map/ppermute | solution.py:154
  34.0 3.4 %copy-done.1 = bf16[512,8192]{1,0:T(8,128)(2,1)S(1)} copy-done((bf16[512,8192]{1,0:T(8,128)(2,1)S(1)}, bf16[512,8192]{1,0:T(8,128)(2,1)}, u32[]{:S(2)}) %copy-start.1) | copy-done | bytes 8388632
  37.3 12.9 %shard_map.122 = (f32[16,8,8,384]{3,2,1,0:T(8,128)S(1)}, f32[16,8,8,384]{3,2,1,0:T(8,128)S(1)}, f32[16,8,8,384]{3,2,1,0:T(8,128)S(1)}, f32[16,8,8,384]{3,2,1,0:T...) custom-call(s32[80]{0:T(128)S(1)} %concatenate.24.places, bf16[512,8192]{1,0:T(8,128)(2,1)S(1)} %copy-done.1, ...), custom_call_target="tpu_custom_call" | custom-call | flops 2147483648 | bytes 21400000 | tf_op jit(solution)/shard_map/pallas_call | solution.py:80
  50.8 1.4 collective-permute-start.13
  52.4 1.4 collective-permute-start.20
  53.9 1.7 collective-permute-start.34
  55.8 4.8 %collective-permute-start.41 = (f32[2,2,2,2,2,2,16,128]{7,6,5,3,1,4,2,0:T(8,128)S(1)}, f32[2,2,2,2,2,2,16,128]{7,6,5,3,1,4,2,0:T(8,128)S(1)}, u32[]{:S(2)}, u32[]{:S(2)}) collective-permute-start(f32[2,2,2,2,2,2,16,128]{7,6,5,3,1,4,2,0:T(8,128)S(1)} %bitcast.284), channel_id=1, source_target_pairs={{0,224},{32,64},{64,32},{96,128},{128,96},{160,192},{192,160},{224... | collective-permute-start | bytes 1572872 | tf_op jit(solution)/shard_map/ppermute | solution.py:115
  60.7 5.8 %collective-permute-done.34 = f32[2,2,2,2,2,2,16,128]{7,6,5,3,1,4,2,0:T(8,128)S(1)} collective-permute-done((f32[2,2,2,2,2,2,16,128]{7,6,5,3,1,4,2,0:T(8,128)S(1)}, f32[2,2,2,2,2,2,16,128]{7,6,5,3,1,4,2,0:T(8,128)S(1)}, u32[]{:S(2)}, u32[]{:S(2)}) %collective-permute-start.34) | collective-permute-done | bytes 524320 | tf_op jit(solution)/shard_map/ppermute | solution.py:115
  66.6 1.9 collective-permute-start.27
  68.6 2.7 %collective-permute-done.41 = f32[2,2,2,2,2,2,16,128]{7,6,5,3,1,4,2,0:T(8,128)S(1)} collective-permute-done((f32[2,2,2,2,2,2,16,128]{7,6,5,3,1,4,2,0:T(8,128)S(1)}, f32[2,2,2,2,2,2,16,128]{7,6,5,3,1,4,2,0:T(8,128)S(1)}, u32[]{:S(2)}, u32[]{:S(2)}) %collective-permute-start.41) | collective-permute-done | bytes 524320 | tf_op jit(solution)/shard_map/ppermute | solution.py:115
  71.7 5.2 %collective-permute-done.35 = f32[2,2,2,2,2,16,128]{6,5,4,2,0,3,1:T(8,128)S(1)} collective-permute-done((f32[2,2,2,2,2,16,128]{6,5,4,2,0,3,1:T(8,128)S(1)}, f32[2,2,2,2,2,16,128]{6,5,4,2,0,3,1:T(8,128)S(1)}, u32[]{:S(2)}, u32[]{:S(2)}) %collective-permute-start.35) | collective-permute-done | bytes 262176 | tf_op jit(solution)/shard_map/ppermute | solution.py:117
  77.9 5.8 %collective-permute-done.42 = f32[2,2,2,2,2,16,128]{6,5,4,2,0,3,1:T(8,128)S(1)} collective-permute-done((f32[2,2,2,2,2,16,128]{6,5,4,2,0,3,1:T(8,128)S(1)}, f32[2,2,2,2,2,16,128]{6,5,4,2,0,3,1:T(8,128)S(1)}, u32[]{:S(2)}, u32[]{:S(2)}) %collective-permute-start.42) | collective-permute-done | bytes 262176 | tf_op jit(solution)/shard_map/ppermute | solution.py:117
  83.7 2.7 %collective-permute-start.43 = (f32[2,2,2,2,16,128]{5,4,3,1,0,2:T(8,128)S(1)}, f32[2,2,2,2,16,128]{5,4,3,1,0,2:T(8,128)S(1)}, u32[]{:S(2)}, u32[]{:S(2)}) collective-permute-start(f32[2,2,2,2,16,128]{5,4,3,1,0,2:T(8,128)S(1)} %slice_bitcast_fusion.20), channel_id=1, source_target_pairs={{0,6},{1,7},{2,4},{3,5},{4,2},{5,3},{6,0},{7,1},{8,14},{9,15},{10,... | collective-permute-start | bytes 393224 | tf_op jit(solution)/shard_map/ppermute | solution.py:117
  88.4 3.3 %collective-permute-start.28 = (f32[2,2,2,2,2,8,384]{6,5,4,1,3,2,0:T(8,128)S(1)}, f32[2,2,2,2,2,8,384]{6,5,4,1,3,2,0:T(8,128)S(1)}, u32[]{:S(2)}, u32[]{:S(2)}) collective-permute-start(f32[2,2,2,2,2,8,384]{6,5,4,1,3,2,0:T(8,128)S(1)} %slice_bitcast_fusion), channel_id=1, source_target_pairs={{0,224},{32,64},{64,32},{96,128},{128,96},{160,192},{192,160},{224... | collective-permute-start | bytes 1179656 | tf_op jit(solution)/shard_map/ppermute | solution.py:115
  91.9 6.1 %collective-permute-done.37 = f32[2,2,2,16,128]{4,3,2,1,0:T(8,128)S(1)} collective-permute-done((f32[2,2,2,16,128]{4,3,2,1,0:T(8,128)S(1)}, f32[2,2,2,16,128]{4,3,2,1,0:T(8,128)S(1)}, u32[]{:S(2)}, u32[]{:S(2)}) %collective-permute-start.37) | collective-permute-done | bytes 65568 | tf_op jit(solution)/shard_map/ppermute | solution.py:115
  98.0 5.0 %collective-permute-done.44 = f32[2,2,2,16,128]{4,3,2,1,0:T(8,128)S(1)} collective-permute-done((f32[2,2,2,16,128]{4,3,2,1,0:T(8,128)S(1)}, f32[2,2,2,16,128]{4,3,2,1,0:T(8,128)S(1)}, u32[]{:S(2)}, u32[]{:S(2)}) %collective-permute-start.44) | collective-permute-done | bytes 65568 | tf_op jit(solution)/shard_map/ppermute | solution.py:115
  104.0 3.1 %collective-permute-done.38 = f32[2,2,16,128]{3,2,1,0:T(8,128)S(1)} collective-permute-done((f32[2,2,16,128]{3,2,1,0:T(8,128)S(1)}, f32[2,2,16,128]{3,2,1,0:T(8,128)S(1)}, u32[]{:S(2)}, u32[]{:S(2)}) %collective-permute-start.38) | collective-permute-done | bytes 32800 | tf_op jit(solution)/shard_map/ppermute | solution.py:117
  107.1 2.7 %collective-permute-done.45 = f32[2,2,16,128]{3,2,1,0:T(8,128)S(1)} collective-permute-done((f32[2,2,16,128]{3,2,1,0:T(8,128)S(1)}, f32[2,2,16,128]{3,2,1,0:T(8,128)S(1)}, u32[]{:S(2)}, u32[]{:S(2)}) %collective-permute-start.45) | collective-permute-done | bytes 32800 | tf_op jit(solution)/shard_map/ppermute | solution.py:117
  109.8 1.9 collective-permute-start.39
  111.7 1.9 collective-permute-done.39
  113.6 2.6 %collective-permute-done.46 = f32[2,16,128]{2,1,0:T(8,128)S(1)} collective-permute-done((f32[2,16,128]{2,1,0:T(8,128)S(1)}, f32[2,16,128]{2,1,0:T(8,128)S(1)}, u32[]{:S(2)}, u32[]{:S(2)}) %collective-permute-start.46) | collective-permute-done | bytes 16416 | tf_op jit(solution)/shard_map/ppermute | solution.py:117
  116.2 1.8 collective-permute-start.40
  118.0 2.8 %collective-permute-done.40 = f32[16,128]{1,0:T(8,128)S(1)} collective-permute-done((f32[16,128]{1,0:T(8,128)S(1)}, f32[16,128]{1,0:T(8,128)S(1)}, u32[]{:S(2)}, u32[]{:S(2)}) %collective-permute-start.40) | collective-permute-done | bytes 8224 | tf_op jit(solution)/shard_map/ppermute | solution.py:115
  120.8 1.8 collective-permute-start.47
  122.6 2.8 %collective-permute-done.47 = f32[16,128]{1,0:T(8,128)S(1)} collective-permute-done((f32[16,128]{1,0:T(8,128)S(1)}, f32[16,128]{1,0:T(8,128)S(1)}, u32[]{:S(2)}, u32[]{:S(2)}) %collective-permute-start.47) | collective-permute-done | bytes 8224 | tf_op jit(solution)/shard_map/ppermute | solution.py:115
  125.7 2.2 %collective-permute-start.15 = (f32[2,2,2,2,8,384]{5,4,3,2,1,0:T(8,128)S(1)}, f32[2,2,2,2,8,384]{5,4,3,2,1,0:T(8,128)S(1)}, u32[]{:S(2)}, u32[]{:S(2)}) collective-permute-start(f32[2,2,2,2,8,384]{5,4,3,2,1,0:T(8,128)S(1)} %slice_bitcast_fusion.16), channel_id=1, source_target_pairs={{0,224},{32,64},{64,32},{96,128},{128,96},{160,192},{192,160},{224... | collective-permute-start | bytes 589832 | tf_op jit(solution)/shard_map/ppermute | solution.py:115
  132.9 1.9 collective-permute-start.23
  135.1 1.9 collective-permute-start.10
  138.7 1.8 collective-permute-start.31
  141.3 1.8 collective-permute-start.18
  143.1 1.3 collective-permute-start.25
  144.8 3.4 %collective-permute-start.12 = (f32[8,384]{1,0:T(8,128)S(1)}, f32[8,384]{1,0:T(8,128)S(1)}, u32[]{:S(2)}, u32[]{:S(2)}) collective-permute-start(f32[8,384]{1,0:T(8,128)S(1)} %slice_bitcast_fusion.66), channel_id=1, source_target_pairs={{0,192},{32,224},{64,128},{96,160},{128,64},{160,96},{192,0},{224,... | collective-permute-start | bytes 36872 | tf_op jit(solution)/shard_map/ppermute | solution.py:115
  148.8 3.2 %collective-permute-start.26 = (f32[8,384]{1,0:T(8,128)S(1)}, f32[8,384]{1,0:T(8,128)S(1)}, u32[]{:S(2)}, u32[]{:S(2)}) collective-permute-start(f32[8,384]{1,0:T(8,128)S(1)} %slice_bitcast_fusion.62), channel_id=1, source_target_pairs={{0,192},{32,224},{64,128},{96,160},{128,64},{160,96},{192,0},{224,... | collective-permute-start | bytes 36872 | tf_op jit(solution)/shard_map/ppermute | solution.py:115
  153.6 3.2 %collective-permute-done.33 = f32[8,384]{1,0:T(8,128)S(1)} collective-permute-done((f32[8,384]{1,0:T(8,128)S(1)}, f32[8,384]{1,0:T(8,128)S(1)}, u32[]{:S(2)}, u32[]{:S(2)}) %collective-permute-start.33) | collective-permute-done | bytes 12320 | tf_op jit(solution)/shard_map/ppermute | solution.py:115
  157.1 21.3 %collective-permute-start.48 = (f32[8,128]{1,0:T(8,128)S(1)}, f32[8,128]{1,0:T(8,128)S(1)}, u32[]{:S(2)}, u32[]{:S(2)}) collective-permute-start(f32[8,128]{1,0:T(8,128)S(1)} %reshape.119), channel_id=1, source_target_pairs={{0,1},{1,0},{2,3},{3,2},{4,5},{5,4},{6,7},{7,6},{8,9},{9,8},{10,11... | collective-permute-start | bytes 12296 | tf_op jit(solution)/shard_map/ppermute | solution.py:128
  179.2 2.3 %collective-permute-start.50 = (f32[8,128]{1,0:T(8,128)S(1)}, f32[8,128]{1,0:T(8,128)S(1)}, u32[]{:S(2)}, u32[]{:S(2)}) collective-permute-start(f32[8,128]{1,0:T(8,128)S(1)} %add.296), channel_id=1, source_target_pairs={{0,16},{1,17},{2,18},{3,19},{4,20},{5,21},{6,22},{7,23},{8,24},{9,... | collective-permute-start | bytes 12296 | tf_op jit(solution)/shard_map/ppermute | solution.py:130
  181.6 1.5 collective-permute-start.51
  183.2 2.0 collective-permute-done.51
  185.5 1.9 collective-permute-start.53
  187.4 1.7 collective-permute-start.54
  189.5 1.6 collective-permute-done.54
  191.8 3.4 %all-to-all-start = ((f32[8,32,128]{2,1,0:T(8,128)}), f32[8,32,128]{2,1,0:T(8,128)S(1)}, u32[]{:S(2)}, u32[]{:S(2)}) async-start(f32[8,32,128]{2,1,0:T(8,128)} %pad_maximum_fusion), calls=%async_computation | async-start | bytes 262144 | tf_op jit(solution)/shard_map/all_to_all | solution.py:176
  195.2 7.8 %all-to-all-done = f32[8,32,128]{2,1,0:T(8,128)S(1)} async-done(((f32[8,32,128]{2,1,0:T(8,128)}), f32[8,32,128]{2,1,0:T(8,128)S(1)}, u32[]{:S(2)}, u32[]{:S(2)}) %all-to-all-start) | async-done | bytes 131104 | tf_op jit(solution)/shard_map/all_to_all | solution.py:176
  204.8 1.3 broadcast_select_fusion
  (222 shorter events, 26.6 us)
Async XLA Ops:
  17.6 6.3 %collective-permute-start.4 = (f32[16,8,16,128]{3,2,1,0:T(8,128)S(1)}, f32[16,8,16,128]{3,2,1,0:T(8,128)S(1)}, u32[]{:S(2)}, u32[]{:S(2)}) collective-permute-start(f32[16,8,16,128]{3,2,1,0:T(8,128)S(1)} %get-tuple-element.19), channel_id=1, source_target_pairs={{0,1},{1,0},{2,3},{3,2},{4,5},{5,4},{6,7},{7,6},{8,9},{9,8},{10,11... | collective-permute-start | bytes 3145736 | tf_op jit(solution)/shard_map/ppermute | solution.py:154
  20.8 13.1 %collective-permute-start = (f32[16,8,8,384]{3,2,1,0:T(8,128)}, f32[16,8,8,384]{3,2,1,0:T(8,128)S(1)}, u32[]{:S(2)}, u32[]{:S(2)}) collective-permute-start(f32[16,8,8,384]{3,2,1,0:T(8,128)} %get-tuple-element.15), channel_id=1, source_target_pairs={{0,1},{1,0},{2,3},{3,2},{4,5},{5,4},{6,7},{7,6},{8,9},{9,8},{10,11... | collective-permute-start | bytes 4718600 | tf_op jit(solution)/shard_map/ppermute | solution.py:154
  20.9 13.1 %collective-permute-start.1 = (f32[16,8,8,384]{3,2,1,0:T(8,128)}, f32[16,8,8,384]{3,2,1,0:T(8,128)}, u32[]{:S(2)}, u32[]{:S(2)}) collective-permute-start(f32[16,8,8,384]{3,2,1,0:T(8,128)} %get-tuple-element.16), channel_id=1, source_target_pairs={{0,1},{1,0},{2,3},{3,2},{4,5},{5,4},{6,7},{7,6},{8,9},{9,8},{10,11... | collective-permute-start | bytes 4718600 | tf_op jit(solution)/shard_map/ppermute | solution.py:154
  21.3 12.6 %collective-permute-start.2 = (f32[16,8,8,384]{3,2,1,0:T(8,128)}, f32[16,8,8,384]{3,2,1,0:T(8,128)}, u32[]{:S(2)}, u32[]{:S(2)}) collective-permute-start(f32[16,8,8,384]{3,2,1,0:T(8,128)} %get-tuple-element.17), channel_id=1, source_target_pairs={{0,1},{1,0},{2,3},{3,2},{4,5},{5,4},{6,7},{7,6},{8,9},{9,8},{10,11... | collective-permute-start | bytes 4718600 | tf_op jit(solution)/shard_map/ppermute | solution.py:154
  21.4 12.6 %collective-permute-start.3 = (f32[16,8,8,384]{3,2,1,0:T(8,128)}, f32[16,8,8,384]{3,2,1,0:T(8,128)}, u32[]{:S(2)}, u32[]{:S(2)}) collective-permute-start(f32[16,8,8,384]{3,2,1,0:T(8,128)} %get-tuple-element.18), channel_id=1, source_target_pairs={{0,1},{1,0},{2,3},{3,2},{4,5},{5,4},{6,7},{7,6},{8,9},{9,8},{10,11... | collective-permute-start | bytes 4718600 | tf_op jit(solution)/shard_map/ppermute | solution.py:154
  23.9 10.1 %collective-permute-start.5 = (f32[16,8,16,128]{3,2,1,0:T(8,128)}, f32[16,8,16,128]{3,2,1,0:T(8,128)}, u32[]{:S(2)}, u32[]{:S(2)}) collective-permute-start(f32[16,8,16,128]{3,2,1,0:T(8,128)} %get-tuple-element.20), channel_id=1, source_target_pairs={{0,1},{1,0},{2,3},{3,2},{4,5},{5,4},{6,7},{7,6},{8,9},{9,8},{10,11... | collective-permute-start | bytes 3145736 | tf_op jit(solution)/shard_map/ppermute | solution.py:154
  50.7 33.1 %collective-permute-start.6 = (f32[2,2,2,2,2,2,8,384]{7,6,5,4,2,0,3,1:T(8,128)S(1)}, f32[2,2,2,2,2,2,8,384]{7,6,5,4,2,0,3,1:T(8,128)S(1)}, u32[]{:S(2)}, u32[]{:S(2)}) collective-permute-start(f32[2,2,2,2,2,2,8,384]{7,6,5,4,2,0,3,1:T(8,128)S(1)} %copy.45), channel_id=1, source_target_pairs={{0,8},{1,9},{2,10},{3,11},{4,12},{5,13},{6,14},{7,15},{8,0},{9,1},... | collective-permute-start | bytes 2359304 | tf_op jit(solution)/shard_map/ppermute | solution.py:117
  50.8 35.7 %collective-permute-start.13 = (f32[2,2,2,2,2,2,8,384]{7,6,5,4,2,0,3,1:T(8,128)S(1)}, f32[2,2,2,2,2,2,8,384]{7,6,5,4,2,0,3,1:T(8,128)S(1)}, u32[]{:S(2)}, u32[]{:S(2)}) collective-permute-start(f32[2,2,2,2,2,2,8,384]{7,6,5,4,2,0,3,1:T(8,128)S(1)} %copy.47), channel_id=1, source_target_pairs={{0,24},{1,25},{2,26},{3,27},{4,28},{5,29},{6,30},{7,31},{8,16},{9,... | collective-permute-start | bytes 2359304 | tf_op jit(solution)/shard_map/ppermute | solution.py:117
  52.4 34.5 %collective-permute-start.20 = (f32[2,2,2,2,2,2,8,384]{7,6,5,1,4,2,0,3:T(8,128)S(1)}, f32[2,2,2,2,2,2,8,384]{7,6,5,1,4,2,0,3:T(8,128)S(1)}, u32[]{:S(2)}, u32[]{:S(2)}) collective-permute-start(f32[2,2,2,2,2,2,8,384]{7,6,5,1,4,2,0,3:T(8,128)S(1)} %bitcast.282), channel_id=1, source_target_pairs={{0,2},{1,3},{2,0},{3,1},{4,6},{5,7},{6,4},{7,5},{8,10},{9,11},{10,... | collective-permute-start | bytes 2359304 | tf_op jit(solution)/shard_map/ppermute | solution.py:117
  53.9 12.6 %collective-permute-start.34 = (f32[2,2,2,2,2,2,16,128]{7,6,5,3,1,4,2,0:T(8,128)S(1)}, f32[2,2,2,2,2,2,16,128]{7,6,5,3,1,4,2,0:T(8,128)S(1)}, u32[]{:S(2)}, u32[]{:S(2)}) collective-permute-start(f32[2,2,2,2,2,2,16,128]{7,6,5,3,1,4,2,0:T(8,128)S(1)} %bitcast.285), channel_id=1, source_target_pairs={{0,32},{32,0},{64,96},{96,64},{128,160},{160,128},{192,224},{224,1... | collective-permute-start | bytes 1572872 | tf_op jit(solution)/shard_map/ppermute | solution.py:115
  55.8 15.5 %collective-permute-start.41 = (f32[2,2,2,2,2,2,16,128]{7,6,5,3,1,4,2,0:T(8,128)S(1)}, f32[2,2,2,2,2,2,16,128]{7,6,5,3,1,4,2,0:T(8,128)S(1)}, u32[]{:S(2)}, u32[]{:S(2)}) collective-permute-start(f32[2,2,2,2,2,2,16,128]{7,6,5,3,1,4,2,0:T(8,128)S(1)} %bitcast.284), channel_id=1, source_target_pairs={{0,224},{32,64},{64,32},{96,128},{128,96},{160,192},{192,160},{224... | collective-permute-start | bytes 1572872 | tf_op jit(solution)/shard_map/ppermute | solution.py:115
  66.6 21.6 %collective-permute-start.27 = (f32[2,2,2,2,2,2,8,384]{7,6,5,1,4,2,0,3:T(8,128)S(1)}, f32[2,2,2,2,2,2,8,384]{7,6,5,1,4,2,0,3:T(8,128)S(1)}, u32[]{:S(2)}, u32[]{:S(2)}) collective-permute-start(f32[2,2,2,2,2,2,8,384]{7,6,5,1,4,2,0,3:T(8,128)S(1)} %bitcast.283), channel_id=1, source_target_pairs={{0,6},{1,7},{2,4},{3,5},{4,2},{5,3},{6,0},{7,1},{8,14},{9,15},{10,... | collective-permute-start | bytes 2359304 | tf_op jit(solution)/shard_map/ppermute | solution.py:117
  71.3 5.7 %collective-permute-start.35 = (f32[2,2,2,2,2,16,128]{6,5,4,2,0,3,1:T(8,128)S(1)}, f32[2,2,2,2,2,16,128]{6,5,4,2,0,3,1:T(8,128)S(1)}, u32[]{:S(2)}, u32[]{:S(2)}) collective-permute-start(f32[2,2,2,2,2,16,128]{6,5,4,2,0,3,1:T(8,128)S(1)} %slice_bitcast_fusion.10), channel_id=1, source_target_pairs={{0,8},{1,9},{2,10},{3,11},{4,12},{5,13},{6,14},{7,15},{8,0},{9,1},... | collective-permute-start | bytes 786440 | tf_op jit(solution)/shard_map/ppermute | solution.py:117
  76.9 6.7 %collective-permute-start.42 = (f32[2,2,2,2,2,16,128]{6,5,4,2,0,3,1:T(8,128)S(1)}, f32[2,2,2,2,2,16,128]{6,5,4,2,0,3,1:T(8,128)S(1)}, u32[]{:S(2)}, u32[]{:S(2)}) collective-permute-start(f32[2,2,2,2,2,16,128]{6,5,4,2,0,3,1:T(8,128)S(1)} %slice_bitcast_fusion.8), channel_id=1, source_target_pairs={{0,24},{1,25},{2,26},{3,27},{4,28},{5,29},{6,30},{7,31},{8,16},{9,... | collective-permute-start | bytes 786440 | tf_op jit(solution)/shard_map/ppermute | solution.py:117
  83.7 4.7 %collective-permute-start.36 = (f32[2,2,2,2,16,128]{5,4,3,1,0,2:T(8,128)S(1)}, f32[2,2,2,2,16,128]{5,4,3,1,0,2:T(8,128)S(1)}, u32[]{:S(2)}, u32[]{:S(2)}) collective-permute-start(f32[2,2,2,2,16,128]{5,4,3,1,0,2:T(8,128)S(1)} %slice_bitcast_fusion.22), channel_id=1, source_target_pairs={{0,2},{1,3},{2,0},{3,1},{4,6},{5,7},{6,4},{7,5},{8,10},{9,11},{10,... | collective-permute-start | bytes 393224 | tf_op jit(solution)/shard_map/ppermute | solution.py:117
  83.7 8.0 %collective-permute-start.43 = (f32[2,2,2,2,16,128]{5,4,3,1,0,2:T(8,128)S(1)}, f32[2,2,2,2,16,128]{5,4,3,1,0,2:T(8,128)S(1)}, u32[]{:S(2)}, u32[]{:S(2)}) collective-permute-start(f32[2,2,2,2,16,128]{5,4,3,1,0,2:T(8,128)S(1)} %slice_bitcast_fusion.20), channel_id=1, source_target_pairs={{0,6},{1,7},{2,4},{3,5},{4,2},{5,3},{6,0},{7,1},{8,14},{9,15},{10,... | collective-permute-start | bytes 393224 | tf_op jit(solution)/shard_map/ppermute | solution.py:117
  86.6 38.9 %collective-permute-start.7 = (f32[2,2,2,2,2,8,384]{6,5,4,3,1,0,2:T(8,128)S(1)}, f32[2,2,2,2,2,8,384]{6,5,4,3,1,0,2:T(8,128)S(1)}, u32[]{:S(2)}, u32[]{:S(2)}) collective-permute-start(f32[2,2,2,2,2,8,384]{6,5,4,3,1,0,2:T(8,128)S(1)} %slice_bitcast_fusion.6), channel_id=1, source_target_pairs={{0,2},{1,3},{2,0},{3,1},{4,6},{5,7},{6,4},{7,5},{8,10},{9,11},{10,... | collective-permute-start | bytes 1179656 | tf_op jit(solution)/shard_map/ppermute | solution.py:117
  87.0 38.6 %collective-permute-start.14 = (f32[2,2,2,2,2,8,384]{6,5,4,3,1,0,2:T(8,128)S(1)}, f32[2,2,2,2,2,8,384]{6,5,4,3,1,0,2:T(8,128)S(1)}, u32[]{:S(2)}, u32[]{:S(2)}) collective-permute-start(f32[2,2,2,2,2,8,384]{6,5,4,3,1,0,2:T(8,128)S(1)} %slice_bitcast_fusion.4), channel_id=1, source_target_pairs={{0,6},{1,7},{2,4},{3,5},{4,2},{5,3},{6,0},{7,1},{8,14},{9,15},{10,... | collective-permute-start | bytes 1179656 | tf_op jit(solution)/shard_map/ppermute | solution.py:117
  88.2 39.8 %collective-permute-start.21 = (f32[2,2,2,2,2,8,384]{6,5,4,1,3,2,0:T(8,128)S(1)}, f32[2,2,2,2,2,8,384]{6,5,4,1,3,2,0:T(8,128)S(1)}, u32[]{:S(2)}, u32[]{:S(2)}) collective-permute-start(f32[2,2,2,2,2,8,384]{6,5,4,1,3,2,0:T(8,128)S(1)} %slice_bitcast_fusion.2), channel_id=1, source_target_pairs={{0,32},{32,0},{64,96},{96,64},{128,160},{160,128},{192,224},{224,1... | collective-permute-start | bytes 1179656 | tf_op jit(solution)/shard_map/ppermute | solution.py:115
  88.4 39.7 %collective-permute-start.28 = (f32[2,2,2,2,2,8,384]{6,5,4,1,3,2,0:T(8,128)S(1)}, f32[2,2,2,2,2,8,384]{6,5,4,1,3,2,0:T(8,128)S(1)}, u32[]{:S(2)}, u32[]{:S(2)}) collective-permute-start(f32[2,2,2,2,2,8,384]{6,5,4,1,3,2,0:T(8,128)S(1)} %slice_bitcast_fusion), channel_id=1, source_target_pairs={{0,224},{32,64},{64,32},{96,128},{128,96},{160,192},{192,160},{224... | collective-permute-start | bytes 1179656 | tf_op jit(solution)/shard_map/ppermute | solution.py:115
  91.8 6.2 %collective-permute-start.37 = (f32[2,2,2,16,128]{4,3,2,1,0:T(8,128)S(1)}, f32[2,2,2,16,128]{4,3,2,1,0:T(8,128)S(1)}, u32[]{:S(2)}, u32[]{:S(2)}) collective-permute-start(f32[2,2,2,16,128]{4,3,2,1,0:T(8,128)S(1)} %slice_bitcast_fusion.34), channel_id=1, source_target_pairs={{0,64},{32,96},{64,0},{96,32},{128,192},{160,224},{192,128},{224,1... | collective-permute-start | bytes 196616 | tf_op jit(solution)/shard_map/ppermute | solution.py:115
  98.0 5.1 %collective-permute-start.44 = (f32[2,2,2,16,128]{4,3,2,1,0:T(8,128)S(1)}, f32[2,2,2,16,128]{4,3,2,1,0:T(8,128)S(1)}, u32[]{:S(2)}, u32[]{:S(2)}) collective-permute-start(f32[2,2,2,16,128]{4,3,2,1,0:T(8,128)S(1)} %slice_bitcast_fusion.32), channel_id=1, source_target_pairs={{0,64},{32,224},{64,0},{96,160},{128,192},{160,96},{192,128},{224,... | collective-permute-start | bytes 196616 | tf_op jit(solution)/shard_map/ppermute | solution.py:115
  103.1 4.0 %collective-permute-start.38 = (f32[2,2,16,128]{3,2,1,0:T(8,128)S(1)}, f32[2,2,16,128]{3,2,1,0:T(8,128)S(1)}, u32[]{:S(2)}, u32[]{:S(2)}) collective-permute-start(f32[2,2,16,128]{3,2,1,0:T(8,128)S(1)} %slice_bitcast_fusion.46), channel_id=1, source_target_pairs={{0,24},{1,25},{2,26},{3,27},{4,28},{5,29},{6,30},{7,31},{8,16},{9,... | collective-permute-start | bytes 98312 | tf_op jit(solution)/shard_map/ppermute | solution.py:117
  116.2 4.6 %collective-permute-start.40 = (f32[16,128]{1,0:T(8,128)S(1)}, f32[16,128]{1,0:T(8,128)S(1)}, u32[]{:S(2)}, u32[]{:S(2)}) collective-permute-start(f32[16,128]{1,0:T(8,128)S(1)} %slice_bitcast_fusion.70), channel_id=1, source_target_pairs={{0,192},{32,224},{64,128},{96,160},{128,64},{160,96},{192,0},{224,... | collective-permute-start | bytes 24584 | tf_op jit(solution)/shard_map/ppermute | solution.py:115
  120.8 4.6 %collective-permute-start.47 = (f32[16,128]{1,0:T(8,128)S(1)}, f32[16,128]{1,0:T(8,128)S(1)}, u32[]{:S(2)}, u32[]{:S(2)}) collective-permute-start(f32[16,128]{1,0:T(8,128)S(1)} %slice_bitcast_fusion.68), channel_id=1, source_target_pairs={{0,192},{32,96},{64,128},{96,32},{128,64},{160,224},{192,0},{224,1... | collective-permute-start | bytes 24584 | tf_op jit(solution)/shard_map/ppermute | solution.py:115
  125.5 4.6 %collective-permute-start.8 = (f32[2,2,2,2,8,384]{5,4,3,2,1,0:T(8,128)S(1)}, f32[2,2,2,2,8,384]{5,4,3,2,1,0:T(8,128)S(1)}, u32[]{:S(2)}, u32[]{:S(2)}) collective-permute-start(f32[2,2,2,2,8,384]{5,4,3,2,1,0:T(8,128)S(1)} %slice_bitcast_fusion.18), channel_id=1, source_target_pairs={{0,32},{32,0},{64,96},{96,64},{128,160},{160,128},{192,224},{224,1... | collective-permute-start | bytes 589832 | tf_op jit(solution)/shard_map/ppermute | solution.py:115
  125.7 5.8 %collective-permute-start.15 = (f32[2,2,2,2,8,384]{5,4,3,2,1,0:T(8,128)S(1)}, f32[2,2,2,2,8,384]{5,4,3,2,1,0:T(8,128)S(1)}, u32[]{:S(2)}, u32[]{:S(2)}) collective-permute-start(f32[2,2,2,2,8,384]{5,4,3,2,1,0:T(8,128)S(1)} %slice_bitcast_fusion.16), channel_id=1, source_target_pairs={{0,224},{32,64},{64,32},{96,128},{128,96},{160,192},{192,160},{224... | collective-permute-start | bytes 589832 | tf_op jit(solution)/shard_map/ppermute | solution.py:115
  128.0 4.9 %collective-permute-start.22 = (f32[2,2,2,2,8,384]{5,4,3,0,2,1:T(8,128)S(1)}, f32[2,2,2,2,8,384]{5,4,3,0,2,1:T(8,128)S(1)}, u32[]{:S(2)}, u32[]{:S(2)}) collective-permute-start(f32[2,2,2,2,8,384]{5,4,3,0,2,1:T(8,128)S(1)} %slice_bitcast_fusion.14), channel_id=1, source_target_pairs={{0,8},{1,9},{2,10},{3,11},{4,12},{5,13},{6,14},{7,15},{8,0},{9,1},... | collective-permute-start | bytes 589832 | tf_op jit(solution)/shard_map/ppermute | solution.py:117
  128.2 6.6 %collective-permute-start.29 = (f32[2,2,2,2,8,384]{5,4,3,0,2,1:T(8,128)S(1)}, f32[2,2,2,2,8,384]{5,4,3,0,2,1:T(8,128)S(1)}, u32[]{:S(2)}, u32[]{:S(2)}) collective-permute-start(f32[2,2,2,2,8,384]{5,4,3,0,2,1:T(8,128)S(1)} %slice_bitcast_fusion.12), channel_id=1, source_target_pairs={{0,24},{1,25},{2,26},{3,27},{4,28},{5,29},{6,30},{7,31},{8,16},{9,... | collective-permute-start | bytes 589832 | tf_op jit(solution)/shard_map/ppermute | solution.py:117
  130.2 4.9 %collective-permute-start.9 = (f32[2,2,2,8,384]{4,3,2,1,0:T(8,128)S(1)}, f32[2,2,2,8,384]{4,3,2,1,0:T(8,128)S(1)}, u32[]{:S(2)}, u32[]{:S(2)}) collective-permute-start(f32[2,2,2,8,384]{4,3,2,1,0:T(8,128)S(1)} %slice_bitcast_fusion.30), channel_id=1, source_target_pairs={{0,24},{1,25},{2,26},{3,27},{4,28},{5,29},{6,30},{7,31},{8,16},{9,... | collective-permute-start | bytes 294920 | tf_op jit(solution)/shard_map/ppermute | solution.py:117
  131.6 5.4 %collective-permute-start.16 = (f32[2,2,2,8,384]{4,3,2,1,0:T(8,128)S(1)}, f32[2,2,2,8,384]{4,3,2,1,0:T(8,128)S(1)}, u32[]{:S(2)}, u32[]{:S(2)}) collective-permute-start(f32[2,2,2,8,384]{4,3,2,1,0:T(8,128)S(1)} %slice_bitcast_fusion.28), channel_id=1, source_target_pairs={{0,8},{1,9},{2,10},{3,11},{4,12},{5,13},{6,14},{7,15},{8,0},{9,1},... | collective-permute-start | bytes 294920 | tf_op jit(solution)/shard_map/ppermute | solution.py:117
  132.9 4.8 %collective-permute-start.23 = (f32[2,2,2,8,384]{4,3,2,0,1:T(8,128)S(1)}, f32[2,2,2,8,384]{4,3,2,0,1:T(8,128)S(1)}, u32[]{:S(2)}, u32[]{:S(2)}) collective-permute-start(f32[2,2,2,8,384]{4,3,2,0,1:T(8,128)S(1)} %slice_bitcast_fusion.26), channel_id=1, source_target_pairs={{0,6},{1,7},{2,4},{3,5},{4,2},{5,3},{6,0},{7,1},{8,14},{9,15},{10,... | collective-permute-start | bytes 294920 | tf_op jit(solution)/shard_map/ppermute | solution.py:117
  135.1 5.4 %collective-permute-start.10 = (f32[2,2,8,384]{3,2,1,0:T(8,128)S(1)}, f32[2,2,8,384]{3,2,1,0:T(8,128)S(1)}, u32[]{:S(2)}, u32[]{:S(2)}) collective-permute-start(f32[2,2,8,384]{3,2,1,0:T(8,128)S(1)} %slice_bitcast_fusion.42), channel_id=1, source_target_pairs={{0,6},{1,7},{2,4},{3,5},{4,2},{5,3},{6,0},{7,1},{8,14},{9,15},{10,... | collective-permute-start | bytes 147464 | tf_op jit(solution)/shard_map/ppermute | solution.py:117
  137.0 4.3 %collective-permute-start.17 = (f32[2,2,8,384]{3,2,1,0:T(8,128)S(1)}, f32[2,2,8,384]{3,2,1,0:T(8,128)S(1)}, u32[]{:S(2)}, u32[]{:S(2)}) collective-permute-start(f32[2,2,8,384]{3,2,1,0:T(8,128)S(1)} %slice_bitcast_fusion.40), channel_id=1, source_target_pairs={{0,2},{1,3},{2,0},{3,1},{4,6},{5,7},{6,4},{7,5},{8,10},{9,11},{10,... | collective-permute-start | bytes 147464 | tf_op jit(solution)/shard_map/ppermute | solution.py:117
  137.7 5.4 %collective-permute-start.24 = (f32[2,2,8,384]{3,2,1,0:T(8,128)S(1)}, f32[2,2,8,384]{3,2,1,0:T(8,128)S(1)}, u32[]{:S(2)}, u32[]{:S(2)}) collective-permute-start(f32[2,2,8,384]{3,2,1,0:T(8,128)S(1)} %slice_bitcast_fusion.38), channel_id=1, source_target_pairs={{0,64},{32,96},{64,0},{96,32},{128,192},{160,224},{192,128},{224,1... | collective-permute-start | bytes 147464 | tf_op jit(solution)/shard_map/ppermute | solution.py:115
  138.7 5.7 %collective-permute-start.31 = (f32[2,2,8,384]{3,2,1,0:T(8,128)S(1)}, f32[2,2,8,384]{3,2,1,0:T(8,128)S(1)}, u32[]{:S(2)}, u32[]{:S(2)}) collective-permute-start(f32[2,2,8,384]{3,2,1,0:T(8,128)S(1)} %slice_bitcast_fusion.36), channel_id=1, source_target_pairs={{0,64},{32,224},{64,0},{96,160},{128,192},{160,96},{192,128},{224,... | collective-permute-start | bytes 147464 | tf_op jit(solution)/shard_map/ppermute | solution.py:115
  140.6 4.2 %collective-permute-start.11 = (f32[2,8,384]{2,1,0:T(8,128)S(1)}, f32[2,8,384]{2,1,0:T(8,128)S(1)}, u32[]{:S(2)}, u32[]{:S(2)}) collective-permute-start(f32[2,8,384]{2,1,0:T(8,128)S(1)} %slice_bitcast_fusion.54), channel_id=1, source_target_pairs={{0,64},{32,96},{64,0},{96,32},{128,192},{160,224},{192,128},{224,1... | collective-permute-start | bytes 73736 | tf_op jit(solution)/shard_map/ppermute | solution.py:115
  141.3 6.9 %collective-permute-start.18 = (f32[2,8,384]{2,1,0:T(8,128)S(1)}, f32[2,8,384]{2,1,0:T(8,128)S(1)}, u32[]{:S(2)}, u32[]{:S(2)}) collective-permute-start(f32[2,8,384]{2,1,0:T(8,128)S(1)} %slice_bitcast_fusion.52), channel_id=1, source_target_pairs={{0,64},{32,224},{64,0},{96,160},{128,192},{160,96},{192,128},{224,... | collective-permute-start | bytes 73736 | tf_op jit(solution)/shard_map/ppermute | solution.py:115
  143.1 5.7 %collective-permute-start.25 = (f32[2,8,384]{2,1,0:T(8,128)S(1)}, f32[2,8,384]{2,1,0:T(8,128)S(1)}, u32[]{:S(2)}, u32[]{:S(2)}) collective-permute-start(f32[2,8,384]{2,1,0:T(8,128)S(1)} %slice_bitcast_fusion.50), channel_id=1, source_target_pairs={{0,24},{1,25},{2,26},{3,27},{4,28},{5,29},{6,30},{7,31},{8,16},{9,... | collective-permute-start | bytes 73736 | tf_op jit(solution)/shard_map/ppermute | solution.py:117
  144.4 7.5 %collective-permute-start.32 = (f32[2,8,384]{2,1,0:T(8,128)S(1)}, f32[2,8,384]{2,1,0:T(8,128)S(1)}, u32[]{:S(2)}, u32[]{:S(2)}) collective-permute-start(f32[2,8,384]{2,1,0:T(8,128)S(1)} %slice_bitcast_fusion.48), channel_id=1, source_target_pairs={{0,8},{1,9},{2,10},{3,11},{4,12},{5,13},{6,14},{7,15},{8,0},{9,1},... | collective-permute-start | bytes 73736 | tf_op jit(solution)/shard_map/ppermute | solution.py:117
  144.8 7.8 %collective-permute-start.12 = (f32[8,384]{1,0:T(8,128)S(1)}, f32[8,384]{1,0:T(8,128)S(1)}, u32[]{:S(2)}, u32[]{:S(2)}) collective-permute-start(f32[8,384]{1,0:T(8,128)S(1)} %slice_bitcast_fusion.66), channel_id=1, source_target_pairs={{0,192},{32,224},{64,128},{96,160},{128,64},{160,96},{192,0},{224,... | collective-permute-start | bytes 36872 | tf_op jit(solution)/shard_map/ppermute | solution.py:115
  148.2 4.7 %collective-permute-start.19 = (f32[8,384]{1,0:T(8,128)S(1)}, f32[8,384]{1,0:T(8,128)S(1)}, u32[]{:S(2)}, u32[]{:S(2)}) collective-permute-start(f32[8,384]{1,0:T(8,128)S(1)} %slice_bitcast_fusion.64), channel_id=1, source_target_pairs={{0,192},{32,96},{64,128},{96,32},{128,64},{160,224},{192,0},{224,1... | collective-permute-start | bytes 36872 | tf_op jit(solution)/shard_map/ppermute | solution.py:115
  148.8 4.7 %collective-permute-start.26 = (f32[8,384]{1,0:T(8,128)S(1)}, f32[8,384]{1,0:T(8,128)S(1)}, u32[]{:S(2)}, u32[]{:S(2)}) collective-permute-start(f32[8,384]{1,0:T(8,128)S(1)} %slice_bitcast_fusion.62), channel_id=1, source_target_pairs={{0,192},{32,224},{64,128},{96,160},{128,64},{160,96},{192,0},{224,... | collective-permute-start | bytes 36872 | tf_op jit(solution)/shard_map/ppermute | solution.py:115
  152.0 4.8 %collective-permute-start.33 = (f32[8,384]{1,0:T(8,128)S(1)}, f32[8,384]{1,0:T(8,128)S(1)}, u32[]{:S(2)}, u32[]{:S(2)}) collective-permute-start(f32[8,384]{1,0:T(8,128)S(1)} %slice_bitcast_fusion.60), channel_id=1, source_target_pairs={{0,192},{32,96},{64,128},{96,32},{128,64},{160,224},{192,0},{224,1... | collective-permute-start | bytes 36872 | tf_op jit(solution)/shard_map/ppermute | solution.py:115
  157.1 22.1 %collective-permute-start.48 = (f32[8,128]{1,0:T(8,128)S(1)}, f32[8,128]{1,0:T(8,128)S(1)}, u32[]{:S(2)}, u32[]{:S(2)}) collective-permute-start(f32[8,128]{1,0:T(8,128)S(1)} %reshape.119), channel_id=1, source_target_pairs={{0,1},{1,0},{2,3},{3,2},{4,5},{5,4},{6,7},{7,6},{8,9},{9,8},{10,11... | collective-permute-start | bytes 12296 | tf_op jit(solution)/shard_map/ppermute | solution.py:128
  185.2 4.3 %collective-permute-start.52 = (f32[8,128]{1,0:T(8,128)S(1)}, f32[8,128]{1,0:T(8,128)S(1)}, u32[]{:S(2)}, u32[]{:S(2)}) collective-permute-start(f32[8,128]{1,0:T(8,128)S(1)} %add_add_fusion.1), channel_id=1, source_target_pairs={{0,2},{1,3},{2,0},{3,1},{4,6},{5,7},{6,4},{7,5},{8,10},{9,11},{10,... | collective-permute-start | bytes 12296 | tf_op jit(solution)/shard_map/ppermute | solution.py:130
  185.5 4.0 %collective-permute-start.53 = (f32[8,128]{1,0:T(8,128)S(1)}, f32[8,128]{1,0:T(8,128)S(1)}, u32[]{:S(2)}, u32[]{:S(2)}) collective-permute-start(f32[8,128]{1,0:T(8,128)S(1)} %add_add_fusion.1), channel_id=1, source_target_pairs={{0,4},{1,5},{2,6},{3,7},{4,0},{5,1},{6,2},{7,3},{8,12},{9,13},{10,... | collective-permute-start | bytes 12296 | tf_op jit(solution)/shard_map/ppermute | solution.py:130
  191.8 11.2 %all-to-all-start = ((f32[8,32,128]{2,1,0:T(8,128)}), f32[8,32,128]{2,1,0:T(8,128)S(1)}, u32[]{:S(2)}, u32[]{:S(2)}) async-start(f32[8,32,128]{2,1,0:T(8,128)} %pad_maximum_fusion), calls=%async_computation | async-start | bytes 262144 | tf_op jit(solution)/shard_map/all_to_all | solution.py:176
  (17 other events, 176.0 us)

commit v2 on v0

v2 whole, which is shorter than its diff:
```python
import functools
import jax
import jax.numpy as jnp
from jax import lax
from jax.experimental import pallas as pl
from jax.experimental.pallas import tpu as pltpu
from jax.sharding import PartitionSpec as P

D = 8192
HEAD_DIM = 256
TOKENS = 131072
DECAY_RATE = 1.0 - 8.0 ** (-0.8)
EPSILON = 1e-30
CLIP_LIMIT = 1.0
MIB = 1024 * 1024

RING4 = ((1, 3), (3, 1))
RING8 = (1, 2, 6)
Z_MASKS = [i * RING8[0] ^ j * RING8[1] ^ k * RING8[2] for i in (0, 1) for j in (0, 1) for k in (0, 1)]
UNITS = ((0, 6), (6, 12), (12, 16))


def swap_cores(value):
    return lax.ppermute(value, "col", [(i, i ^ 1) for i in range(32)])


def along(axis, step, value):
    if axis == "z":
        pairs = []
        for z in range(8):
            for i in range(32):
                core = i % 2
                to = ((((z + core) % 8) ^ RING8[step]) + 8 - core) % 8
                pairs.append((z * 32 + i, to * 32 + i))
        return lax.ppermute(value, ("row", "col"), pairs)
    shift = 3 if axis == "x" else 1
    return lax.ppermute(value, "col", [(i, i ^ (RING4[i % 2][step] << shift)) for i in range(32)])


def partial_kernel(chunk, to_sibling, pos, *refs):
    xs, y_ref, acc = refs[:4], refs[4], refs[-1]
    z, core = pos[0], lax.rem(pos[1], 2)
    core = 1 - core if to_sibling else core
    if to_sibling:
        out = refs[5]
    else:
        got = refs[5]
        outs = refs[6:-1]
    starts = [
        pl.multiple_of(lax.rem((lax.rem(z + core, 8) ^ mask) + 8 - core, 8) * 32, 32) for mask in Z_MASKS
    ]
    for s in range(4):
        acc[s] = lax.dot_general(
            xs[s][...], y_ref[...], (((0,), (0,)), ((), ())), preferred_element_type=jnp.float32
        )
        for slot in range(8):
            for unit in range(16):
                group, lane = divmod(unit, 4)
                value = acc[s, pl.ds(starts[slot] + group * 8, 8), lane * 128 : lane * 128 + 128]
                if to_sibling:
                    out[0, s, slot, unit] = value
                    continue
                value = value + got[0, s, slot, unit]
                if unit < 6:
                    outs[0][0, s, slot, unit] = value
                elif unit < 12:
                    outs[1 if s >= 2 else 2][0, s % 2, slot, unit - 6] = value
                else:
                    outs[3 if slot >= 4 else 4][0, s, slot % 4, unit - 12] = value


def partial(pos, x, y, chunk, got=None):
    to_sibling = got is None

    def block(s):
        def index(step, pos):
            core = lax.rem(pos[1], 2)
            core = 1 - core if to_sibling else core
            first, second = 1 + 2 * core, 3 - 2 * core
            xi = lax.div(pos[1], 8) ^ (first * chunk) ^ (second * step)
            yi = lax.rem(lax.div(pos[1], 2), 4) ^ (first * (s // 2)) ^ (second * (s % 2))
            return (0, (xi * 4 + yi) * 2 + core)

        return pl.BlockSpec((512, 256), index)

    def whole(shape):
        return pl.BlockSpec((1,) + shape[1:], lambda step, pos: (step,) + (0,) * (len(shape) - 1))

    full = (2, 4, 8, 16, 8, 128)
    if to_sibling:
        shapes = [full]
    else:
        part_b, part_c = (2, 2, 8, 6, 8, 128), (2, 4, 4, 4, 8, 128)
        shapes = [(2, 4, 8, 6, 8, 128), part_b, part_b, part_c, part_c]
    return pl.pallas_call(
        functools.partial(partial_kernel, chunk, to_sibling),
        grid_spec=pltpu.PrefetchScalarGridSpec(
            num_scalar_prefetch=1,
            grid=(2,),
            in_specs=[block(s) for s in range(4)]
            + [pl.BlockSpec((512, 512), lambda step, pos: (0, 0))]
            + ([] if to_sibling else [whole(full)]),
            out_specs=[whole(s) for s in shapes],
            scratch_shapes=[pltpu.VMEM((4, 256, 512), jnp.float32)],
        ),
        out_shape=[jax.ShapeDtypeStruct(s, jnp.float32) for s in shapes],
        compiler_params=pltpu.CompilerParams(vmem_limit_bytes=56 * MIB),
        cost_estimate=pl.CostEstimate(
            flops=2 * 512 * 512 * 2048, bytes_accessed=(7 if to_sibling else 11) * MIB, transcendentals=0
        ),
        name=("away" if to_sibling else "near") + str(chunk),
    )(pos, x, x, x, x, y, *([] if to_sibling else [got]))


def stats_kernel(pos, units, col_old, row_old, tile, stats):
    z = pos[0]
    lane = lax.broadcasted_iota(jnp.int32, (8, 128), 1)
    sub = lax.broadcasted_iota(jnp.int32, (8, 128), 0)
    even = lane % 2 == 0
    upper = lane >= 64
    scale = float(TOKENS) ** -0.5
    place = 64 + 32 * lax.rem(z, 2)
    col_row = [jnp.zeros((1, 128), jnp.float32)] * 2
    squares_of = [jnp.zeros((1, 128), jnp.float32)] * 4
    raised_of = [jnp.zeros((1, 128), jnp.float32)] * 4
    for group in range(4):
        grads = [units[group * 4 + i] * scale for i in range(4)]
        square = [g * g for g in grads]
        total = sum(s + EPSILON for s in square)
        sums = [
            jnp.sum(jnp.where(even, total, 0.0), axis=1, keepdims=True),
            jnp.sum(jnp.where(even, 0.0, total), axis=1, keepdims=True),
        ]
        factor = []
        for m in range(2):
            old = col_old[group * 8 : group * 8 + 8, m : m + 1]
            new = DECAY_RATE * old + (1.0 - DECAY_RATE) * (sums[m] / HEAD_DIM)
            new = jnp.broadcast_to(new, (8, 128))
            factor.append(new)
            placed = jnp.where(lane == sub + (group * 8 + place), new, 0.0)
            col_row[m] = col_row[m] + jnp.sum(placed, axis=0, keepdims=True)
        inverse = lax.rsqrt(jnp.where(even, factor[0], factor[1]))
        for i in range(4):
            scaled = grads[i] * inverse
            squares_of[i] = squares_of[i] + jnp.sum(square[i] + EPSILON, axis=0, keepdims=True)
            raised_of[i] = raised_of[i] + jnp.sum(scaled * scaled, axis=0, keepdims=True)
            low = jnp.where(upper, 0.0, scaled)
            high = jnp.where(upper, 0.0, pltpu.roll(scaled, 64, 1))
            tile[2 * i, group * 8 : group * 8 + 8] = low
            tile[2 * i + 1, group * 8 : group * 8 + 8] = high
    for base, rows in ((0, squares_of), (8, raised_of)):
        value = jnp.zeros((8, 128), jnp.float32)
        for i in range(4):
            both = jnp.broadcast_to(rows[i], (8, 128))
            value = jnp.where(sub == 2 * i, pltpu.roll(both, 64, 1), value)
            value = jnp.where(sub == 2 * i + 1, both, value)
        stats[base : base + 8] = jnp.where(upper, value, 0.0)
    olds = jnp.where((sub == z) & upper, jnp.broadcast_to(row_old[...], (8, 128)), 0.0)
    cols = jnp.zeros((8, 128), jnp.float32)
    for m in range(2):
        cols = jnp.where(sub == 4 * m + lax.div(z, 2), jnp.broadcast_to(col_row[m], (8, 128)), cols)
    for to in range(8):
        tile[to, 16:24] = tile[to, 16:24] + olds
        tile[to, 24:32] = tile[to, 24:32] + cols


def finish_kernel(pos, load, direction, row_new, col_new, scales, rows):
    z = pos[0]
    lane = lax.broadcasted_iota(jnp.int32, (8, 128), 1)
    even = lane % 2 == 0
    upper = lane >= 64
    total = load[0]
    for i in range(1, 8):
        total = total + load[i]
    row_all = DECAY_RATE * total[16:24] + (1.0 - DECAY_RATE) * (total[0:8] / D)
    row_all = jnp.where(upper, row_all, 1.0)
    per_row = jnp.where(upper, total[8:16] / row_all, 0.0)
    limiter = []
    for keep in (even, jnp.logical_not(even)):
        clip = jnp.sum(jnp.where(keep, per_row, 0.0), axis=(0, 1), keepdims=True)
        limiter.append(jnp.maximum(1.0, jnp.sqrt(clip / (HEAD_DIM * D)) / CLIP_LIMIT))
    bound = jnp.where(even, jnp.broadcast_to(limiter[0], (8, 128)), jnp.broadcast_to(limiter[1], (8, 128)))
    scales[...] = pltpu.roll(lax.rsqrt(row_all) / bound, 64, 1)
    rows[...] = pltpu.roll(row_all, 64, 1)
    row_new[...] = rows[pl.ds(z, 1), 0:64]
    mine = jnp.broadcast_to(scales[pl.ds(z, 1), :], (128, 128))
    for half in range(2):
        block = jnp.concatenate([load[4 * half + i] for i in range(4)], axis=0) * mine
        direction[:, half * 128 : half * 128 + 128] = block.T[0:64]
    cols = total[24:32]
    moved = pltpu.roll(cols, 64, 1)
    for m in range(2):
        for half in range(2):
            at = 4 * m + 2 * half
            pair = jnp.where(upper[0:1], cols[at + 1 : at + 2], moved[at : at + 1])
            col_new[m : m + 1, half * 128 : half * 128 + 128] = pair


def on_device(activations, kv_grads, row_state, col_state):
    z = lax.axis_index("row").astype(jnp.int32)
    pos = jnp.stack([z, lax.axis_index("col").astype(jnp.int32)])
    col_old = lax.dynamic_slice_in_dim(col_state, z * 32, 32, axis=1).T
    row_old = jnp.concatenate([row_state, row_state]).reshape(1, 128)

    sent = [swap_cores(partial(pos, activations, kv_grads, chunk)[0]) for chunk in (1, 0)]
    a_send, b_send1, b_keep1, c_send1, c_keep1 = partial(pos, activations, kv_grads, 1, sent[0])
    a_keep, b_send0, b_keep0, c_send0, c_keep0 = partial(pos, activations, kv_grads, 0, sent[1])

    got = along("x", 0, a_send), along("y", 0, b_send1), along("z", 0, c_send1)
    got = got + (along("y", 0, b_send0), along("z", 0, c_send0))
    got = lax.optimization_barrier(got)
    a = (a_keep + got[0]).reshape(2, 2, 2, 2, 2, 2, 6, 8, 128)
    b1 = (b_keep1 + got[1]).reshape(2, 2, 2, 2, 2, 6, 8, 128)
    b0 = (b_keep0 + got[3]).reshape(2, 2, 2, 2, 2, 6, 8, 128)
    c1 = (c_keep1 + got[2]).reshape(2, 2, 2, 2, 2, 4, 8, 128)
    c0 = (c_keep0 + got[4]).reshape(2, 2, 2, 2, 2, 4, 8, 128)

    got = along("y", 0, a[:, 1]), along("z", 0, jnp.stack([b1[:, :, 1], b0[:, :, 1]])), along("x", 0, c1)
    got = lax.optimization_barrier(got)
    a = a[:, 0] + got[0]
    b1, b0 = b1[:, :, 0] + got[1][0], b0[:, :, 0] + got[1][1]
    c = c0 + got[2]

    got = along("z", 0, a[:, :, 1]), along("x", 0, b1), along("y", 0, c[:, 1])
    got = lax.optimization_barrier(got)
    a = a[:, :, 0] + got[0]
    b = b0 + got[1]
    c = c[:, 0] + got[2]

    value = jnp.concatenate([a, b, c], axis=4)
    for axis, step in (("x", 1), ("y", 1), ("z", 1), ("z", 2)):
        value = value[0] + along(axis, step, value[1])

    tile, stats = pl.pallas_call(
        stats_kernel,
        in_specs=[pl.BlockSpec(memory_space=pltpu.SMEM)] + [pl.BlockSpec(memory_space=pltpu.VMEM)] * 3,
        out_specs=[pl.BlockSpec(memory_space=pltpu.VMEM)] * 2,
        out_shape=[
            jax.ShapeDtypeStruct((8, 32, 128), jnp.float32),
            jax.ShapeDtypeStruct((16, 128), jnp.float32),
        ],
        name="stats",
    )(pos, value, col_old, row_old)

    stats = stats + swap_cores(stats)
    for shift in (3, 1):
        others = [lax.ppermute(stats, "col", [(i, i ^ (m << shift)) for i in range(32)]) for m in (1, 2, 3)]
        stats = stats + others[0] + others[1] + others[2]
    load = jnp.concatenate([tile[:, :16] + stats[None], tile[:, 16:]], axis=1)
    load = lax.all_to_all(load, "row", 0, 0, tiled=True)

    direction, row_new, col_new = pl.pallas_call(
        finish_kernel,
        in_specs=[pl.BlockSpec(memory_space=pltpu.SMEM), pl.BlockSpec(memory_space=pltpu.VMEM)],
        out_specs=[pl.BlockSpec(memory_space=pltpu.VMEM)] * 3,
        out_shape=[
            jax.ShapeDtypeStruct((64, 256), jnp.float32),
            jax.ShapeDtypeStruct((1, 64), jnp.float32),
            jax.ShapeDtypeStruct((2, 256), jnp.float32),
        ],
        scratch_shapes=[pltpu.VMEM((8, 128), jnp.float32)] * 2,
        name="finish",
    )(pos, load)
    return (direction, row_new.reshape(64), col_new)


def solution(mesh):
    placed = (P(("row", "col"), None), P(("row", "col"), None), P("row"), P(None, "col"))
    return jax.shard_map(
        on_device,
        mesh=mesh,
        in_specs=placed,
        out_specs=(P("row", "col"), P("row"), P(None, "col")),
        check_vma=False,
    )
```

time: 349 us -> 146 us (0.42)
  blocking collectives: 156 us -> 14.4 us
  waiting for transfers between devices: 159 us -> 61.2 us
  starting transfers between devices: 0.08 us -> 31.7 us
  Pallas kernels: 0 us -> 26 us
  matrix products: 14.3 us -> 0 us
  between operations: 14.1 us -> 0.93 us
  other arithmetic: 1.73 us -> 5.82 us
    psum x3 -> x0, blocking collectives: 156 us -> none  [the longest x1 72.6 us: on_device(): clip_total = lax.psum(clip_terms, ('row', 'col'))]
    reduce_scatter x1 -> x0, waiting for transfers between devices: 126 us -> none  [on_device(): lax.psum_scatter(lax.dot_general(activations, kv_grads, contract, preferr...]
    ppermute x0 -> x24, waiting for transfers between devices: none -> 61.2 us  [the longest x9 26.8 us: along(): lax.ppermute(value, 'col', [(i, i ^ RING4[i % 2][step] << shift) for i in...]
    unnamed x3 -> x0, waiting for transfers between devices: 33.7 us -> none
    ppermute x0 -> x24, starting transfers between devices: none -> 31.7 us  [the longest x9 9.86 us: along(): lax.ppermute(value, 'col', [(i, i ^ RING4[i % 2][step] << shift) for i in...]
    pallas_call x0 -> x6, Pallas kernels: none -> 26 us  [the longest x4 22.3 us: partial(): pl.pallas_call(functools.partial(partial_kernel, chunk, to_sibling), grid...]
    all_to_all x0 -> x1, blocking collectives: none -> 14.4 us  [on_device(): load = lax.all_to_all(load, 'row', 0, 0, tiled=True)]
    dot_general x5 -> x0, matrix products: 14.3 us -> none  [the longest x1 11.7 us: on_device(): lax.dot_general(activations, kv_grads, contract, preferred_element_type=j...]
  transfers between devices with their start and end apart: 2 -> 24, of which waited for: 2 -> 16; matrix products, arithmetic and copies ran while one was open for 0% -> 2% of each run, Pallas kernels for 0% -> 12%
where the time goes in v2:
time: 146 us; the launch traced here: 143 us
  waiting for transfers between devices  61.2 us (42%)
  starting transfers between devices  31.7 us (22%)
  Pallas kernels  26 us (18%)
  blocking collectives  14.4 us (10%)
  other arithmetic  5.82 us (4%)
  local copies, waits for them, and re-layouts  3.14 us (2%)
    ppermute x9, waiting for transfers between devices, along(): lax.ppermute(value, 'col', [(i, i ^ RING4[i % 2][step] << shift) for i in...  26.8 us
    ppermute x6, waiting for transfers between devices, along(): return lax.ppermute(value, ('row', 'col'), pairs)  23.7 us
    pallas_call x4, Pallas kernels, partial(): pl.pallas_call(functools.partial(partial_kernel, chunk, to_sibling), grid...  22.3 us
    all_to_all x1, blocking collectives, on_device(): load = lax.all_to_all(load, 'row', 0, 0, tiled=True)  14.4 us
    ppermute x9, starting transfers between devices, along(): lax.ppermute(value, 'col', [(i, i ^ RING4[i % 2][step] << shift) for i in...  9.86 us
    ppermute x6, starting transfers between devices, along(): return lax.ppermute(value, ('row', 'col'), pairs)  9.17 us
    ppermute x6, starting transfers between devices, on_device(): lax.ppermute(stats, 'col', [(i, i ^ m << shift) for i in range(32)])  7.79 us
    ppermute x6, waiting for transfers between devices, on_device(): lax.ppermute(stats, 'col', [(i, i ^ m << shift) for i in range(32)])  7.63 us
  transfers between devices with their start and end apart: 24, of which 16 were waited for; matrix products, arithmetic and copies ran while one was open for 2% of the time, Pallas kernels for 12%

profile of v2, /device:TPU:1, one launch (start us, length us, event | category | flops | bytes accessed | tf_op | source)
XLA Modules:
  0.0 143.2 jit_solution(2026316145857481931)
XLA Ops:
  0.6 0.7 pad_add_fusion.pos
  1.3 5.1 %away1.1 = f32[2,4,8,16,8,128]{5,4,3,2,1,0:T(8,128)} custom-call(s32[2]{0:T(128)} %pad_add_fusion.pos, bf16[512,8192]{1,0:T(8,128)(2,1)} %refs_3_.7, bf16[512,8192]{1,0:T(8,128)(2,1)} %refs_3_.7, bf16[512,8192]{1,0:T(8,128)(2,1)} %refs_3_.7, bf16[512,8192]{1,0:T(8,128)(2,1)} %refs_3_.7, bf16[512,512]{1,0:T(8,128)(2,1)} %refs_4_.7), custom_call_target="tpu_custom_call" | custom-call | flops 1073741824 | bytes 7340032 | tf_op jit(solution)/shard_map/away1/pallas_call | solution.py:95
  6.4 3.2 %collective-permute-start.1 = (f32[2,4,8,16,8,128]{5,4,3,2,1,0:T(8,128)}, f32[2,4,8,16,8,128]{5,4,3,2,1,0:T(8,128)}, u32[]{:S(2)}, u32[]{:S(2)}) collective-permute-start(f32[2,4,8,16,8,128]{5,4,3,2,1,0:T(8,128)} %away1.1), channel_id=1, source_target_pairs={{0,1},{1,0},{2,3},{3,2},{4,5},{5,4},{6,7},{7,6},{8,9},{9,8},{10,11... | collective-permute-start | bytes 12582920 | tf_op jit(solution)/shard_map/ppermute | solution.py:24
  9.7 5.2 %away0.1 = f32[2,4,8,16,8,128]{5,4,3,2,1,0:T(8,128)} custom-call(s32[2]{0:T(128)} %pad_add_fusion.pos, bf16[512,8192]{1,0:T(8,128)(2,1)} %refs_3_.7, bf16[512,8192]{1,0:T(8,128)(2,1)} %refs_3_.7, bf16[512,8192]{1,0:T(8,128)(2,1)} %refs_3_.7, bf16[512,8192]{1,0:T(8,128)(2,1)} %refs_3_.7, bf16[512,512]{1,0:T(8,128)(2,1)} %refs_4_.7), custom_call_target="tpu_custom_call" | custom-call | flops 1073741824 | bytes 7340032 | tf_op jit(solution)/shard_map/away0/pallas_call | solution.py:95
  14.8 2.0 %collective-permute-done.1.refs_5_ = f32[2,4,8,16,8,128]{5,4,3,2,1,0:T(8,128)} collective-permute-done((f32[2,4,8,16,8,128]{5,4,3,2,1,0:T(8,128)}, f32[2,4,8,16,8,128]{5,4,3,2,1,0:T(8,128)}, u32[]{:S(2)}, u32[]{:S(2)}) %collective-permute-start.1) | collective-permute-done | bytes 4194336 | tf_op jit(solution)/shard_map/ppermute | solution.py:24
  16.8 6.0 %near1.1 = (f32[2,4,8,6,8,128]{5,4,3,2,1,0:T(8,128)}, f32[2,2,8,6,8,128]{5,4,3,2,1,0:T(8,128)}, f32[2,2,8,6,8,128]{5,4,3,2,1,0:T(8,128)}, f32[2,4,4,4,8,128]{5,4,3,2,1,0:T(8,128)}, f32[2,4,4,4,8,128]{5,4,3,2,1,0:T(8,128)}) custom-call(s32[2]{0:T(128)} %pad_add_fusion.pos, bf16[512,8192]{1,0:T(8,128)(2,1)} %refs_3_.7, bf16[512,8192]{1,0:T(8,128)(2,1)} %refs_3_.7, ...), custom_call_target="tpu_custom_call" | custom-call | flops 1073741824 | bytes 11534336 | tf_op jit(solution)/shard_map/near1/pallas_call | solution.py:95
  22.8 0.8 collective-permute-start.2
  23.6 2.7 %collective-permute-start.3 = (f32[2,2,8,6,8,128]{5,4,3,2,1,0:T(8,128)}, f32[2,2,8,6,8,128]{5,4,3,2,1,0:T(8,128)S(1)}, u32[]{:S(2)}, u32[]{:S(2)}) collective-permute-start(f32[2,2,8,6,8,128]{5,4,3,2,1,0:T(8,128)} %get-tuple-element.31), channel_id=1, source_target_pairs={{0,2},{1,7},{2,0},{3,5},{4,6},{5,3},{6,4},{7,1},{8,10},{9,15},{10,... | collective-permute-start | bytes 2359304 | tf_op jit(solution)/shard_map/ppermute | solution.py:37
  26.3 2.0 %copy-done.1 = f32[2,4,8,16,8,128]{5,4,3,2,1,0:T(8,128)} copy-done((f32[2,4,8,16,8,128]{5,4,3,2,1,0:T(8,128)}, f32[2,4,8,16,8,128]{5,4,3,2,1,0:T(8,128)S(1)}, u32[]{:S(2)}) %copy-start.1) | copy-done | bytes 4194328
  28.3 6.0 %near0.1 = (f32[2,4,8,6,8,128]{5,4,3,2,1,0:T(8,128)}, f32[2,2,8,6,8,128]{5,4,3,2,1,0:T(8,128)}, f32[2,2,8,6,8,128]{5,4,3,2,1,0:T(8,128)}, f32[2,4,4,4,8,128]{5,4,3,2,1,0:T(8,128)}, f32[2,4,4,4,8,128]{5,4,3,2,1,0:T(8,128)}) custom-call(s32[2]{0:T(128)} %pad_add_fusion.pos, bf16[512,8192]{1,0:T(8,128)(2,1)} %refs_3_.7, bf16[512,8192]{1,0:T(8,128)(2,1)} %refs_3_.7, ...), custom_call_target="tpu_custom_call" | custom-call | flops 1073741824 | bytes 11534336 | tf_op jit(solution)/shard_map/near0/pallas_call | solution.py:95
  34.4 5.7 %collective-permute-start.4 = (f32[2,4,4,4,8,128]{5,4,3,2,1,0:T(8,128)S(1)}, f32[2,4,4,4,8,128]{5,4,3,2,1,0:T(8,128)S(1)}, u32[]{:S(2)}, u32[]{:S(2)}) collective-permute-start(f32[2,4,4,4,8,128]{5,4,3,2,1,0:T(8,128)S(1)} %copy-done.6), channel_id=1, source_target_pairs={{0,32},{1,225},{2,34},{3,227},{4,36},{5,229},{6,38},{7,231},{8,40}... | collective-permute-start | bytes 1572872 | tf_op jit(solution)/shard_map/ppermute | solution.py:35
  40.2 6.5 %collective-permute-done.4 = f32[2,4,4,4,8,128]{5,4,3,2,1,0:T(8,128)S(1)} collective-permute-done((f32[2,4,4,4,8,128]{5,4,3,2,1,0:T(8,128)S(1)}, f32[2,4,4,4,8,128]{5,4,3,2,1,0:T(8,128)S(1)}, u32[]{:S(2)}, u32[]{:S(2)}) %collective-permute-start.4) | collective-permute-done | bytes 524320 | tf_op jit(solution)/shard_map/ppermute | solution.py:35
  46.7 5.6 %collective-permute-done.6 = f32[2,4,4,4,8,128]{5,4,3,2,1,0:T(8,128)S(1)} collective-permute-done((f32[2,4,4,4,8,128]{5,4,3,2,1,0:T(8,128)}, f32[2,4,4,4,8,128]{5,4,3,2,1,0:T(8,128)S(1)}, u32[]{:S(2)}, u32[]{:S(2)}) %collective-permute-start.6) | collective-permute-done | bytes 524320 | tf_op jit(solution)/shard_map/ppermute | solution.py:35
  52.4 1.2 add.82
  53.8 2.8 %collective-permute-start.8 = (f32[2,2,2,2,2,6,8,128]{7,6,5,4,3,2,1,0:T(8,128)S(1)}, f32[2,2,2,2,2,6,8,128]{7,6,5,4,3,2,1,0:T(8,128)S(1)}, u32[]{:S(2)}, u32[]{:S(2)}) collective-permute-start(f32[2,2,2,2,2,6,8,128]{7,6,5,4,3,2,1,0:T(8,128)S(1)} %pad_maximum_fusion.1), channel_id=1, source_target_pairs={{0,32},{1,225},{2,34},{3,227},{4,36},{5,229},{6,38},{7,231},{8,40}... | collective-permute-start | bytes 2359304 | tf_op jit(solution)/shard_map/ppermute | solution.py:35
  56.5 0.2 add.80
  56.9 2.7 %collective-permute-start.7 = (f32[2,2,2,2,2,6,8,128]{7,6,5,4,3,1,0,2:T(8,128)S(1)}, f32[2,2,2,2,2,6,8,128]{7,6,5,4,3,1,0,2:T(8,128)S(1)}, u32[]{:S(2)}, u32[]{:S(2)}) collective-permute-start(f32[2,2,2,2,2,6,8,128]{7,6,5,4,3,1,0,2:T(8,128)S(1)} %bitcast.87), channel_id=1, source_target_pairs={{0,2},{1,7},{2,0},{3,5},{4,6},{5,3},{6,4},{7,1},{8,10},{9,15},{10,... | collective-permute-start | bytes 2359304 | tf_op jit(solution)/shard_map/ppermute | solution.py:37
  59.7 0.3 collective-permute-start.9
  60.1 8.9 %collective-permute-done.9 = f32[2,2,2,2,2,4,8,128]{7,6,5,4,3,2,0,1:T(8,128)S(1)} collective-permute-done((f32[2,2,2,2,2,4,8,128]{7,6,5,4,3,2,0,1:T(8,128)S(1)}, f32[2,2,2,2,2,4,8,128]{7,6,5,4,3,2,0,1:T(8,128)S(1)}, u32[]{:S(2)}, u32[]{:S(2)}) %collective-permute-start.9) | collective-permute-done | bytes 524320 | tf_op jit(solution)/shard_map/ppermute | solution.py:37
  69.1 0.3 collective-permute-start.11
  69.4 0.1 fusion
  69.5 0.1 collective-permute-start.10
  69.8 2.7 %collective-permute-start.12 = (f32[2,2,2,2,4,8,128]{6,5,4,3,2,1,0:T(8,128)S(1)}, f32[2,2,2,2,4,8,128]{6,5,4,3,2,1,0:T(8,128)S(1)}, u32[]{:S(2)}, u32[]{:S(2)}) collective-permute-start(f32[2,2,2,2,4,8,128]{6,5,4,3,2,1,0:T(8,128)S(1)} %slice_bitcast_fusion.11), channel_id=1, source_target_pairs={{0,2},{1,7},{2,0},{3,5},{4,6},{5,3},{6,4},{7,1},{8,10},{9,15},{10,... | collective-permute-start | bytes 786440 | tf_op jit(solution)/shard_map/ppermute | solution.py:37
  72.4 3.9 %collective-permute-done.12 = f32[2,2,2,2,4,8,128]{6,5,4,3,2,1,0:T(8,128)S(1)} collective-permute-done((f32[2,2,2,2,4,8,128]{6,5,4,3,2,1,0:T(8,128)S(1)}, f32[2,2,2,2,4,8,128]{6,5,4,3,2,1,0:T(8,128)S(1)}, u32[]{:S(2)}, u32[]{:S(2)}) %collective-permute-start.12) | collective-permute-done | bytes 262176 | tf_op jit(solution)/shard_map/ppermute | solution.py:37
  76.3 0.7 collective-permute-done.11
  77.0 0.4 collective-permute-done.10
  77.8 0.3 collective-permute-start.13
  78.1 8.0 %collective-permute-done.13 = f32[2,2,2,16,8,128]{5,4,3,2,1,0:T(8,128)S(1)} collective-permute-done((f32[2,2,2,16,8,128]{5,4,3,2,1,0:T(8,128)S(1)}, f32[2,2,2,16,8,128]{5,4,3,2,1,0:T(8,128)S(1)}, u32[]{:S(2)}, u32[]{:S(2)}) %collective-permute-start.13) | collective-permute-done | bytes 524320 | tf_op jit(solution)/shard_map/ppermute | solution.py:37
  86.3 5.2 %collective-permute-done.14 = f32[2,2,16,8,128]{4,3,2,1,0:T(8,128)S(1)} collective-permute-done((f32[2,2,16,8,128]{4,3,2,1,0:T(8,128)S(1)}, f32[2,2,16,8,128]{4,3,2,1,0:T(8,128)S(1)}, u32[]{:S(2)}, u32[]{:S(2)}) %collective-permute-start.14) | collective-permute-done | bytes 262176 | tf_op jit(solution)/shard_map/ppermute | solution.py:37
  91.8 0.7 copy.23
  92.5 6.2 %collective-permute-done.15 = f32[2,16,8,128]{3,2,1,0:T(8,128)S(1)} collective-permute-done((f32[2,16,8,128]{3,2,1,0:T(8,128)S(1)}, f32[2,16,8,128]{3,2,1,0:T(8,128)S(1)}, u32[]{:S(2)}, u32[]{:S(2)}) %collective-permute-start.15) | collective-permute-done | bytes 131104 | tf_op jit(solution)/shard_map/ppermute | solution.py:35
  98.7 0.4 collective-permute-start.16
  99.1 0.6 maximum_bitcast_fusion.row_old
  99.7 5.0 %collective-permute-done.16 = f32[16,8,128]{2,1,0:T(8,128)S(1)} collective-permute-done((f32[16,8,128]{2,1,0:T(8,128)S(1)}, f32[16,8,128]{2,1,0:T(8,128)S(1)}, u32[]{:S(2)}, u32[]{:S(2)}) %collective-permute-start.16) | collective-permute-done | bytes 65568 | tf_op jit(solution)/shard_map/ppermute | solution.py:35
  104.7 0.6 fusion.9.units
  105.4 1.8 %stats.1 = (f32[8,32,128]{2,1,0:T(8,128)}, f32[16,128]{1,0:T(8,128)}) custom-call(s32[2]{0:T(128)} %pad_add_fusion.pos, f32[16,8,128]{2,1,0:T(8,128)} %fusion.9.units, f32[32,2]{1,0:T(8,128)} %bitcast.88, f32[1,128]{1,0:T(1,128)} %maximum_bitcast_fusion.row_old), custom_call_target="tpu_custom_call" | custom-call | tf_op jit(solution)/shard_map/stats/pallas_call | solution.py:234
  107.2 1.7 %collective-permute-start.17 = (f32[16,128]{1,0:T(8,128)}, f32[16,128]{1,0:T(8,128)S(1)}, u32[]{:S(2)}, u32[]{:S(2)}) collective-permute-start(f32[16,128]{1,0:T(8,128)} %get-tuple-element.51), channel_id=1, source_target_pairs={{0,1},{1,0},{2,3},{3,2},{4,5},{5,4},{6,7},{7,6},{8,9},{9,8},{10,11... | collective-permute-start | bytes 24584 | tf_op jit(solution)/shard_map/ppermute | solution.py:24
  108.9 1.0 collective-permute-done.17
  109.9 0.7 add.97
  110.7 3.8 %collective-permute-start.19 = (f32[16,128]{1,0:T(8,128)S(1)}, f32[16,128]{1,0:T(8,128)S(1)}, u32[]{:S(2)}, u32[]{:S(2)}) collective-permute-start(f32[16,128]{1,0:T(8,128)S(1)} %add.97), channel_id=1, source_target_pairs={{0,16},{1,17},{2,18},{3,19},{4,20},{5,21},{6,22},{7,23},{8,24},{9,... | collective-permute-start | bytes 24584 | tf_op jit(solution)/shard_map/ppermute | solution.py:247
  114.5 1.1 collective-permute-done.19
  115.7 2.6 %collective-permute-done.20 = f32[16,128]{1,0:T(8,128)S(1)} collective-permute-done((f32[16,128]{1,0:T(8,128)S(1)}, f32[16,128]{1,0:T(8,128)S(1)}, u32[]{:S(2)}, u32[]{:S(2)}) %collective-permute-start.20) | collective-permute-done | bytes 8224 | tf_op jit(solution)/shard_map/ppermute | solution.py:247
  118.3 3.8 %collective-permute-start.22 = (f32[16,128]{1,0:T(8,128)S(1)}, f32[16,128]{1,0:T(8,128)S(1)}, u32[]{:S(2)}, u32[]{:S(2)}) collective-permute-start(f32[16,128]{1,0:T(8,128)S(1)} %add_add_fusion.1), channel_id=1, source_target_pairs={{0,4},{1,5},{2,6},{3,7},{4,0},{5,1},{6,2},{7,3},{8,12},{9,13},{10,... | collective-permute-start | bytes 24584 | tf_op jit(solution)/shard_map/ppermute | solution.py:247
  122.1 1.1 collective-permute-done.22
  123.2 2.8 %collective-permute-done.23 = f32[16,128]{1,0:T(8,128)S(1)} collective-permute-done((f32[16,128]{1,0:T(8,128)S(1)}, f32[16,128]{1,0:T(8,128)S(1)}, u32[]{:S(2)}, u32[]{:S(2)}) %collective-permute-start.23) | collective-permute-done | bytes 8224 | tf_op jit(solution)/shard_map/ppermute | solution.py:247
  126.0 0.9 slice_add_fusion
  126.9 14.4 %all_to_all.5.load = f32[8,32,128]{2,1,0:T(8,128)} all-to-all(f32[8,32,128]{2,1,0:T(8,128)S(1)} %pad_maximum_fusion.2), channel_id=1, replica_groups=mesh['row'=8,'col'=32] {'row'}, dimensions={0} | all-to-all | bytes 262144 | tf_op jit(solution)/shard_map/all_to_all | solution.py:250
  141.4 1.9 %finish.1 = (f32[64,256]{1,0:T(8,128)}, f32[1,64]{1,0:T(1,128)}, f32[2,256]{1,0:T(2,128)}) custom-call(s32[2]{0:T(128)} %pad_add_fusion.pos, f32[8,32,128]{2,1,0:T(8,128)} %all_to_all.5.load), custom_call_target="tpu_custom_call" | custom-call | tf_op jit(solution)/shard_map/finish/pallas_call | solution.py:252
  (59 shorter events, 1.8 us)
Async XLA Ops:
  0.6 91.1 %copy-start = (f32[2,256]{1,0:T(2,128)S(1)}, f32[2,256]{1,0:T(2,128)}, u32[]{:S(2)}) copy-start(f32[2,256]{1,0:T(2,128)} %param.7) | copy-start | bytes 6148
  6.4 10.4 %collective-permute-start.1 = (f32[2,4,8,16,8,128]{5,4,3,2,1,0:T(8,128)}, f32[2,4,8,16,8,128]{5,4,3,2,1,0:T(8,128)}, u32[]{:S(2)}, u32[]{:S(2)}) collective-permute-start(f32[2,4,8,16,8,128]{5,4,3,2,1,0:T(8,128)} %away1.1), channel_id=1, source_target_pairs={{0,1},{1,0},{2,3},{3,2},{4,5},{5,4},{6,7},{7,6},{8,9},{9,8},{10,11... | collective-permute-start | bytes 12582920 | tf_op jit(solution)/shard_map/ppermute | solution.py:24
  14.8 11.5 %collective-permute-start = (f32[2,4,8,16,8,128]{5,4,3,2,1,0:T(8,128)}, f32[2,4,8,16,8,128]{5,4,3,2,1,0:T(8,128)S(1)}, u32[]{:S(2)}, u32[]{:S(2)}) collective-permute-start(f32[2,4,8,16,8,128]{5,4,3,2,1,0:T(8,128)} %away0.1), channel_id=1, source_target_pairs={{0,1},{1,0},{2,3},{3,2},{4,5},{5,4},{6,7},{7,6},{8,9},{9,8},{10,11... | collective-permute-start | bytes 12582920 | tf_op jit(solution)/shard_map/ppermute | solution.py:24
  22.8 29.5 %collective-permute-start.2 = (f32[2,4,8,6,8,128]{5,4,3,2,1,0:T(8,128)}, f32[2,4,8,6,8,128]{5,4,3,2,1,0:T(8,128)S(1)}, u32[]{:S(2)}, u32[]{:S(2)}) collective-permute-start(f32[2,4,8,6,8,128]{5,4,3,2,1,0:T(8,128)} %get-tuple-element.30), channel_id=1, source_target_pairs={{0,8},{1,25},{2,10},{3,27},{4,12},{5,29},{6,14},{7,31},{8,0},{9,17... | collective-permute-start | bytes 4718600 | tf_op jit(solution)/shard_map/ppermute | solution.py:37
  23.6 10.9 %copy-start.6 = (f32[2,4,4,4,8,128]{5,4,3,2,1,0:T(8,128)S(1)}, f32[2,4,4,4,8,128]{5,4,3,2,1,0:T(8,128)}, u32[]{:S(2)}) copy-start(f32[2,4,4,4,8,128]{5,4,3,2,1,0:T(8,128)} %get-tuple-element.32) | copy-start | bytes 1572868
  23.6 28.7 %copy-start.3 = (f32[2,2,8,6,8,128]{5,4,3,2,1,0:T(8,128)S(1)}, f32[2,2,8,6,8,128]{5,4,3,2,1,0:T(8,128)}, u32[]{:S(2)}) copy-start(f32[2,2,8,6,8,128]{5,4,3,2,1,0:T(8,128)} %get-tuple-element.36) | copy-start | bytes 2359300
  23.6 28.7 %collective-permute-start.3 = (f32[2,2,8,6,8,128]{5,4,3,2,1,0:T(8,128)}, f32[2,2,8,6,8,128]{5,4,3,2,1,0:T(8,128)S(1)}, u32[]{:S(2)}, u32[]{:S(2)}) collective-permute-start(f32[2,2,8,6,8,128]{5,4,3,2,1,0:T(8,128)} %get-tuple-element.31), channel_id=1, source_target_pairs={{0,2},{1,7},{2,0},{3,5},{4,6},{5,3},{6,4},{7,1},{8,10},{9,15},{10,... | collective-permute-start | bytes 2359304 | tf_op jit(solution)/shard_map/ppermute | solution.py:37
  26.3 2.0 %copy-start.1 = (f32[2,4,8,16,8,128]{5,4,3,2,1,0:T(8,128)}, f32[2,4,8,16,8,128]{5,4,3,2,1,0:T(8,128)S(1)}, u32[]{:S(2)}) copy-start(f32[2,4,8,16,8,128]{5,4,3,2,1,0:T(8,128)S(1)} %collective-permute-done.refs_5_) | copy-start | bytes 12582916
  34.3 22.2 %copy-start.2 = (f32[2,4,8,6,8,128]{5,4,3,2,1,0:T(8,128)S(1)}, f32[2,4,8,6,8,128]{5,4,3,2,1,0:T(8,128)}, u32[]{:S(2)}) copy-start(f32[2,4,8,6,8,128]{5,4,3,2,1,0:T(8,128)} %get-tuple-element.29) | copy-start | bytes 4718596
  34.3 18.0 %collective-permute-start.5 = (f32[2,2,8,6,8,128]{5,4,3,2,1,0:T(8,128)}, f32[2,2,8,6,8,128]{5,4,3,2,1,0:T(8,128)S(1)}, u32[]{:S(2)}, u32[]{:S(2)}) collective-permute-start(f32[2,2,8,6,8,128]{5,4,3,2,1,0:T(8,128)} %get-tuple-element.33), channel_id=1, source_target_pairs={{0,2},{1,7},{2,0},{3,5},{4,6},{5,3},{6,4},{7,1},{8,10},{9,15},{10,... | collective-permute-start | bytes 2359304 | tf_op jit(solution)/shard_map/ppermute | solution.py:37
  34.4 12.2 %collective-permute-start.4 = (f32[2,4,4,4,8,128]{5,4,3,2,1,0:T(8,128)S(1)}, f32[2,4,4,4,8,128]{5,4,3,2,1,0:T(8,128)S(1)}, u32[]{:S(2)}, u32[]{:S(2)}) collective-permute-start(f32[2,4,4,4,8,128]{5,4,3,2,1,0:T(8,128)S(1)} %copy-done.6), channel_id=1, source_target_pairs={{0,32},{1,225},{2,34},{3,227},{4,36},{5,229},{6,38},{7,231},{8,40}... | collective-permute-start | bytes 1572872 | tf_op jit(solution)/shard_map/ppermute | solution.py:35
  40.1 12.2 %collective-permute-start.6 = (f32[2,4,4,4,8,128]{5,4,3,2,1,0:T(8,128)}, f32[2,4,4,4,8,128]{5,4,3,2,1,0:T(8,128)S(1)}, u32[]{:S(2)}, u32[]{:S(2)}) collective-permute-start(f32[2,4,4,4,8,128]{5,4,3,2,1,0:T(8,128)} %get-tuple-element.34), channel_id=1, source_target_pairs={{0,32},{1,225},{2,34},{3,227},{4,36},{5,229},{6,38},{7,231},{8,40}... | collective-permute-start | bytes 1572872 | tf_op jit(solution)/shard_map/ppermute | solution.py:35
  53.8 15.3 %collective-permute-start.8 = (f32[2,2,2,2,2,6,8,128]{7,6,5,4,3,2,1,0:T(8,128)S(1)}, f32[2,2,2,2,2,6,8,128]{7,6,5,4,3,2,1,0:T(8,128)S(1)}, u32[]{:S(2)}, u32[]{:S(2)}) collective-permute-start(f32[2,2,2,2,2,6,8,128]{7,6,5,4,3,2,1,0:T(8,128)S(1)} %pad_maximum_fusion.1), channel_id=1, source_target_pairs={{0,32},{1,225},{2,34},{3,227},{4,36},{5,229},{6,38},{7,231},{8,40}... | collective-permute-start | bytes 2359304 | tf_op jit(solution)/shard_map/ppermute | solution.py:35
  56.5 3.1 %copy-start.4 = (f32[2,4,4,4,8,128]{5,4,3,2,1,0:T(8,128)S(1)}, f32[2,4,4,4,8,128]{5,4,3,2,1,0:T(8,128)}, u32[]{:S(2)}) copy-start(f32[2,4,4,4,8,128]{5,4,3,2,1,0:T(8,128)} %get-tuple-element.40) | copy-start | bytes 1572868
  56.7 3.3 %copy-start.5 = (f32[2,4,4,4,8,128]{5,4,3,2,1,0:T(8,128)S(1)}, f32[2,4,4,4,8,128]{5,4,3,2,1,0:T(8,128)}, u32[]{:S(2)}) copy-start(f32[2,4,4,4,8,128]{5,4,3,2,1,0:T(8,128)} %get-tuple-element.44) | copy-start | bytes 1572868
  56.9 12.1 %collective-permute-start.7 = (f32[2,2,2,2,2,6,8,128]{7,6,5,4,3,1,0,2:T(8,128)S(1)}, f32[2,2,2,2,2,6,8,128]{7,6,5,4,3,1,0,2:T(8,128)S(1)}, u32[]{:S(2)}, u32[]{:S(2)}) collective-permute-start(f32[2,2,2,2,2,6,8,128]{7,6,5,4,3,1,0,2:T(8,128)S(1)} %bitcast.87), channel_id=1, source_target_pairs={{0,2},{1,7},{2,0},{3,5},{4,6},{5,3},{6,4},{7,1},{8,10},{9,15},{10,... | collective-permute-start | bytes 2359304 | tf_op jit(solution)/shard_map/ppermute | solution.py:37
  59.7 9.3 %collective-permute-start.9 = (f32[2,2,2,2,2,4,8,128]{7,6,5,4,3,2,0,1:T(8,128)S(1)}, f32[2,2,2,2,2,4,8,128]{7,6,5,4,3,2,0,1:T(8,128)S(1)}, u32[]{:S(2)}, u32[]{:S(2)}) collective-permute-start(f32[2,2,2,2,2,4,8,128]{7,6,5,4,3,2,0,1:T(8,128)S(1)} %copy.12), channel_id=1, source_target_pairs={{0,8},{1,25},{2,10},{3,27},{4,12},{5,29},{6,14},{7,31},{8,0},{9,17... | collective-permute-start | bytes 1572872 | tf_op jit(solution)/shard_map/ppermute | solution.py:37
  69.1 7.9 %collective-permute-start.11 = (f32[2,2,2,2,6,8,128]{6,5,4,3,2,1,0:T(8,128)S(1)}, f32[2,2,2,2,6,8,128]{6,5,4,3,2,1,0:T(8,128)S(1)}, u32[]{:S(2)}, u32[]{:S(2)}) collective-permute-start(f32[2,2,2,2,6,8,128]{6,5,4,3,2,1,0:T(8,128)S(1)} %fusion.4), channel_id=1, source_target_pairs={{0,8},{1,25},{2,10},{3,27},{4,12},{5,29},{6,14},{7,31},{8,0},{9,17... | collective-permute-start | bytes 1179656 | tf_op jit(solution)/shard_map/ppermute | solution.py:37
  69.5 7.9 %collective-permute-start.10 = (f32[2,2,2,2,6,8,128]{6,5,4,3,2,1,0:T(8,128)S(1)}, f32[2,2,2,2,6,8,128]{6,5,4,3,2,1,0:T(8,128)S(1)}, u32[]{:S(2)}, u32[]{:S(2)}) collective-permute-start(f32[2,2,2,2,6,8,128]{6,5,4,3,2,1,0:T(8,128)S(1)} %slice_bitcast_fusion.4), channel_id=1, source_target_pairs={{0,32},{1,225},{2,34},{3,227},{4,36},{5,229},{6,38},{7,231},{8,40}... | collective-permute-start | bytes 1179656 | tf_op jit(solution)/shard_map/ppermute | solution.py:35
  69.8 6.5 %collective-permute-start.12 = (f32[2,2,2,2,4,8,128]{6,5,4,3,2,1,0:T(8,128)S(1)}, f32[2,2,2,2,4,8,128]{6,5,4,3,2,1,0:T(8,128)S(1)}, u32[]{:S(2)}, u32[]{:S(2)}) collective-permute-start(f32[2,2,2,2,4,8,128]{6,5,4,3,2,1,0:T(8,128)S(1)} %slice_bitcast_fusion.11), channel_id=1, source_target_pairs={{0,2},{1,7},{2,0},{3,5},{4,6},{5,3},{6,4},{7,1},{8,10},{9,15},{10,... | collective-permute-start | bytes 786440 | tf_op jit(solution)/shard_map/ppermute | solution.py:37
  77.6 21.5 %copy-start.7 = (f32[64]{0:T(128)S(1)}, f32[64]{0:T(128)}, u32[]{:S(2)}) copy-start(f32[64]{0:T(128)} %param.6) | copy-start | bytes 772
  77.8 8.3 %collective-permute-start.13 = (f32[2,2,2,16,8,128]{5,4,3,2,1,0:T(8,128)S(1)}, f32[2,2,2,16,8,128]{5,4,3,2,1,0:T(8,128)S(1)}, u32[]{:S(2)}, u32[]{:S(2)}) collective-permute-start(f32[2,2,2,16,8,128]{5,4,3,2,1,0:T(8,128)S(1)} %slice_bitcast_fusion), channel_id=1, source_target_pairs={{0,24},{1,9},{2,26},{3,11},{4,28},{5,13},{6,30},{7,15},{8,16},{9,1... | collective-permute-start | bytes 1572872 | tf_op jit(solution)/shard_map/ppermute | solution.py:37
  86.2 5.3 %collective-permute-start.14 = (f32[2,2,16,8,128]{4,3,2,1,0:T(8,128)S(1)}, f32[2,2,16,8,128]{4,3,2,1,0:T(8,128)S(1)}, u32[]{:S(2)}, u32[]{:S(2)}) collective-permute-start(f32[2,2,16,8,128]{4,3,2,1,0:T(8,128)S(1)} %slice_bitcast_fusion.8), channel_id=1, source_target_pairs={{0,6},{1,3},{2,4},{3,1},{4,2},{5,7},{6,0},{7,5},{8,14},{9,11},{10,... | collective-permute-start | bytes 786440 | tf_op jit(solution)/shard_map/ppermute | solution.py:37
  91.6 7.1 %collective-permute-start.15 = (f32[2,16,8,128]{3,2,1,0:T(8,128)S(1)}, f32[2,16,8,128]{3,2,1,0:T(8,128)S(1)}, u32[]{:S(2)}, u32[]{:S(2)}) collective-permute-start(f32[2,16,8,128]{3,2,1,0:T(8,128)S(1)} %slice_bitcast_fusion.12), channel_id=1, source_target_pairs={{0,64},{1,65},{2,66},{3,67},{4,68},{5,69},{6,70},{7,71},{8,72},{9,... | collective-permute-start | bytes 393224 | tf_op jit(solution)/shard_map/ppermute | solution.py:35
  98.7 6.0 %collective-permute-start.16 = (f32[16,8,128]{2,1,0:T(8,128)S(1)}, f32[16,8,128]{2,1,0:T(8,128)S(1)}, u32[]{:S(2)}, u32[]{:S(2)}) collective-permute-start(f32[16,8,128]{2,1,0:T(8,128)S(1)} %slice_bitcast_fusion.14), channel_id=1, source_target_pairs={{0,192},{1,193},{2,194},{3,195},{4,196},{5,197},{6,198},{7,199},{8... | collective-permute-start | bytes 196616 | tf_op jit(solution)/shard_map/ppermute | solution.py:35
  107.2 2.7 %collective-permute-start.17 = (f32[16,128]{1,0:T(8,128)}, f32[16,128]{1,0:T(8,128)S(1)}, u32[]{:S(2)}, u32[]{:S(2)}) collective-permute-start(f32[16,128]{1,0:T(8,128)} %get-tuple-element.51), channel_id=1, source_target_pairs={{0,1},{1,0},{2,3},{3,2},{4,5},{5,4},{6,7},{7,6},{8,9},{9,8},{10,11... | collective-permute-start | bytes 24584 | tf_op jit(solution)/shard_map/ppermute | solution.py:24
  110.6 3.9 %collective-permute-start.18 = (f32[16,128]{1,0:T(8,128)S(1)}, f32[16,128]{1,0:T(8,128)S(1)}, u32[]{:S(2)}, u32[]{:S(2)}) collective-permute-start(f32[16,128]{1,0:T(8,128)S(1)} %add.97), channel_id=1, source_target_pairs={{0,8},{1,9},{2,10},{3,11},{4,12},{5,13},{6,14},{7,15},{8,0},{9,1},... | collective-permute-start | bytes 24584 | tf_op jit(solution)/shard_map/ppermute | solution.py:247
  110.7 5.0 %collective-permute-start.19 = (f32[16,128]{1,0:T(8,128)S(1)}, f32[16,128]{1,0:T(8,128)S(1)}, u32[]{:S(2)}, u32[]{:S(2)}) collective-permute-start(f32[16,128]{1,0:T(8,128)S(1)} %add.97), channel_id=1, source_target_pairs={{0,16},{1,17},{2,18},{3,19},{4,20},{5,21},{6,22},{7,23},{8,24},{9,... | collective-permute-start | bytes 24584 | tf_op jit(solution)/shard_map/ppermute | solution.py:247
  114.5 3.7 %collective-permute-start.20 = (f32[16,128]{1,0:T(8,128)S(1)}, f32[16,128]{1,0:T(8,128)S(1)}, u32[]{:S(2)}, u32[]{:S(2)}) collective-permute-start(f32[16,128]{1,0:T(8,128)S(1)} %add.97), channel_id=1, source_target_pairs={{0,24},{1,25},{2,26},{3,27},{4,28},{5,29},{6,30},{7,31},{8,16},{9,... | collective-permute-start | bytes 24584 | tf_op jit(solution)/shard_map/ppermute | solution.py:247
  118.2 3.9 %collective-permute-start.21 = (f32[16,128]{1,0:T(8,128)S(1)}, f32[16,128]{1,0:T(8,128)S(1)}, u32[]{:S(2)}, u32[]{:S(2)}) collective-permute-start(f32[16,128]{1,0:T(8,128)S(1)} %add_add_fusion.1), channel_id=1, source_target_pairs={{0,2},{1,3},{2,0},{3,1},{4,6},{5,7},{6,4},{7,5},{8,10},{9,11},{10,... | collective-permute-start | bytes 24584 | tf_op jit(solution)/shard_map/ppermute | solution.py:247
  118.3 5.0 %collective-permute-start.22 = (f32[16,128]{1,0:T(8,128)S(1)}, f32[16,128]{1,0:T(8,128)S(1)}, u32[]{:S(2)}, u32[]{:S(2)}) collective-permute-start(f32[16,128]{1,0:T(8,128)S(1)} %add_add_fusion.1), channel_id=1, source_target_pairs={{0,4},{1,5},{2,6},{3,7},{4,0},{5,1},{6,2},{7,3},{8,12},{9,13},{10,... | collective-permute-start | bytes 24584 | tf_op jit(solution)/shard_map/ppermute | solution.py:247
  122.1 3.9 %collective-permute-start.23 = (f32[16,128]{1,0:T(8,128)S(1)}, f32[16,128]{1,0:T(8,128)S(1)}, u32[]{:S(2)}, u32[]{:S(2)}) collective-permute-start(f32[16,128]{1,0:T(8,128)S(1)} %add_add_fusion.1), channel_id=1, source_target_pairs={{0,6},{1,7},{2,4},{3,5},{4,2},{5,3},{6,0},{7,1},{8,14},{9,15},{10,... | collective-permute-start | bytes 24584 | tf_op jit(solution)/shard_map/ppermute | solution.py:247

commit v3 on v2

--- a/solution.py
+++ b/solution.py
@@ -13,11 +13,12 @@
 EPSILON = 1e-30
 CLIP_LIMIT = 1.0
 MIB = 1024 * 1024
+GRANTS = (52, 44, 20, 20)
 
 RING4 = ((1, 3), (3, 1))
 RING8 = (1, 2, 6)
 Z_MASKS = [i * RING8[0] ^ j * RING8[1] ^ k * RING8[2] for i in (0, 1) for j in (0, 1) for k in (0, 1)]
-UNITS = ((0, 6), (6, 12), (12, 16))
+UNITS = ((0, 6), (6, 11), (11, 16))
 
 
 def swap_cores(value):
@@ -33,44 +34,48 @@
                 to = ((((z + core) % 8) ^ RING8[step]) + 8 - core) % 8
                 pairs.append((z * 32 + i, to * 32 + i))
         return lax.ppermute(value, ("row", "col"), pairs)
-    shift = 3 if axis == "x" else 1
-    return lax.ppermute(value, "col", [(i, i ^ (RING4[i % 2][step] << shift)) for i in range(32)])
+    unit = sum({"x": 8, "y": 2}[name] for name in axis)
+    return lax.ppermute(value, "col", [(i, i ^ (RING4[i % 2][step] * unit)) for i in range(32)])
 
 
 def partial_kernel(chunk, to_sibling, pos, *refs):
-    xs, y_ref, acc = refs[:4], refs[4], refs[-1]
+    step = pl.program_id(0)
     z, core = pos[0], lax.rem(pos[1], 2)
     core = 1 - core if to_sibling else core
+    xs, y = refs[:4], refs[4]
     if to_sibling:
-        out = refs[5]
+        full = refs[5]
     else:
-        got = refs[5]
-        outs = refs[6:-1]
-    starts = [
-        pl.multiple_of(lax.rem((lax.rem(z + core, 8) ^ mask) + 8 - core, 8) * 32, 32) for mask in Z_MASKS
-    ]
+        got, a, b_send, b_keep, c = refs[5:]
+    slots = []
+    for place in range(8):
+        mask = lax.rem(place + core, 8) ^ lax.rem(z + core, 8)
+        high = lax.div(mask, 4)
+        slots.append(lax.rem(mask, 2) * 4 + (lax.rem(lax.div(mask, 2), 2) ^ high) * 2 + high)
     for s in range(4):
-        acc[s] = lax.dot_general(
-            xs[s][...], y_ref[...], (((0,), (0,)), ((), ())), preferred_element_type=jnp.float32
+        value = lax.dot_general(
+            xs[s][...], y[...], (((0,), (0,)), ((), ())), preferred_element_type=jnp.float32
         )
-        for slot in range(8):
+        for place, slot in enumerate(slots):
             for unit in range(16):
                 group, lane = divmod(unit, 4)
-                value = acc[s, pl.ds(starts[slot] + group * 8, 8), lane * 128 : lane * 128 + 128]
+                top = place * 32 + group * 8
+                piece = value[top : top + 8, lane * 128 : lane * 128 + 128]
                 if to_sibling:
-                    out[0, s, slot, unit] = value
+                    full[step, s, slot, unit] = piece
                     continue
-                value = value + got[0, s, slot, unit]
-                if unit < 6:
-                    outs[0][0, s, slot, unit] = value
-                elif unit < 12:
-                    outs[1 if s >= 2 else 2][0, s % 2, slot, unit - 6] = value
+                piece = piece + got[step, s, slot, unit]
+                if unit < UNITS[0][1]:
+                    a[step, s, slot, unit] = piece
+                elif unit < UNITS[1][1]:
+                    (b_send if s >= 2 else b_keep)[step, s % 2, slot, unit - UNITS[1][0]] = piece
                 else:
-                    outs[3 if slot >= 4 else 4][0, s, slot % 4, unit - 12] = value
-
-
-def partial(pos, x, y, chunk, got=None):
+                    c[step, s, slot, unit - UNITS[2][0]] = piece
+
+
+def partial(pos, x, y, chunk, grant, got=None):
     to_sibling = got is None
+    na, nb, nc = (to - start for start, to in UNITS)
 
     def block(s):
         def index(step, pos):
@@ -83,15 +88,12 @@
 
         return pl.BlockSpec((512, 256), index)
 
-    def whole(shape):
-        return pl.BlockSpec((1,) + shape[1:], lambda step, pos: (step,) + (0,) * (len(shape) - 1))
-
-    full = (2, 4, 8, 16, 8, 128)
     if to_sibling:
-        shapes = [full]
+        shapes = [(2, 4, 8, 16, 8, 128)]
     else:
-        part_b, part_c = (2, 2, 8, 6, 8, 128), (2, 4, 4, 4, 8, 128)
-        shapes = [(2, 4, 8, 6, 8, 128), part_b, part_b, part_c, part_c]
+        part_b, part_c = (2, 2, 8, nb, 8, 128), (2, 4, 8, nc, 8, 128)
+        shapes = [(2, 4, 8, na, 8, 128), part_b, part_b, part_c]
+    whole = pl.BlockSpec(memory_space=pltpu.VMEM)
     return pl.pallas_call(
         functools.partial(partial_kernel, chunk, to_sibling),
         grid_spec=pltpu.PrefetchScalarGridSpec(
@@ -99,12 +101,11 @@
             grid=(2,),
             in_specs=[block(s) for s in range(4)]
             + [pl.BlockSpec((512, 512), lambda step, pos: (0, 0))]
-            + ([] if to_sibling else [whole(full)]),
-            out_specs=[whole(s) for s in shapes],
-            scratch_shapes=[pltpu.VMEM((4, 256, 512), jnp.float32)],
+            + ([] if to_sibling else [whole]),
+            out_specs=[whole] * len(shapes),
         ),
-        out_shape=[jax.ShapeDtypeStruct(s, jnp.float32) for s in shapes],
-        compiler_params=pltpu.CompilerParams(vmem_limit_bytes=56 * MIB),
+        out_shape=[pltpu.VMEM(s, jnp.float32) for s in shapes],
+        compiler_params=pltpu.CompilerParams(vmem_limit_bytes=grant * MIB),
         cost_estimate=pl.CostEstimate(
             flops=2 * 512 * 512 * 2048, bytes_accessed=(7 if to_sibling else 11) * MIB, transcendentals=0
         ),
@@ -148,13 +149,11 @@
             high = jnp.where(upper, 0.0, pltpu.roll(scaled, 64, 1))
             tile[2 * i, group * 8 : group * 8 + 8] = low
             tile[2 * i + 1, group * 8 : group * 8 + 8] = high
-    for base, rows in ((0, squares_of), (8, raised_of)):
-        value = jnp.zeros((8, 128), jnp.float32)
-        for i in range(4):
-            both = jnp.broadcast_to(rows[i], (8, 128))
-            value = jnp.where(sub == 2 * i, pltpu.roll(both, 64, 1), value)
-            value = jnp.where(sub == 2 * i + 1, both, value)
-        stats[base : base + 8] = jnp.where(upper, value, 0.0)
+    value = jnp.zeros((8, 128), jnp.float32)
+    for i, row in enumerate(squares_of + raised_of):
+        value = jnp.where(sub == i, jnp.broadcast_to(row, (8, 128)), value)
+    for to in range(32):
+        stats[to] = value
     olds = jnp.where((sub == z) & upper, jnp.broadcast_to(row_old[...], (8, 128)), 0.0)
     cols = jnp.zeros((8, 128), jnp.float32)
     for m in range(2):
@@ -162,6 +161,26 @@
     for to in range(8):
         tile[to, 16:24] = tile[to, 16:24] + olds
         tile[to, 24:32] = tile[to, 24:32] + cols
+
+
+def pack_kernel(tile, stats, load):
+    sub = lax.broadcasted_iota(jnp.int32, (8, 128), 0)
+    upper = lax.broadcasted_iota(jnp.int32, (8, 128), 1) >= 64
+    sums = [stats[i] for i in range(32)]
+    while len(sums) > 1:
+        sums = [p + q for p, q in zip(sums[::2], sums[1::2])]
+    placed = []
+    for base in (0, 4):
+        value = jnp.zeros((8, 128), jnp.float32)
+        for i in range(4):
+            both = jnp.broadcast_to(sums[0][base + i : base + i + 1], (8, 128))
+            value = jnp.where(sub == 2 * i, pltpu.roll(both, 64, 1), value)
+            value = jnp.where(sub == 2 * i + 1, both, value)
+        placed.append(jnp.where(upper, value, 0.0))
+    for to in range(8):
+        load[to, 0:8] = tile[to, 0:8] + placed[0]
+        load[to, 8:16] = tile[to, 8:16] + placed[1]
+        load[to, 16:32] = tile[to, 16:32]
 
 
 def finish_kernel(pos, load, direction, row_new, col_new, scales, rows):
@@ -202,34 +221,43 @@
     col_old = lax.dynamic_slice_in_dim(col_state, z * 32, 32, axis=1).T
     row_old = jnp.concatenate([row_state, row_state]).reshape(1, 128)
 
-    sent = [swap_cores(partial(pos, activations, kv_grads, chunk)[0]) for chunk in (1, 0)]
-    a_send, b_send1, b_keep1, c_send1, c_keep1 = partial(pos, activations, kv_grads, 1, sent[0])
-    a_keep, b_send0, b_keep0, c_send0, c_keep0 = partial(pos, activations, kv_grads, 0, sent[1])
-
+    x, y = activations, kv_grads
+    sent1 = swap_cores(partial(pos, x, y, 1, GRANTS[0])[0])
+    sent0 = swap_cores(partial(pos, x, y, 0, GRANTS[1])[0])
+    a_send, b_send1, b_keep1, c1 = partial(pos, x, y, 1, GRANTS[2], sent1)
+    a_keep, b_send0, b_keep0, c0 = partial(pos, x, y, 0, GRANTS[3], sent0)
+    c_send1, c_keep1, c_send0, c_keep0 = c1[:, :, 4:], c1[:, :, :4], c0[:, :, 4:], c0[:, :, :4]
+
+    na, nb, nc = (to - start for start, to in UNITS)
     got = along("x", 0, a_send), along("y", 0, b_send1), along("z", 0, c_send1)
     got = got + (along("y", 0, b_send0), along("z", 0, c_send0))
-    got = lax.optimization_barrier(got)
-    a = (a_keep + got[0]).reshape(2, 2, 2, 2, 2, 2, 6, 8, 128)
-    b1 = (b_keep1 + got[1]).reshape(2, 2, 2, 2, 2, 6, 8, 128)
-    b0 = (b_keep0 + got[3]).reshape(2, 2, 2, 2, 2, 6, 8, 128)
-    c1 = (c_keep1 + got[2]).reshape(2, 2, 2, 2, 2, 4, 8, 128)
-    c0 = (c_keep0 + got[4]).reshape(2, 2, 2, 2, 2, 4, 8, 128)
-
-    got = along("y", 0, a[:, 1]), along("z", 0, jnp.stack([b1[:, :, 1], b0[:, :, 1]])), along("x", 0, c1)
-    got = lax.optimization_barrier(got)
-    a = a[:, 0] + got[0]
-    b1, b0 = b1[:, :, 0] + got[1][0], b0[:, :, 0] + got[1][1]
-    c = c0 + got[2]
-
-    got = along("z", 0, a[:, :, 1]), along("x", 0, b1), along("y", 0, c[:, 1])
-    got = lax.optimization_barrier(got)
-    a = a[:, :, 0] + got[0]
-    b = b0 + got[1]
-    c = c[:, 0] + got[2]
-
-    value = jnp.concatenate([a, b, c], axis=4)
-    for axis, step in (("x", 1), ("y", 1), ("z", 1), ("z", 2)):
-        value = value[0] + along(axis, step, value[1])
+    ga, gb1, gc1, gb0, gc0 = lax.optimization_barrier(got)
+    a, ga = (v.reshape(2, 2, 2, 2, 2, 2, na, 8, 128) for v in (a_keep, ga))
+    b1, b0, gb1, gb0 = (v.reshape(2, 2, 2, 2, 2, nb, 8, 128) for v in (b_keep1, b_keep0, gb1, gb0))
+    c1, c0, gc1, gc0 = (v.reshape(2, 2, 2, 2, 2, nc, 8, 128) for v in (c_keep1, c_keep0, gc1, gc0))
+
+    a_send = a[:, 1] + ga[:, 1]
+    b_send = jnp.stack([b1[:, :, 1] + gb1[:, :, 1], b0[:, :, 1] + gb0[:, :, 1]])
+    got = along("y", 0, a_send), along("z", 0, b_send), along("x", 0, c1 + gc1)
+    a = a[:, 0] + ga[:, 0]
+    b1, b0 = b1[:, :, 0] + gb1[:, :, 0], b0[:, :, 0] + gb0[:, :, 0]
+    c = c0 + gc0
+    ga, gb, gc = lax.optimization_barrier(got)
+
+    a_send = a[:, :, 1] + ga[:, :, 1]
+    got = along("z", 0, a_send), along("x", 0, b1 + gb[0]), along("y", 0, c[:, 1] + gc[:, 1])
+    a = a[:, :, 0] + ga[:, :, 0]
+    b = b0 + gb[1]
+    c = c[:, 0] + gc[:, 0]
+    ga, gb, gc = lax.optimization_barrier(got)
+
+    def quarter(i, j):
+        return jnp.concatenate([v[i, j] + g[i, j] for v, g in ((a, ga), (b, gb), (c, gc))], axis=2)
+
+    got = along("xy", 1, quarter(1, 1)), along("x", 1, quarter(1, 0)), along("y", 1, quarter(0, 1))
+    value = quarter(0, 0) + got[0] + got[1] + got[2]
+    for step in (1, 2):
+        value = value[0] + along("z", step, value[1])
 
     tile, stats = pl.pallas_call(
         stats_kernel,
@@ -237,16 +265,19 @@
         out_specs=[pl.BlockSpec(memory_space=pltpu.VMEM)] * 2,
         out_shape=[
             jax.ShapeDtypeStruct((8, 32, 128), jnp.float32),
-            jax.ShapeDtypeStruct((16, 128), jnp.float32),
+            jax.ShapeDtypeStruct((32, 8, 128), jnp.float32),
         ],
         name="stats",
     )(pos, value, col_old, row_old)
 
-    stats = stats + swap_cores(stats)
-    for shift in (3, 1):
-        others = [lax.ppermute(stats, "col", [(i, i ^ (m << shift)) for i in range(32)]) for m in (1, 2, 3)]
-        stats = stats + others[0] + others[1] + others[2]
-    load = jnp.concatenate([tile[:, :16] + stats[None], tile[:, 16:]], axis=1)
+    stats = lax.all_to_all(stats, "col", 0, 0, tiled=True)
+    load = pl.pallas_call(
+        pack_kernel,
+        in_specs=[pl.BlockSpec(memory_space=pltpu.VMEM)] * 2,
+        out_specs=pl.BlockSpec(memory_space=pltpu.VMEM),
+        out_shape=jax.ShapeDtypeStruct((8, 32, 128), jnp.float32),
+        name="pack",
+    )(tile, stats)
     load = lax.all_to_all(load, "row", 0, 0, tiled=True)
 
     direction, row_new, col_new = pl.pallas_call(

time: 146 us -> 127 us (0.87); the launches traced: 143 us -> 126 us
  waiting for transfers between devices: 61.2 us -> 49 us
  blocking collectives: 14.4 us -> 26.6 us
  Pallas kernels: 26 us -> 20.1 us
  starting transfers between devices: 31.7 us -> 25.8 us
  other arithmetic: 5.82 us -> 2.84 us
  local copies, waits for them, and re-layouts: 3.14 us -> 1.27 us
    ppermute x15 -> x10, waiting for transfers between devices: 34.4 us -> 21.1 us  [along(): lax.ppermute(value, 'col', [(i, i ^ RING4[i % 2][step] * unit) for i in r...]
    all_to_all x0 -> x1, blocking collectives: none -> 12.7 us  [on_device(): stats = lax.all_to_all(stats, 'col', 0, 0, tiled=True)]
    pallas_call x4, Pallas kernels: 22.3 us -> 14.7 us  [partial(): pl.pallas_call(functools.partial(partial_kernel, chunk, to_sibling), grid...]
    ppermute x15 -> x10, starting transfers between devices: 17.7 us -> 13.2 us  [along(): lax.ppermute(value, 'col', [(i, i ^ RING4[i % 2][step] * unit) for i in r...]
    add x19 -> x14, other arithmetic: 4.42 us -> 1.55 us  [the longest x2 0.65 us: on_device(): value = value[0] + along('z', step, value[1])]
    unnamed x18 -> x13, local copies, waits for them, and re-layouts: 2.74 us -> 0.72 us
    pallas_call x0 -> x1, Pallas kernels: none -> 1.7 us  [on_device(): pl.pallas_call(pack_kernel, in_specs=[pl.BlockSpec(memory_space=pltpu.VME...]
    ppermute x3 -> x2, starting transfers between devices: 4.91 us -> 3.82 us  [swap_cores(): return lax.ppermute(value, 'col', [(i, i ^ 1) for i in range(32)])]
  transfers between devices with their start and end apart: 24 -> 18, of which waited for: 16 -> 13; matrix products, arithmetic and copies ran while one was open for 2% -> 2% of each run, Pallas kernels for 12% -> 8%
where the time goes in v3:
time: 127 us; the launch traced here: 126 us
  waiting for transfers between devices  49 us (39%)
  blocking collectives  26.6 us (21%)
  starting transfers between devices  25.8 us (20%)
  Pallas kernels  20.1 us (16%)
  other arithmetic  2.84 us (2%)
  local copies, waits for them, and re-layouts  1.27 us (1%)
    ppermute x6, waiting for transfers between devices, along(): return lax.ppermute(value, ('row', 'col'), pairs)  24.8 us
    ppermute x10, waiting for transfers between devices, along(): lax.ppermute(value, 'col', [(i, i ^ RING4[i % 2][step] * unit) for i in r...  21.1 us
    pallas_call x4, Pallas kernels, partial(): pl.pallas_call(functools.partial(partial_kernel, chunk, to_sibling), grid...  14.7 us
    all_to_all x1, blocking collectives, on_device(): load = lax.all_to_all(load, 'row', 0, 0, tiled=True)  13.9 us
    ppermute x10, starting transfers between devices, along(): lax.ppermute(value, 'col', [(i, i ^ RING4[i % 2][step] * unit) for i in r...  13.2 us
    all_to_all x1, blocking collectives, on_device(): stats = lax.all_to_all(stats, 'col', 0, 0, tiled=True)  12.7 us
    ppermute x6, starting transfers between devices, along(): return lax.ppermute(value, ('row', 'col'), pairs)  8.81 us
    ppermute x2, starting transfers between devices, swap_cores(): return lax.ppermute(value, 'col', [(i, i ^ 1) for i in range(32)])  3.82 us
  transfers between devices with their start and end apart: 18, of which 13 were waited for; matrix products, arithmetic and copies ran while one was open for 2% of the time, Pallas kernels for 8%

profile of v3, /device:TPU:1, one launch (start us, length us, event | category | flops | bytes accessed | tf_op | source)
XLA Modules:
  0.0 126.4 jit_solution(14503549355564878655)
XLA Ops:
  0.6 0.6 pad_add_fusion.pos
  1.3 4.2 %away1.1 = f32[2,4,8,16,8,128]{5,4,3,2,1,0:T(8,128)S(1)} custom-call(s32[2]{0:T(128)} %pad_add_fusion.pos, bf16[512,8192]{1,0:T(8,128)(2,1)} %refs_3_.7, bf16[512,8192]{1,0:T(8,128)(2,1)} %refs_3_.7, bf16[512,8192]{1,0:T(8,128)(2,1)} %refs_3_.7, bf16[512,8192]{1,0:T(8,128)(2,1)} %refs_3_.7, bf16[512,512]{1,0:T(8,128)(2,1)} %refs_4_.7), custom_call_target="tpu_custom_call" | custom-call | flops 1073741824 | bytes 7340032 | tf_op jit(solution)/shard_map/away1/pallas_call | solution.py:97
  5.4 3.3 %collective-permute-start.1 = (f32[2,4,8,16,8,128]{5,4,3,2,1,0:T(8,128)S(1)}, f32[2,4,8,16,8,128]{5,4,3,2,1,0:T(8,128)}, u32[]{:S(2)}, u32[]{:S(2)}) collective-permute-start(f32[2,4,8,16,8,128]{5,4,3,2,1,0:T(8,128)S(1)} %away1.1), channel_id=1, source_target_pairs={{0,1},{1,0},{2,3},{3,2},{4,5},{5,4},{6,7},{7,6},{8,9},{9,8},{10,11... | collective-permute-start | bytes 12582920 | tf_op jit(solution)/shard_map/ppermute | solution.py:25
  8.8 3.4 %away0.1 = f32[2,4,8,16,8,128]{5,4,3,2,1,0:T(8,128)S(1)} custom-call(s32[2]{0:T(128)S(1)} %copy-done.2, bf16[512,8192]{1,0:T(8,128)(2,1)} %refs_3_.7, bf16[512,8192]{1,0:T(8,128)(2,1)} %refs_3_.7, bf16[512,8192]{1,0:T(8,128)(2,1)} %refs_3_.7, bf16[512,8192]{1,0:T(8,128)(2,1)} %refs_3_.7, bf16[512,512]{1,0:T(8,128)(2,1)S(1)} %copy-done.1), custom_call_target="tpu_custom_call" | custom-call | flops 1073741824 | bytes 7340032 | tf_op jit(solution)/shard_map/away0/pallas_call | solution.py:97
  12.2 0.5 collective-permute-start
  12.7 3.0 %collective-permute-done.1.refs_5_ = f32[2,4,8,16,8,128]{5,4,3,2,1,0:T(8,128)} collective-permute-done((f32[2,4,8,16,8,128]{5,4,3,2,1,0:T(8,128)S(1)}, f32[2,4,8,16,8,128]{5,4,3,2,1,0:T(8,128)}, u32[]{:S(2)}, u32[]{:S(2)}) %collective-permute-start.1) | collective-permute-done | bytes 4194336 | tf_op jit(solution)/shard_map/ppermute | solution.py:25
  15.7 4.6 %near1.1 = (f32[2,4,8,6,8,128]{5,4,3,2,1,0:T(8,128)S(1)}, f32[2,2,8,5,8,128]{5,4,3,2,1,0:T(8,128)S(1)}, f32[2,2,8,5,8,128]{5,4,3,2,1,0:T(8,128)S(1)}, f32[2,4,8,5,8,128]{5,4,3,2,1,0:T(8,128)S(1)}) custom-call(s32[2]{0:T(128)S(1)} %copy-done.2, bf16[512,8192]{1,0:T(8,128)(2,1)S(1)} %bitcast.135, bf16[512,8192]{1,0:T(8,128)(2,1)S(1)} %bitcast.135, ...), custom_call_target="tpu_custom_call" | custom-call | flops 1073741824 | bytes 11534336 | tf_op jit(solution)/shard_map/near1/pallas_call | solution.py:97
  20.3 0.8 collective-permute-start.2
  21.1 2.7 %collective-permute-start.3 = (f32[2,2,8,5,8,128]{5,4,3,2,1,0:T(8,128)S(1)}, f32[2,2,8,5,8,128]{5,4,3,2,1,0:T(8,128)S(1)}, u32[]{:S(2)}, u32[]{:S(2)}) collective-permute-start(f32[2,2,8,5,8,128]{5,4,3,2,1,0:T(8,128)S(1)} %get-tuple-element.29), channel_id=1, source_target_pairs={{0,2},{1,7},{2,0},{3,5},{4,6},{5,3},{6,4},{7,1},{8,10},{9,15},{10,... | collective-permute-start | bytes 1966088 | tf_op jit(solution)/shard_map/ppermute | solution.py:38
  23.9 5.7 %collective-permute-start.4 = (f32[2,4,4,5,8,128]{5,4,3,2,1,0:T(8,128)S(1)}, f32[2,4,4,5,8,128]{5,4,3,2,1,0:T(8,128)S(1)}, u32[]{:S(2)}, u32[]{:S(2)}) collective-permute-start(f32[2,4,4,5,8,128]{5,4,3,2,1,0:T(8,128)S(1)} %slice.163), channel_id=1, source_target_pairs={{0,32},{1,225},{2,34},{3,227},{4,36},{5,229},{6,38},{7,231},{8,40}... | collective-permute-start | bytes 1966088 | tf_op jit(solution)/shard_map/ppermute | solution.py:36
  29.6 2.6 %near0.1 = (f32[2,4,8,6,8,128]{5,4,3,2,1,0:T(8,128)S(1)}, f32[2,2,8,5,8,128]{5,4,3,2,1,0:T(8,128)S(1)}, f32[2,2,8,5,8,128]{5,4,3,2,1,0:T(8,128)S(1)}, f32[2,4,8,5,8,128]{5,4,3,2,1,0:T(8,128)S(1)}) custom-call(s32[2]{0:T(128)S(1)} %copy-done.2, bf16[512,8192]{1,0:T(8,128)(2,1)S(1)} %bitcast.135, bf16[512,8192]{1,0:T(8,128)(2,1)S(1)} %bitcast.135, ...), custom_call_target="tpu_custom_call" | custom-call | flops 1073741824 | bytes 11534336 | tf_op jit(solution)/shard_map/near0/pallas_call | solution.py:97
  32.2 0.1 collective-permute-start.5
  32.3 0.1 collective-permute-start.6
  32.4 5.1 %collective-permute-done.4 = f32[2,4,4,5,8,128]{5,4,3,2,1,0:T(8,128)S(1)} collective-permute-done((f32[2,4,4,5,8,128]{5,4,3,2,1,0:T(8,128)S(1)}, f32[2,4,4,5,8,128]{5,4,3,2,1,0:T(8,128)S(1)}, u32[]{:S(2)}, u32[]{:S(2)}) %collective-permute-start.4) | collective-permute-done | bytes 655392 | tf_op jit(solution)/shard_map/ppermute | solution.py:36
  37.5 5.4 %collective-permute-done.5 = f32[2,2,8,5,8,128]{5,4,3,2,1,0:T(8,128)S(1)} collective-permute-done((f32[2,2,8,5,8,128]{5,4,3,2,1,0:T(8,128)S(1)}, f32[2,2,8,5,8,128]{5,4,3,2,1,0:T(8,128)S(1)}, u32[]{:S(2)}, u32[]{:S(2)}) %collective-permute-start.5) | collective-permute-done | bytes 655392 | tf_op jit(solution)/shard_map/ppermute | solution.py:38
  42.9 1.7 %collective-permute-done.6 = f32[2,4,4,5,8,128]{5,4,3,2,1,0:T(8,128)S(1)} collective-permute-done((f32[2,4,4,5,8,128]{5,4,3,2,1,0:T(8,128)S(1)}, f32[2,4,4,5,8,128]{5,4,3,2,1,0:T(8,128)S(1)}, u32[]{:S(2)}, u32[]{:S(2)}) %collective-permute-start.6) | collective-permute-done | bytes 655392 | tf_op jit(solution)/shard_map/ppermute | solution.py:36
  44.6 0.3 fusion.34
  44.9 0.1 fusion
  45.0 1.2 collective-permute-start.7
  46.4 1.8 %collective-permute-start.8 = (f32[2,2,2,2,2,5,8,128]{7,6,5,4,3,2,1,0:T(8,128)S(1)}, f32[2,2,2,2,2,5,8,128]{7,6,5,4,3,2,1,0:T(8,128)S(1)}, u32[]{:S(2)}, u32[]{:S(2)}) collective-permute-start(f32[2,2,2,2,2,5,8,128]{7,6,5,4,3,2,1,0:T(8,128)S(1)} %pad_maximum_fusion), channel_id=1, source_target_pairs={{0,32},{1,225},{2,34},{3,227},{4,36},{5,229},{6,38},{7,231},{8,40}... | collective-permute-start | bytes 1966088 | tf_op jit(solution)/shard_map/ppermute | solution.py:36
  48.3 2.6 %collective-permute-start.9 = (f32[2,2,2,2,2,5,8,128]{7,6,5,4,3,2,0,1:T(8,128)S(1)}, f32[2,2,2,2,2,5,8,128]{7,6,5,4,3,2,0,1:T(8,128)S(1)}, u32[]{:S(2)}, u32[]{:S(2)}) collective-permute-start(f32[2,2,2,2,2,5,8,128]{7,6,5,4,3,2,0,1:T(8,128)S(1)} %copy.16), channel_id=1, source_target_pairs={{0,8},{1,25},{2,10},{3,27},{4,12},{5,29},{6,14},{7,31},{8,0},{9,17... | collective-permute-start | bytes 1966088 | tf_op jit(solution)/shard_map/ppermute | solution.py:38
  51.0 6.1 %collective-permute-done.8 = f32[2,2,2,2,2,5,8,128]{7,6,5,4,3,2,1,0:T(8,128)S(1)} collective-permute-done((f32[2,2,2,2,2,5,8,128]{7,6,5,4,3,2,1,0:T(8,128)S(1)}, f32[2,2,2,2,2,5,8,128]{7,6,5,4,3,2,1,0:T(8,128)S(1)}, u32[]{:S(2)}, u32[]{:S(2)}) %collective-permute-start.8) | collective-permute-done | bytes 655392 | tf_op jit(solution)/shard_map/ppermute | solution.py:36
  57.1 1.9 %collective-permute-done.9 = f32[2,2,2,2,2,5,8,128]{7,6,5,4,3,2,0,1:T(8,128)S(1)} collective-permute-done((f32[2,2,2,2,2,5,8,128]{7,6,5,4,3,2,0,1:T(8,128)S(1)}, f32[2,2,2,2,2,5,8,128]{7,6,5,4,3,2,0,1:T(8,128)S(1)}, u32[]{:S(2)}, u32[]{:S(2)}) %collective-permute-start.9) | collective-permute-done | bytes 655392 | tf_op jit(solution)/shard_map/ppermute | solution.py:38
  59.0 0.1 fusion.3
  59.1 1.1 collective-permute-start.10
  60.2 0.1 fusion.8
  60.3 1.6 %collective-permute-start.11 = (f32[2,2,2,2,5,8,128]{6,5,4,3,2,1,0:T(8,128)S(1)}, f32[2,2,2,2,5,8,128]{6,5,4,3,2,1,0:T(8,128)S(1)}, u32[]{:S(2)}, u32[]{:S(2)}) collective-permute-start(f32[2,2,2,2,5,8,128]{6,5,4,3,2,1,0:T(8,128)S(1)} %get-tuple-element.72), channel_id=1, source_target_pairs={{0,8},{1,25},{2,10},{3,27},{4,12},{5,29},{6,14},{7,31},{8,0},{9,17... | collective-permute-start | bytes 983048 | tf_op jit(solution)/shard_map/ppermute | solution.py:38
  62.0 1.0 collective-permute-start.12
  63.1 4.5 %collective-permute-done.11 = f32[2,2,2,2,5,8,128]{6,5,4,3,2,1,0:T(8,128)S(1)} collective-permute-done((f32[2,2,2,2,5,8,128]{6,5,4,3,2,1,0:T(8,128)S(1)}, f32[2,2,2,2,5,8,128]{6,5,4,3,2,1,0:T(8,128)S(1)}, u32[]{:S(2)}, u32[]{:S(2)}) %collective-permute-start.11) | collective-permute-done | bytes 327712 | tf_op jit(solution)/shard_map/ppermute | solution.py:38
  67.5 2.9 %collective-permute-done.12 = f32[2,2,2,2,5,8,128]{6,5,4,3,2,1,0:T(8,128)S(1)} collective-permute-done((f32[2,2,2,2,5,8,128]{6,5,4,3,2,1,0:T(8,128)S(1)}, f32[2,2,2,2,5,8,128]{6,5,4,3,2,1,0:T(8,128)S(1)}, u32[]{:S(2)}, u32[]{:S(2)}) %collective-permute-start.12) | collective-permute-done | bytes 327712 | tf_op jit(solution)/shard_map/ppermute | solution.py:38
  70.6 0.3 collective-permute-start.15
  70.9 0.1 collective-permute-start.14
  71.0 2.7 %collective-permute-start.13 = (f32[2,2,16,8,128]{4,3,2,1,0:T(8,128)S(1)}, f32[2,2,16,8,128]{4,3,2,1,0:T(8,128)S(1)}, u32[]{:S(2)}, u32[]{:S(2)}) collective-permute-start(f32[2,2,16,8,128]{4,3,2,1,0:T(8,128)S(1)} %pad_maximum_fusion.1), channel_id=1, source_target_pairs={{0,30},{1,11},{2,28},{3,9},{4,26},{5,15},{6,24},{7,13},{8,22},{9,3... | collective-permute-start | bytes 786440 | tf_op jit(solution)/shard_map/ppermute | solution.py:38
  73.7 2.7 %collective-permute-done.15 = f32[2,2,16,8,128]{4,3,2,1,0:T(8,128)S(1)} collective-permute-done((f32[2,2,16,8,128]{4,3,2,1,0:T(8,128)S(1)}, f32[2,2,16,8,128]{4,3,2,1,0:T(8,128)S(1)}, u32[]{:S(2)}, u32[]{:S(2)}) %collective-permute-start.15) | collective-permute-done | bytes 262176 | tf_op jit(solution)/shard_map/ppermute | solution.py:38
  76.4 0.1 collective-permute-done.14
  76.5 3.7 %collective-permute-done.13 = f32[2,2,16,8,128]{4,3,2,1,0:T(8,128)S(1)} collective-permute-done((f32[2,2,16,8,128]{4,3,2,1,0:T(8,128)S(1)}, f32[2,2,16,8,128]{4,3,2,1,0:T(8,128)S(1)}, u32[]{:S(2)}, u32[]{:S(2)}) %collective-permute-start.13) | collective-permute-done | bytes 262176 | tf_op jit(solution)/shard_map/ppermute | solution.py:38
  80.2 0.1 collective-permute-start.16
  80.4 0.7 copy.38
  81.1 5.9 %collective-permute-done.16 = f32[2,16,8,128]{3,2,1,0:T(8,128)S(1)} collective-permute-done((f32[2,16,8,128]{3,2,1,0:T(8,128)S(1)}, f32[2,16,8,128]{3,2,1,0:T(8,128)S(1)}, u32[]{:S(2)}, u32[]{:S(2)}) %collective-permute-start.16) | collective-permute-done | bytes 131104 | tf_op jit(solution)/shard_map/ppermute | solution.py:36
  87.1 0.1 collective-permute-start.17
  87.2 0.6 maximum_bitcast_fusion.row_old
  87.8 6.0 %collective-permute-done.17 = f32[16,8,128]{2,1,0:T(8,128)S(1)} collective-permute-done((f32[16,8,128]{2,1,0:T(8,128)S(1)}, f32[16,8,128]{2,1,0:T(8,128)S(1)}, u32[]{:S(2)}, u32[]{:S(2)}) %collective-permute-start.17) | collective-permute-done | bytes 65568 | tf_op jit(solution)/shard_map/ppermute | solution.py:36
  93.8 0.6 fusion.33.units
  94.5 1.8 %stats.1 = (f32[8,32,128]{2,1,0:T(8,128)}, f32[32,8,128]{2,1,0:T(8,128)}) custom-call(s32[2]{0:T(128)} %pad_add_fusion.pos, f32[16,8,128]{2,1,0:T(8,128)} %fusion.33.units, f32[32,2]{1,0:T(8,128)} %bitcast.148, f32[1,128]{1,0:T(1,128)} %maximum_bitcast_fusion.row_old), custom_call_target="tpu_custom_call" | custom-call | tf_op jit(solution)/shard_map/stats/pallas_call | solution.py:262
  96.3 12.7 %all_to_all.10.stats = f32[32,8,128]{2,1,0:T(8,128)} all-to-all(f32[32,8,128]{2,1,0:T(8,128)} %get-tuple-element.47), channel_id=1, replica_groups=mesh['row'=8,'col'=32] {'col'}, dimensions={0} | all-to-all | bytes 262144 | tf_op jit(solution)/shard_map/all_to_all | solution.py:273
  108.9 1.7 %pack.1 = f32[8,32,128]{2,1,0:T(8,128)} custom-call(f32[8,32,128]{2,1,0:T(8,128)} %get-tuple-element.46.tile, f32[32,8,128]{2,1,0:T(8,128)} %all_to_all.10.stats), custom_call_target="tpu_custom_call" | custom-call | tf_op jit(solution)/shard_map/pack/pallas_call | solution.py:274
  110.6 13.9 %all_to_all.11.load = f32[8,32,128]{2,1,0:T(8,128)} all-to-all(f32[8,32,128]{2,1,0:T(8,128)} %pack.1), channel_id=1, replica_groups=mesh['row'=8,'col'=32] {'row'}, dimensions={0} | all-to-all | bytes 262144 | tf_op jit(solution)/shard_map/all_to_all | solution.py:281
  124.5 1.9 %finish.1 = (f32[64,256]{1,0:T(8,128)}, f32[1,64]{1,0:T(1,128)}, f32[2,256]{1,0:T(2,128)}) custom-call(s32[2]{0:T(128)} %pad_add_fusion.pos, f32[8,32,128]{2,1,0:T(8,128)} %all_to_all.11.load), custom_call_target="tpu_custom_call" | custom-call | tf_op jit(solution)/shard_map/finish/pallas_call | solution.py:283
  (38 shorter events, 1.0 us)
Async XLA Ops:
  0.6 79.7 %copy-start = (f32[2,256]{1,0:T(2,128)S(1)}, f32[2,256]{1,0:T(2,128)}, u32[]{:S(2)}) copy-start(f32[2,256]{1,0:T(2,128)} %param.7) | copy-start | bytes 6148
  1.3 7.5 %copy-start.1 = (bf16[512,512]{1,0:T(8,128)(2,1)S(1)}, bf16[512,512]{1,0:T(8,128)(2,1)}, u32[]{:S(2)}) copy-start(bf16[512,512]{1,0:T(8,128)(2,1)} %refs_4_.7) | copy-start | bytes 1572868
  1.3 7.5 %copy-start.2 = (s32[2]{0:T(128)S(1)}, s32[2]{0:T(128)}, u32[]{:S(2)}) copy-start(s32[2]{0:T(128)} %pad_add_fusion.pos) | copy-start | bytes 28
  1.3 14.4 %slice-start = ((s8[8388608]{0:T(1024)(128)(4,1)}), s8[4194304]{0:T(1024)(128)(4,1)S(1)}, s32[]{:S(2)}) async-start(s8[8388608]{0:T(1024)(128)(4,1)} %bitcast.134), calls=%async_computation.2 | async-start | bytes 8388608
  5.4 10.3 %slice-start.1 = ((s8[8388608]{0:T(1024)(128)(4,1)}), s8[4194304]{0:T(1024)(128)(4,1)S(1)}, s32[]{:S(2)}) async-start(s8[8388608]{0:T(1024)(128)(4,1)} %bitcast.134), calls=%async_computation.3 | async-start | bytes 8388608
  5.4 10.2 %collective-permute-start.1 = (f32[2,4,8,16,8,128]{5,4,3,2,1,0:T(8,128)S(1)}, f32[2,4,8,16,8,128]{5,4,3,2,1,0:T(8,128)}, u32[]{:S(2)}, u32[]{:S(2)}) collective-permute-start(f32[2,4,8,16,8,128]{5,4,3,2,1,0:T(8,128)S(1)} %away1.1), channel_id=1, source_target_pairs={{0,1},{1,0},{2,3},{3,2},{4,5},{5,4},{6,7},{7,6},{8,9},{9,8},{10,11... | collective-permute-start | bytes 12582920 | tf_op jit(solution)/shard_map/ppermute | solution.py:25
  12.2 17.4 %collective-permute-start = (f32[2,4,8,16,8,128]{5,4,3,2,1,0:T(8,128)S(1)}, f32[2,4,8,16,8,128]{5,4,3,2,1,0:T(8,128)S(1)}, u32[]{:S(2)}, u32[]{:S(2)}) collective-permute-start(f32[2,4,8,16,8,128]{5,4,3,2,1,0:T(8,128)S(1)} %away0.1), channel_id=1, source_target_pairs={{0,1},{1,0},{2,3},{3,2},{4,5},{5,4},{6,7},{7,6},{8,9},{9,8},{10,11... | collective-permute-start | bytes 12582920 | tf_op jit(solution)/shard_map/ppermute | solution.py:25
  20.3 24.3 %collective-permute-start.2 = (f32[2,4,8,6,8,128]{5,4,3,2,1,0:T(8,128)S(1)}, f32[2,4,8,6,8,128]{5,4,3,2,1,0:T(8,128)S(1)}, u32[]{:S(2)}, u32[]{:S(2)}) collective-permute-start(f32[2,4,8,6,8,128]{5,4,3,2,1,0:T(8,128)S(1)} %get-tuple-element.28), channel_id=1, source_target_pairs={{0,8},{1,25},{2,10},{3,27},{4,12},{5,29},{6,14},{7,31},{8,0},{9,17... | collective-permute-start | bytes 4718600 | tf_op jit(solution)/shard_map/ppermute | solution.py:38
  21.1 11.3 %collective-permute-start.3 = (f32[2,2,8,5,8,128]{5,4,3,2,1,0:T(8,128)S(1)}, f32[2,2,8,5,8,128]{5,4,3,2,1,0:T(8,128)S(1)}, u32[]{:S(2)}, u32[]{:S(2)}) collective-permute-start(f32[2,2,8,5,8,128]{5,4,3,2,1,0:T(8,128)S(1)} %get-tuple-element.29), channel_id=1, source_target_pairs={{0,2},{1,7},{2,0},{3,5},{4,6},{5,3},{6,4},{7,1},{8,10},{9,15},{10,... | collective-permute-start | bytes 1966088 | tf_op jit(solution)/shard_map/ppermute | solution.py:38
  23.9 13.6 %collective-permute-start.4 = (f32[2,4,4,5,8,128]{5,4,3,2,1,0:T(8,128)S(1)}, f32[2,4,4,5,8,128]{5,4,3,2,1,0:T(8,128)S(1)}, u32[]{:S(2)}, u32[]{:S(2)}) collective-permute-start(f32[2,4,4,5,8,128]{5,4,3,2,1,0:T(8,128)S(1)} %slice.163), channel_id=1, source_target_pairs={{0,32},{1,225},{2,34},{3,227},{4,36},{5,229},{6,38},{7,231},{8,40}... | collective-permute-start | bytes 1966088 | tf_op jit(solution)/shard_map/ppermute | solution.py:36
  32.2 10.7 %collective-permute-start.5 = (f32[2,2,8,5,8,128]{5,4,3,2,1,0:T(8,128)S(1)}, f32[2,2,8,5,8,128]{5,4,3,2,1,0:T(8,128)S(1)}, u32[]{:S(2)}, u32[]{:S(2)}) collective-permute-start(f32[2,2,8,5,8,128]{5,4,3,2,1,0:T(8,128)S(1)} %get-tuple-element.31), channel_id=1, source_target_pairs={{0,2},{1,7},{2,0},{3,5},{4,6},{5,3},{6,4},{7,1},{8,10},{9,15},{10,... | collective-permute-start | bytes 1966088 | tf_op jit(solution)/shard_map/ppermute | solution.py:38
  32.3 12.2 %collective-permute-start.6 = (f32[2,4,4,5,8,128]{5,4,3,2,1,0:T(8,128)S(1)}, f32[2,4,4,5,8,128]{5,4,3,2,1,0:T(8,128)S(1)}, u32[]{:S(2)}, u32[]{:S(2)}) collective-permute-start(f32[2,4,4,5,8,128]{5,4,3,2,1,0:T(8,128)S(1)} %slice.164), channel_id=1, source_target_pairs={{0,32},{1,225},{2,34},{3,227},{4,36},{5,229},{6,38},{7,231},{8,40}... | collective-permute-start | bytes 1966088 | tf_op jit(solution)/shard_map/ppermute | solution.py:36
  45.0 14.0 %collective-permute-start.7 = (f32[2,2,2,2,2,6,8,128]{7,6,5,4,3,1,0,2:T(8,128)S(1)}, f32[2,2,2,2,2,6,8,128]{7,6,5,4,3,1,0,2:T(8,128)S(1)}, u32[]{:S(2)}, u32[]{:S(2)}) collective-permute-start(f32[2,2,2,2,2,6,8,128]{7,6,5,4,3,1,0,2:T(8,128)S(1)} %fusion), channel_id=1, source_target_pairs={{0,2},{1,7},{2,0},{3,5},{4,6},{5,3},{6,4},{7,1},{8,10},{9,15},{10,... | collective-permute-start | bytes 2359304 | tf_op jit(solution)/shard_map/ppermute | solution.py:38
  46.4 10.7 %collective-permute-start.8 = (f32[2,2,2,2,2,5,8,128]{7,6,5,4,3,2,1,0:T(8,128)S(1)}, f32[2,2,2,2,2,5,8,128]{7,6,5,4,3,2,1,0:T(8,128)S(1)}, u32[]{:S(2)}, u32[]{:S(2)}) collective-permute-start(f32[2,2,2,2,2,5,8,128]{7,6,5,4,3,2,1,0:T(8,128)S(1)} %pad_maximum_fusion), channel_id=1, source_target_pairs={{0,32},{1,225},{2,34},{3,227},{4,36},{5,229},{6,38},{7,231},{8,40}... | collective-permute-start | bytes 1966088 | tf_op jit(solution)/shard_map/ppermute | solution.py:36
  48.3 10.7 %collective-permute-start.9 = (f32[2,2,2,2,2,5,8,128]{7,6,5,4,3,2,0,1:T(8,128)S(1)}, f32[2,2,2,2,2,5,8,128]{7,6,5,4,3,2,0,1:T(8,128)S(1)}, u32[]{:S(2)}, u32[]{:S(2)}) collective-permute-start(f32[2,2,2,2,2,5,8,128]{7,6,5,4,3,2,0,1:T(8,128)S(1)} %copy.16), channel_id=1, source_target_pairs={{0,8},{1,25},{2,10},{3,27},{4,12},{5,29},{6,14},{7,31},{8,0},{9,17... | collective-permute-start | bytes 1966088 | tf_op jit(solution)/shard_map/ppermute | solution.py:38
  59.1 11.3 %collective-permute-start.10 = (f32[2,2,2,2,6,8,128]{6,5,4,3,2,1,0:T(8,128)S(1)}, f32[2,2,2,2,6,8,128]{6,5,4,3,2,1,0:T(8,128)S(1)}, u32[]{:S(2)}, u32[]{:S(2)}) collective-permute-start(f32[2,2,2,2,6,8,128]{6,5,4,3,2,1,0:T(8,128)S(1)} %get-tuple-element.52), channel_id=1, source_target_pairs={{0,32},{1,225},{2,34},{3,227},{4,36},{5,229},{6,38},{7,231},{8,40}... | collective-permute-start | bytes 1179656 | tf_op jit(solution)/shard_map/ppermute | solution.py:36
  60.3 7.2 %collective-permute-start.11 = (f32[2,2,2,2,5,8,128]{6,5,4,3,2,1,0:T(8,128)S(1)}, f32[2,2,2,2,5,8,128]{6,5,4,3,2,1,0:T(8,128)S(1)}, u32[]{:S(2)}, u32[]{:S(2)}) collective-permute-start(f32[2,2,2,2,5,8,128]{6,5,4,3,2,1,0:T(8,128)S(1)} %get-tuple-element.72), channel_id=1, source_target_pairs={{0,8},{1,25},{2,10},{3,27},{4,12},{5,29},{6,14},{7,31},{8,0},{9,17... | collective-permute-start | bytes 983048 | tf_op jit(solution)/shard_map/ppermute | solution.py:38
  62.0 8.4 %collective-permute-start.12 = (f32[2,2,2,2,5,8,128]{6,5,4,3,2,1,0:T(8,128)S(1)}, f32[2,2,2,2,5,8,128]{6,5,4,3,2,1,0:T(8,128)S(1)}, u32[]{:S(2)}, u32[]{:S(2)}) collective-permute-start(f32[2,2,2,2,5,8,128]{6,5,4,3,2,1,0:T(8,128)S(1)} %get-tuple-element.57), channel_id=1, source_target_pairs={{0,2},{1,7},{2,0},{3,5},{4,6},{5,3},{6,4},{7,1},{8,10},{9,15},{10,... | collective-permute-start | bytes 983048 | tf_op jit(solution)/shard_map/ppermute | solution.py:38
  70.6 5.8 %collective-permute-start.15 = (f32[2,2,16,8,128]{4,3,2,1,0:T(8,128)S(1)}, f32[2,2,16,8,128]{4,3,2,1,0:T(8,128)S(1)}, u32[]{:S(2)}, u32[]{:S(2)}) collective-permute-start(f32[2,2,16,8,128]{4,3,2,1,0:T(8,128)S(1)} %pad_maximum_fusion.3), channel_id=1, source_target_pairs={{0,6},{1,3},{2,4},{3,1},{4,2},{5,7},{6,0},{7,5},{8,14},{9,11},{10,... | collective-permute-start | bytes 786440 | tf_op jit(solution)/shard_map/ppermute | solution.py:38
  70.9 16.3 %copy-start.3 = (f32[64]{0:T(128)S(1)}, f32[64]{0:T(128)}, u32[]{:S(2)}) copy-start(f32[64]{0:T(128)} %param.6) | copy-start | bytes 772
  70.9 5.6 %collective-permute-start.14 = (f32[2,2,16,8,128]{4,3,2,1,0:T(8,128)S(1)}, f32[2,2,16,8,128]{4,3,2,1,0:T(8,128)S(1)}, u32[]{:S(2)}, u32[]{:S(2)}) collective-permute-start(f32[2,2,16,8,128]{4,3,2,1,0:T(8,128)S(1)} %pad_maximum_fusion.2), channel_id=1, source_target_pairs={{0,24},{1,9},{2,26},{3,11},{4,28},{5,13},{6,30},{7,15},{8,16},{9,1... | collective-permute-start | bytes 786440 | tf_op jit(solution)/shard_map/ppermute | solution.py:38
  71.0 9.1 %collective-permute-start.13 = (f32[2,2,16,8,128]{4,3,2,1,0:T(8,128)S(1)}, f32[2,2,16,8,128]{4,3,2,1,0:T(8,128)S(1)}, u32[]{:S(2)}, u32[]{:S(2)}) collective-permute-start(f32[2,2,16,8,128]{4,3,2,1,0:T(8,128)S(1)} %pad_maximum_fusion.1), channel_id=1, source_target_pairs={{0,30},{1,11},{2,28},{3,9},{4,26},{5,15},{6,24},{7,13},{8,22},{9,3... | collective-permute-start | bytes 786440 | tf_op jit(solution)/shard_map/ppermute | solution.py:38
  80.2 6.8 %collective-permute-start.16 = (f32[2,16,8,128]{3,2,1,0:T(8,128)S(1)}, f32[2,16,8,128]{3,2,1,0:T(8,128)S(1)}, u32[]{:S(2)}, u32[]{:S(2)}) collective-permute-start(f32[2,16,8,128]{3,2,1,0:T(8,128)S(1)} %slice_bitcast_fusion.10), channel_id=1, source_target_pairs={{0,64},{1,65},{2,66},{3,67},{4,68},{5,69},{6,70},{7,71},{8,72},{9,... | collective-permute-start | bytes 393224 | tf_op jit(solution)/shard_map/ppermute | solution.py:36
  87.1 6.7 %collective-permute-start.17 = (f32[16,8,128]{2,1,0:T(8,128)S(1)}, f32[16,8,128]{2,1,0:T(8,128)S(1)}, u32[]{:S(2)}, u32[]{:S(2)}) collective-permute-start(f32[16,8,128]{2,1,0:T(8,128)S(1)} %slice_bitcast_fusion.12), channel_id=1, source_target_pairs={{0,192},{1,193},{2,194},{3,195},{4,196},{5,197},{6,198},{7,199},{8... | collective-permute-start | bytes 196616 | tf_op jit(solution)/shard_map/ppermute | solution.py:36

commit v4 on v3

--- a/solution.py
+++ b/solution.py
@@ -13,6 +13,7 @@
 EPSILON = 1e-30
 CLIP_LIMIT = 1.0
 MIB = 1024 * 1024
+SMALL = pltpu.CompilerParams(vmem_limit_bytes=4 * MIB)
 GRANTS = (52, 44, 20, 20)
 
 RING4 = ((1, 3), (3, 1))
@@ -39,7 +40,7 @@
 
 
 def partial_kernel(chunk, to_sibling, pos, *refs):
-    step = pl.program_id(0)
+    bit = 1 - pl.program_id(0)
     z, core = pos[0], lax.rem(pos[1], 2)
     core = 1 - core if to_sibling else core
     xs, y = refs[:4], refs[4]
@@ -62,15 +63,15 @@
                 top = place * 32 + group * 8
                 piece = value[top : top + 8, lane * 128 : lane * 128 + 128]
                 if to_sibling:
-                    full[step, s, slot, unit] = piece
+                    full[bit, s, slot, unit] = piece
                     continue
-                piece = piece + got[step, s, slot, unit]
+                piece = piece + got[bit, s, slot, unit]
                 if unit < UNITS[0][1]:
-                    a[step, s, slot, unit] = piece
+                    a[bit, s, slot, unit] = piece
                 elif unit < UNITS[1][1]:
-                    (b_send if s >= 2 else b_keep)[step, s % 2, slot, unit - UNITS[1][0]] = piece
+                    (b_send if s >= 2 else b_keep)[bit, s % 2, slot, unit - UNITS[1][0]] = piece
                 else:
-                    c[step, s, slot, unit - UNITS[2][0]] = piece
+                    c[bit, s, slot, unit - UNITS[2][0]] = piece
 
 
 def partial(pos, x, y, chunk, grant, got=None):
@@ -82,7 +83,7 @@
             core = lax.rem(pos[1], 2)
             core = 1 - core if to_sibling else core
             first, second = 1 + 2 * core, 3 - 2 * core
-            xi = lax.div(pos[1], 8) ^ (first * chunk) ^ (second * step)
+            xi = lax.div(pos[1], 8) ^ (first * (1 - step)) ^ (second * chunk)
             yi = lax.rem(lax.div(pos[1], 2), 4) ^ (first * (s // 2)) ^ (second * (s % 2))
             return (0, (xi * 4 + yi) * 2 + core)
 
@@ -222,37 +223,32 @@
     row_old = jnp.concatenate([row_state, row_state]).reshape(1, 128)
 
     x, y = activations, kv_grads
-    sent1 = swap_cores(partial(pos, x, y, 1, GRANTS[0])[0])
-    sent0 = swap_cores(partial(pos, x, y, 0, GRANTS[1])[0])
-    a_send, b_send1, b_keep1, c1 = partial(pos, x, y, 1, GRANTS[2], sent1)
-    a_keep, b_send0, b_keep0, c0 = partial(pos, x, y, 0, GRANTS[3], sent0)
-    c_send1, c_keep1, c_send0, c_keep0 = c1[:, :, 4:], c1[:, :, :4], c0[:, :, 4:], c0[:, :, :4]
-
     na, nb, nc = (to - start for start, to in UNITS)
-    got = along("x", 0, a_send), along("y", 0, b_send1), along("z", 0, c_send1)
-    got = got + (along("y", 0, b_send0), along("z", 0, c_send0))
-    ga, gb1, gc1, gb0, gc0 = lax.optimization_barrier(got)
-    a, ga = (v.reshape(2, 2, 2, 2, 2, 2, na, 8, 128) for v in (a_keep, ga))
-    b1, b0, gb1, gb0 = (v.reshape(2, 2, 2, 2, 2, nb, 8, 128) for v in (b_keep1, b_keep0, gb1, gb0))
-    c1, c0, gc1, gc0 = (v.reshape(2, 2, 2, 2, 2, nc, 8, 128) for v in (c_keep1, c_keep0, gc1, gc0))
-
-    a_send = a[:, 1] + ga[:, 1]
-    b_send = jnp.stack([b1[:, :, 1] + gb1[:, :, 1], b0[:, :, 1] + gb0[:, :, 1]])
-    got = along("y", 0, a_send), along("z", 0, b_send), along("x", 0, c1 + gc1)
-    a = a[:, 0] + ga[:, 0]
-    b1, b0 = b1[:, :, 0] + gb1[:, :, 0], b0[:, :, 0] + gb0[:, :, 0]
-    c = c0 + gc0
-    ga, gb, gc = lax.optimization_barrier(got)
-
-    a_send = a[:, :, 1] + ga[:, :, 1]
-    got = along("z", 0, a_send), along("x", 0, b1 + gb[0]), along("y", 0, c[:, 1] + gc[:, 1])
-    a = a[:, :, 0] + ga[:, :, 0]
-    b = b0 + gb[1]
-    c = c[:, 0] + gc[:, 0]
-    ga, gb, gc = lax.optimization_barrier(got)
+    sent = [swap_cores(partial(pos, x, y, 1 - i, GRANTS[i])[0]) for i in (0, 1)]
+    streams = [None, None]
+    for i in (0, 1):
+        a, b_send, b_keep, c = partial(pos, x, y, 1 - i, GRANTS[2 + i], sent[i])
+        a = a.reshape(2, 2, 2, 2, 2, 2, na, 8, 128)
+        b_send, b_keep = (v.reshape(2, 2, 2, 2, 2, nb, 8, 128) for v in (b_send, b_keep))
+        c = c.reshape(2, 2, 2, 2, 2, 2, nc, 8, 128)
+
+        got = along("x", 0, a[1]), along("y", 0, b_send), along("z", 0, c[:, :, :, 1])
+        a, b, c = a[0], b_keep, c[:, :, :, 0]
+        ga, gb, gc = lax.optimization_barrier(got)
+
+        a_send, b_send, c_send = a[1] + ga[1], b[:, :, 1] + gb[:, :, 1], c[1] + gc[1]
+        got = along("y", 0, a_send), along("z", 0, b_send), along("x", 0, c_send)
+        a, b, c = a[0] + ga[0], b[:, :, 0] + gb[:, :, 0], c[0] + gc[0]
+        ga, gb, gc = lax.optimization_barrier(got)
+
+        a_send, b_send, c_send = a[:, 1] + ga[:, 1], b[1] + gb[1], c[1] + gc[1]
+        got = along("z", 0, a_send), along("x", 0, b_send), along("y", 0, c_send)
+        a, b, c = a[:, 0] + ga[:, 0], b[0] + gb[0], c[0] + gc[0]
+        ga, gb, gc = lax.optimization_barrier(got)
+        streams[1 - i] = ((a, ga), (b, gb), (c, gc))
 
     def quarter(i, j):
-        return jnp.concatenate([v[i, j] + g[i, j] for v, g in ((a, ga), (b, gb), (c, gc))], axis=2)
+        return jnp.concatenate([v[j] + g[j] for v, g in streams[i]], axis=2)
 
     got = along("xy", 1, quarter(1, 1)), along("x", 1, quarter(1, 0)), along("y", 1, quarter(0, 1))
     value = quarter(0, 0) + got[0] + got[1] + got[2]
@@ -264,9 +260,10 @@
         in_specs=[pl.BlockSpec(memory_space=pltpu.SMEM)] + [pl.BlockSpec(memory_space=pltpu.VMEM)] * 3,
         out_specs=[pl.BlockSpec(memory_space=pltpu.VMEM)] * 2,
         out_shape=[
-            jax.ShapeDtypeStruct((8, 32, 128), jnp.float32),
-            jax.ShapeDtypeStruct((32, 8, 128), jnp.float32),
+            pltpu.VMEM((8, 32, 128), jnp.float32),
+            pltpu.VMEM((32, 8, 128), jnp.float32),
         ],
+        compiler_params=SMALL,
         name="stats",
     )(pos, value, col_old, row_old)
 
@@ -275,7 +272,8 @@
         pack_kernel,
         in_specs=[pl.BlockSpec(memory_space=pltpu.VMEM)] * 2,
         out_specs=pl.BlockSpec(memory_space=pltpu.VMEM),
-        out_shape=jax.ShapeDtypeStruct((8, 32, 128), jnp.float32),
+        out_shape=pltpu.VMEM((8, 32, 128), jnp.float32),
+        compiler_params=SMALL,
         name="pack",
     )(tile, stats)
     load = lax.all_to_all(load, "row", 0, 0, tiled=True)
@@ -290,6 +288,7 @@
             jax.ShapeDtypeStruct((2, 256), jnp.float32),
         ],
         scratch_shapes=[pltpu.VMEM((8, 128), jnp.float32)] * 2,
+        compiler_params=SMALL,
         name="finish",
     )(pos, load)
     return (direction, row_new.reshape(64), col_new)

time: 127 us -> 118 us (0.929)
  waiting for transfers between devices: 49 us -> 33.2 us
  starting transfers between devices: 25.8 us -> 35.2 us
  Pallas kernels: 20.1 us -> 17.1 us
  blocking collectives: 26.6 us -> 28.5 us
    ppermute x6 -> x8, waiting for transfers between devices: 24.8 us -> 14.9 us  [along(): return lax.ppermute(value, ('row', 'col'), pairs)]
    ppermute x10 -> x15, waiting for transfers between devices: 21.1 us -> 15.3 us  [along(): lax.ppermute(value, 'col', [(i, i ^ RING4[i % 2][step] * unit) for i in r...]
    ppermute x10 -> x15, starting transfers between devices: 13.2 us -> 18.9 us  [along(): lax.ppermute(value, 'col', [(i, i ^ RING4[i % 2][step] * unit) for i in r...]
    ppermute x6 -> x8, starting transfers between devices: 8.81 us -> 12.5 us  [along(): return lax.ppermute(value, ('row', 'col'), pairs)]
    pallas_call x1, Pallas kernels: 1.7 us -> 0.09 us  [on_device(): pl.pallas_call(pack_kernel, in_specs=[pl.BlockSpec(memory_space=pltpu.VME...]
    all_to_all x1, blocking collectives: 13.9 us -> 15.4 us  [on_device(): load = lax.all_to_all(load, 'row', 0, 0, tiled=True)]
  transfers between devices with their start and end apart: 18 -> 25, of which waited for: 13 -> 11; matrix products, arithmetic and copies ran while one was open for 2% -> 1% of each run, Pallas kernels for 8% -> 9%
where the time goes in v4:
time: 118 us; the launch traced here: 117 us
  starting transfers between devices  35.2 us (30%)
  waiting for transfers between devices  33.2 us (28%)
  blocking collectives  28.5 us (24%)
  Pallas kernels  17.1 us (14%)
  other arithmetic  1.75 us (1%)
    ppermute x15, starting transfers between devices, along(): lax.ppermute(value, 'col', [(i, i ^ RING4[i % 2][step] * unit) for i in r...  18.9 us
    all_to_all x1, blocking collectives, on_device(): load = lax.all_to_all(load, 'row', 0, 0, tiled=True)  15.4 us
    ppermute x15, waiting for transfers between devices, along(): lax.ppermute(value, 'col', [(i, i ^ RING4[i % 2][step] * unit) for i in r...  15.3 us
    ppermute x8, waiting for transfers between devices, along(): return lax.ppermute(value, ('row', 'col'), pairs)  14.9 us
    pallas_call x4, Pallas kernels, partial(): pl.pallas_call(functools.partial(partial_kernel, chunk, to_sibling), grid...  14.7 us
    all_to_all x1, blocking collectives, on_device(): stats = lax.all_to_all(stats, 'col', 0, 0, tiled=True)  13.1 us
    ppermute x8, starting transfers between devices, along(): return lax.ppermute(value, ('row', 'col'), pairs)  12.5 us
    ppermute x2, starting transfers between devices, swap_cores(): return lax.ppermute(value, 'col', [(i, i ^ 1) for i in range(32)])  3.82 us
  transfers between devices with their start and end apart: 25, of which 11 were waited for; matrix products, arithmetic and copies ran while one was open for 1% of the time, Pallas kernels for 9%

profile of v4, /device:TPU:1, one launch (start us, length us, event | category | flops | bytes accessed | tf_op | source)
XLA Modules:
  0.0 117.3 jit_solution(16351964482152928124)
XLA Ops:
  0.6 0.6 pad_add_fusion.pos
  1.2 4.2 %away1.1 = f32[2,4,8,16,8,128]{5,4,3,2,1,0:T(8,128)S(1)} custom-call(s32[2]{0:T(128)} %pad_add_fusion.pos, bf16[512,8192]{1,0:T(8,128)(2,1)} %refs_3_.7, bf16[512,8192]{1,0:T(8,128)(2,1)} %refs_3_.7, bf16[512,8192]{1,0:T(8,128)(2,1)} %refs_3_.7, bf16[512,8192]{1,0:T(8,128)(2,1)} %refs_3_.7, bf16[512,512]{1,0:T(8,128)(2,1)} %refs_4_.7), custom_call_target="tpu_custom_call" | custom-call | flops 1073741824 | bytes 7340032 | tf_op jit(solution)/shard_map/away1/pallas_call | solution.py:98
  5.4 3.3 %collective-permute-start.10 = (f32[2,4,8,16,8,128]{5,4,3,2,1,0:T(8,128)S(1)}, f32[2,4,8,16,8,128]{5,4,3,2,1,0:T(8,128)}, u32[]{:S(2)}, u32[]{:S(2)}) collective-permute-start(f32[2,4,8,16,8,128]{5,4,3,2,1,0:T(8,128)S(1)} %away1.1), channel_id=1, source_target_pairs={{0,1},{1,0},{2,3},{3,2},{4,5},{5,4},{6,7},{7,6},{8,9},{9,8},{10,11... | collective-permute-start | bytes 12582920 | tf_op jit(solution)/shard_map/ppermute | solution.py:26
  8.8 3.4 %away0.1 = f32[2,4,8,16,8,128]{5,4,3,2,1,0:T(8,128)S(1)} custom-call(s32[2]{0:T(128)S(1)} %copy-done.2, bf16[512,8192]{1,0:T(8,128)(2,1)} %refs_3_.7, bf16[512,8192]{1,0:T(8,128)(2,1)} %refs_3_.7, bf16[512,8192]{1,0:T(8,128)(2,1)} %refs_3_.7, bf16[512,8192]{1,0:T(8,128)(2,1)} %refs_3_.7, bf16[512,512]{1,0:T(8,128)(2,1)S(1)} %copy-done.1), custom_call_target="tpu_custom_call" | custom-call | flops 1073741824 | bytes 7340032 | tf_op jit(solution)/shard_map/away0/pallas_call | solution.py:98
  12.1 0.5 collective-permute-start
  12.6 3.0 %collective-permute-done.10.refs_5_ = f32[2,4,8,16,8,128]{5,4,3,2,1,0:T(8,128)} collective-permute-done((f32[2,4,8,16,8,128]{5,4,3,2,1,0:T(8,128)S(1)}, f32[2,4,8,16,8,128]{5,4,3,2,1,0:T(8,128)}, u32[]{:S(2)}, u32[]{:S(2)}) %collective-permute-start.10) | collective-permute-done | bytes 4194336 | tf_op jit(solution)/shard_map/ppermute | solution.py:26
  15.7 4.6 %near1.1 = (f32[2,4,8,6,8,128]{5,4,3,2,1,0:T(8,128)S(1)}, f32[2,2,8,5,8,128]{5,4,3,2,1,0:T(8,128)S(1)}, f32[2,2,8,5,8,128]{5,4,3,2,1,0:T(8,128)S(1)}, f32[2,4,8,5,8,128]{5,4,3,2,1,0:T(8,128)S(1)}) custom-call(s32[2]{0:T(128)S(1)} %copy-done.2, bf16[512,8192]{1,0:T(8,128)(2,1)S(1)} %bitcast.231, bf16[512,8192]{1,0:T(8,128)(2,1)S(1)} %bitcast.231, ...), custom_call_target="tpu_custom_call" | custom-call | flops 1073741824 | bytes 11534336 | tf_op jit(solution)/shard_map/near1/pallas_call | solution.py:98
  20.3 0.8 collective-permute-start.11
  21.2 5.7 %collective-permute-start.13 = (f32[2,2,2,2,2,5,8,128]{7,6,5,4,3,2,1,0:T(8,128)S(1)}, f32[2,2,2,2,2,5,8,128]{7,6,5,4,3,2,1,0:T(8,128)S(1)}, u32[]{:S(2)}, u32[]{:S(2)}) collective-permute-start(f32[2,2,2,2,2,5,8,128]{7,6,5,4,3,2,1,0:T(8,128)S(1)} %slice_bitcast_fusion), channel_id=1, source_target_pairs={{0,32},{1,225},{2,34},{3,227},{4,36},{5,229},{6,38},{7,231},{8,40}... | collective-permute-start | bytes 1966088 | tf_op jit(solution)/shard_map/ppermute | solution.py:37
  26.9 2.8 %collective-permute-start.12 = (f32[2,2,2,2,2,5,8,128]{7,6,5,4,3,1,2,0:T(8,128)S(1)}, f32[2,2,2,2,2,5,8,128]{7,6,5,4,3,1,2,0:T(8,128)S(1)}, u32[]{:S(2)}, u32[]{:S(2)}) collective-permute-start(f32[2,2,2,2,2,5,8,128]{7,6,5,4,3,1,2,0:T(8,128)S(1)} %copy.14), channel_id=1, source_target_pairs={{0,2},{1,7},{2,0},{3,5},{4,6},{5,3},{6,4},{7,1},{8,10},{9,15},{10,... | collective-permute-start | bytes 1966088 | tf_op jit(solution)/shard_map/ppermute | solution.py:39
  29.8 2.6 %near0.1 = (f32[2,4,8,6,8,128]{5,4,3,2,1,0:T(8,128)S(1)}, f32[2,2,8,5,8,128]{5,4,3,2,1,0:T(8,128)S(1)}, f32[2,2,8,5,8,128]{5,4,3,2,1,0:T(8,128)S(1)}, f32[2,4,8,5,8,128]{5,4,3,2,1,0:T(8,128)S(1)}) custom-call(s32[2]{0:T(128)S(1)} %copy-done.2, bf16[512,8192]{1,0:T(8,128)(2,1)S(1)} %bitcast.231, bf16[512,8192]{1,0:T(8,128)(2,1)S(1)} %bitcast.231, ...), custom_call_target="tpu_custom_call" | custom-call | flops 1073741824 | bytes 11534336 | tf_op jit(solution)/shard_map/near0/pallas_call | solution.py:98
  32.4 0.3 collective-permute-start.1
  32.9 0.1 collective-permute-start.3
  33.0 1.8 %collective-permute-done.13 = f32[2,2,2,2,2,5,8,128]{7,6,5,4,3,2,1,0:T(8,128)S(1)} collective-permute-done((f32[2,2,2,2,2,5,8,128]{7,6,5,4,3,2,1,0:T(8,128)S(1)}, f32[2,2,2,2,2,5,8,128]{7,6,5,4,3,2,1,0:T(8,128)S(1)}, u32[]{:S(2)}, u32[]{:S(2)}) %collective-permute-start.13) | collective-permute-done | bytes 655392 | tf_op jit(solution)/shard_map/ppermute | solution.py:37
  34.9 2.7 %collective-permute-start.2 = (f32[2,2,2,2,2,5,8,128]{7,6,5,4,3,1,2,0:T(8,128)S(1)}, f32[2,2,2,2,2,5,8,128]{7,6,5,4,3,1,2,0:T(8,128)S(1)}, u32[]{:S(2)}, u32[]{:S(2)}) collective-permute-start(f32[2,2,2,2,2,5,8,128]{7,6,5,4,3,1,2,0:T(8,128)S(1)} %copy.8), channel_id=1, source_target_pairs={{0,2},{1,7},{2,0},{3,5},{4,6},{5,3},{6,4},{7,1},{8,10},{9,15},{10,... | collective-permute-start | bytes 1966088 | tf_op jit(solution)/shard_map/ppermute | solution.py:39
  37.6 0.1 collective-permute-done.12
  37.7 0.1 bitcast_add_fusion.1
  37.8 2.8 %collective-permute-start.14 = (f32[2,2,2,2,6,8,128]{6,5,4,3,2,1,0:T(8,128)S(1)}, f32[2,2,2,2,6,8,128]{6,5,4,3,2,1,0:T(8,128)S(1)}, u32[]{:S(2)}, u32[]{:S(2)}) collective-permute-start(f32[2,2,2,2,6,8,128]{6,5,4,3,2,1,0:T(8,128)S(1)} %get-tuple-element.80), channel_id=1, source_target_pairs={{0,2},{1,7},{2,0},{3,5},{4,6},{5,3},{6,4},{7,1},{8,10},{9,15},{10,... | collective-permute-start | bytes 1179656 | tf_op jit(solution)/shard_map/ppermute | solution.py:39
  40.7 0.3 collective-permute-start.16
  41.0 2.6 %collective-permute-done.3 = f32[2,2,2,2,2,5,8,128]{7,6,5,4,3,2,1,0:T(8,128)S(1)} collective-permute-done((f32[2,2,2,2,2,5,8,128]{7,6,5,4,3,2,1,0:T(8,128)S(1)}, f32[2,2,2,2,2,5,8,128]{7,6,5,4,3,2,1,0:T(8,128)S(1)}, u32[]{:S(2)}, u32[]{:S(2)}) %collective-permute-start.3) | collective-permute-done | bytes 655392 | tf_op jit(solution)/shard_map/ppermute | solution.py:37
  43.6 0.9 collective-permute-start.15
  44.6 1.0 collective-permute-done.2
  45.6 0.1 bitcast_add_fusion.3
  45.7 2.8 %collective-permute-start.4 = (f32[2,2,2,2,6,8,128]{6,5,4,3,2,1,0:T(8,128)S(1)}, f32[2,2,2,2,6,8,128]{6,5,4,3,2,1,0:T(8,128)S(1)}, u32[]{:S(2)}, u32[]{:S(2)}) collective-permute-start(f32[2,2,2,2,6,8,128]{6,5,4,3,2,1,0:T(8,128)S(1)} %get-tuple-element.84), channel_id=1, source_target_pairs={{0,2},{1,7},{2,0},{3,5},{4,6},{5,3},{6,4},{7,1},{8,10},{9,15},{10,... | collective-permute-start | bytes 1179656 | tf_op jit(solution)/shard_map/ppermute | solution.py:39
  48.4 0.1 fusion.7
  48.5 0.3 collective-permute-start.6
  48.8 0.1 fusion.6
  48.9 2.8 %collective-permute-start.5 = (f32[2,2,2,2,5,8,128]{6,5,4,3,2,1,0:T(8,128)S(1)}, f32[2,2,2,2,5,8,128]{6,5,4,3,2,1,0:T(8,128)S(1)}, u32[]{:S(2)}, u32[]{:S(2)}) collective-permute-start(f32[2,2,2,2,5,8,128]{6,5,4,3,2,1,0:T(8,128)S(1)} %get-tuple-element.76), channel_id=1, source_target_pairs={{0,32},{1,225},{2,34},{3,227},{4,36},{5,229},{6,38},{7,231},{8,40}... | collective-permute-start | bytes 983048 | tf_op jit(solution)/shard_map/ppermute | solution.py:37
  51.7 2.7 %collective-permute-start.18 = (f32[2,2,2,5,8,128]{5,4,3,2,1,0:T(8,128)S(1)}, f32[2,2,2,5,8,128]{5,4,3,2,1,0:T(8,128)S(1)}, u32[]{:S(2)}, u32[]{:S(2)}) collective-permute-start(f32[2,2,2,5,8,128]{5,4,3,2,1,0:T(8,128)S(1)} %get-tuple-element.86), channel_id=1, source_target_pairs={{0,8},{1,25},{2,10},{3,27},{4,12},{5,29},{6,14},{7,31},{8,0},{9,17... | collective-permute-start | bytes 491528 | tf_op jit(solution)/shard_map/ppermute | solution.py:39
  54.5 0.1 collective-permute-start.17
  54.7 1.1 collective-permute-done.6
  55.8 0.2 collective-permute-start.19
  55.9 0.2 collective-permute-done.5
  56.2 2.6 %collective-permute-start.8 = (f32[2,2,2,5,8,128]{5,4,3,2,1,0:T(8,128)S(1)}, f32[2,2,2,5,8,128]{5,4,3,2,1,0:T(8,128)S(1)}, u32[]{:S(2)}, u32[]{:S(2)}) collective-permute-start(f32[2,2,2,5,8,128]{5,4,3,2,1,0:T(8,128)S(1)} %get-tuple-element.90), channel_id=1, source_target_pairs={{0,8},{1,25},{2,10},{3,27},{4,12},{5,29},{6,14},{7,31},{8,0},{9,17... | collective-permute-start | bytes 491528 | tf_op jit(solution)/shard_map/ppermute | solution.py:39
  58.8 2.8 %collective-permute-start.7 = (f32[2,2,2,6,8,128]{5,4,3,2,1,0:T(8,128)S(1)}, f32[2,2,2,6,8,128]{5,4,3,2,1,0:T(8,128)S(1)}, u32[]{:S(2)}, u32[]{:S(2)}) collective-permute-start(f32[2,2,2,6,8,128]{5,4,3,2,1,0:T(8,128)S(1)} %get-tuple-element.82), channel_id=1, source_target_pairs={{0,32},{1,225},{2,34},{3,227},{4,36},{5,229},{6,38},{7,231},{8,40}... | collective-permute-start | bytes 589832 | tf_op jit(solution)/shard_map/ppermute | solution.py:37
  61.6 0.1 collective-permute-start.9
  62.0 0.4 collective-permute-start.21
  62.4 7.8 %collective-permute-done.9 = f32[2,2,2,5,8,128]{5,4,3,2,1,0:T(8,128)S(1)} collective-permute-done((f32[2,2,2,5,8,128]{5,4,3,2,1,0:T(8,128)S(1)}, f32[2,2,2,5,8,128]{5,4,3,2,1,0:T(8,128)S(1)}, u32[]{:S(2)}, u32[]{:S(2)}) %collective-permute-start.9) | collective-permute-done | bytes 163872 | tf_op jit(solution)/shard_map/ppermute | solution.py:39
  70.3 0.1 collective-permute-start.22
  70.4 5.2 %collective-permute-done.22 = f32[2,2,16,8,128]{4,3,2,1,0:T(8,128)S(1)} collective-permute-done((f32[2,2,16,8,128]{4,3,2,1,0:T(8,128)S(1)}, f32[2,2,16,8,128]{4,3,2,1,0:T(8,128)S(1)}, u32[]{:S(2)}, u32[]{:S(2)}) %collective-permute-start.22) | collective-permute-done | bytes 262176 | tf_op jit(solution)/shard_map/ppermute | solution.py:39
  75.7 0.1 collective-permute-start.23
  76.0 4.5 %collective-permute-done.23 = f32[2,16,8,128]{3,2,1,0:T(8,128)S(1)} collective-permute-done((f32[2,16,8,128]{3,2,1,0:T(8,128)S(1)}, f32[2,16,8,128]{3,2,1,0:T(8,128)S(1)}, u32[]{:S(2)}, u32[]{:S(2)}) %collective-permute-start.23) | collective-permute-done | bytes 131104 | tf_op jit(solution)/shard_map/ppermute | solution.py:37
  80.5 0.1 collective-permute-start.24
  80.7 5.8 %collective-permute-done.24 = f32[16,8,128]{2,1,0:T(8,128)S(1)} collective-permute-done((f32[16,8,128]{2,1,0:T(8,128)S(1)}, f32[16,8,128]{2,1,0:T(8,128)S(1)}, u32[]{:S(2)}, u32[]{:S(2)}) %collective-permute-start.24) | collective-permute-done | bytes 65568 | tf_op jit(solution)/shard_map/ppermute | solution.py:37
  86.5 0.8 stats.1
  87.3 13.1 %all_to_all.10.stats = f32[32,8,128]{2,1,0:T(8,128)S(1)} all-to-all(f32[32,8,128]{2,1,0:T(8,128)S(1)} %get-tuple-element.61), channel_id=1, replica_groups=mesh['row'=8,'col'=32] {'col'}, dimensions={0} | all-to-all | bytes 262144 | tf_op jit(solution)/shard_map/all_to_all | solution.py:270
  100.5 15.4 %all_to_all.11.load = f32[8,32,128]{2,1,0:T(8,128)S(1)} all-to-all(f32[8,32,128]{2,1,0:T(8,128)S(1)} %pack.1), channel_id=1, replica_groups=mesh['row'=8,'col'=32] {'row'}, dimensions={0} | all-to-all | bytes 262144 | tf_op jit(solution)/shard_map/all_to_all | solution.py:279
  115.9 1.5 %finish.1 = (f32[64,256]{1,0:T(8,128)}, f32[1,64]{1,0:T(1,128)}, f32[2,256]{1,0:T(2,128)}) custom-call(s32[2]{0:T(128)S(1)} %copy-done.2, f32[8,32,128]{2,1,0:T(8,128)S(1)} %all_to_all.11.load), custom_call_target="tpu_custom_call" | custom-call | tf_op jit(solution)/shard_map/finish/pallas_call | solution.py:281
  (60 shorter events, 1.6 us)
Async XLA Ops:
  0.6 75.2 %copy-start = (f32[2,256]{1,0:T(2,128)S(1)}, f32[2,256]{1,0:T(2,128)}, u32[]{:S(2)}) copy-start(f32[2,256]{1,0:T(2,128)} %param.7) | copy-start | bytes 6148
  1.2 7.5 %copy-start.1 = (bf16[512,512]{1,0:T(8,128)(2,1)S(1)}, bf16[512,512]{1,0:T(8,128)(2,1)}, u32[]{:S(2)}) copy-start(bf16[512,512]{1,0:T(8,128)(2,1)} %refs_4_.7) | copy-start | bytes 1572868
  1.2 7.5 %copy-start.2 = (s32[2]{0:T(128)S(1)}, s32[2]{0:T(128)}, u32[]{:S(2)}) copy-start(s32[2]{0:T(128)} %pad_add_fusion.pos) | copy-start | bytes 28
  1.2 14.4 %slice-start = ((s8[8388608]{0:T(1024)(128)(4,1)}), s8[4194304]{0:T(1024)(128)(4,1)S(1)}, s32[]{:S(2)}) async-start(s8[8388608]{0:T(1024)(128)(4,1)} %bitcast.230), calls=%async_computation.2 | async-start | bytes 8388608
  5.4 10.3 %slice-start.1 = ((s8[8388608]{0:T(1024)(128)(4,1)}), s8[4194304]{0:T(1024)(128)(4,1)S(1)}, s32[]{:S(2)}) async-start(s8[8388608]{0:T(1024)(128)(4,1)} %bitcast.230), calls=%async_computation.3 | async-start | bytes 8388608
  5.4 10.2 %collective-permute-start.10 = (f32[2,4,8,16,8,128]{5,4,3,2,1,0:T(8,128)S(1)}, f32[2,4,8,16,8,128]{5,4,3,2,1,0:T(8,128)}, u32[]{:S(2)}, u32[]{:S(2)}) collective-permute-start(f32[2,4,8,16,8,128]{5,4,3,2,1,0:T(8,128)S(1)} %away1.1), channel_id=1, source_target_pairs={{0,1},{1,0},{2,3},{3,2},{4,5},{5,4},{6,7},{7,6},{8,9},{9,8},{10,11... | collective-permute-start | bytes 12582920 | tf_op jit(solution)/shard_map/ppermute | solution.py:26
  12.1 17.6 %collective-permute-start = (f32[2,4,8,16,8,128]{5,4,3,2,1,0:T(8,128)S(1)}, f32[2,4,8,16,8,128]{5,4,3,2,1,0:T(8,128)S(1)}, u32[]{:S(2)}, u32[]{:S(2)}) collective-permute-start(f32[2,4,8,16,8,128]{5,4,3,2,1,0:T(8,128)S(1)} %away0.1), channel_id=1, source_target_pairs={{0,1},{1,0},{2,3},{3,2},{4,5},{5,4},{6,7},{7,6},{8,9},{9,8},{10,11... | collective-permute-start | bytes 12582920 | tf_op jit(solution)/shard_map/ppermute | solution.py:26
  20.3 17.4 %collective-permute-start.11 = (f32[2,2,2,2,2,6,8,128]{7,6,5,4,3,2,1,0:T(8,128)S(1)}, f32[2,2,2,2,2,6,8,128]{7,6,5,4,3,2,1,0:T(8,128)S(1)}, u32[]{:S(2)}, u32[]{:S(2)}) collective-permute-start(f32[2,2,2,2,2,6,8,128]{7,6,5,4,3,2,1,0:T(8,128)S(1)} %bitcast.246), channel_id=1, source_target_pairs={{0,8},{1,25},{2,10},{3,27},{4,12},{5,29},{6,14},{7,31},{8,0},{9,17... | collective-permute-start | bytes 2359304 | tf_op jit(solution)/shard_map/ppermute | solution.py:39
  21.2 13.6 %collective-permute-start.13 = (f32[2,2,2,2,2,5,8,128]{7,6,5,4,3,2,1,0:T(8,128)S(1)}, f32[2,2,2,2,2,5,8,128]{7,6,5,4,3,2,1,0:T(8,128)S(1)}, u32[]{:S(2)}, u32[]{:S(2)}) collective-permute-start(f32[2,2,2,2,2,5,8,128]{7,6,5,4,3,2,1,0:T(8,128)S(1)} %slice_bitcast_fusion), channel_id=1, source_target_pairs={{0,32},{1,225},{2,34},{3,227},{4,36},{5,229},{6,38},{7,231},{8,40}... | collective-permute-start | bytes 1966088 | tf_op jit(solution)/shard_map/ppermute | solution.py:37
  26.9 10.8 %collective-permute-start.12 = (f32[2,2,2,2,2,5,8,128]{7,6,5,4,3,1,2,0:T(8,128)S(1)}, f32[2,2,2,2,2,5,8,128]{7,6,5,4,3,1,2,0:T(8,128)S(1)}, u32[]{:S(2)}, u32[]{:S(2)}) collective-permute-start(f32[2,2,2,2,2,5,8,128]{7,6,5,4,3,1,2,0:T(8,128)S(1)} %copy.14), channel_id=1, source_target_pairs={{0,2},{1,7},{2,0},{3,5},{4,6},{5,3},{6,4},{7,1},{8,10},{9,15},{10,... | collective-permute-start | bytes 1966088 | tf_op jit(solution)/shard_map/ppermute | solution.py:39
  32.4 13.2 %collective-permute-start.1 = (f32[2,2,2,2,2,6,8,128]{7,6,5,4,3,2,1,0:T(8,128)S(1)}, f32[2,2,2,2,2,6,8,128]{7,6,5,4,3,2,1,0:T(8,128)S(1)}, u32[]{:S(2)}, u32[]{:S(2)}) collective-permute-start(f32[2,2,2,2,2,6,8,128]{7,6,5,4,3,2,1,0:T(8,128)S(1)} %bitcast.245), channel_id=1, source_target_pairs={{0,8},{1,25},{2,10},{3,27},{4,12},{5,29},{6,14},{7,31},{8,0},{9,17... | collective-permute-start | bytes 2359304 | tf_op jit(solution)/shard_map/ppermute | solution.py:39
  32.9 10.7 %collective-permute-start.3 = (f32[2,2,2,2,2,5,8,128]{7,6,5,4,3,2,1,0:T(8,128)S(1)}, f32[2,2,2,2,2,5,8,128]{7,6,5,4,3,2,1,0:T(8,128)S(1)}, u32[]{:S(2)}, u32[]{:S(2)}) collective-permute-start(f32[2,2,2,2,2,5,8,128]{7,6,5,4,3,2,1,0:T(8,128)S(1)} %slice_bitcast_fusion.1), channel_id=1, source_target_pairs={{0,32},{1,225},{2,34},{3,227},{4,36},{5,229},{6,38},{7,231},{8,40}... | collective-permute-start | bytes 1966088 | tf_op jit(solution)/shard_map/ppermute | solution.py:37
  34.9 10.7 %collective-permute-start.2 = (f32[2,2,2,2,2,5,8,128]{7,6,5,4,3,1,2,0:T(8,128)S(1)}, f32[2,2,2,2,2,5,8,128]{7,6,5,4,3,1,2,0:T(8,128)S(1)}, u32[]{:S(2)}, u32[]{:S(2)}) collective-permute-start(f32[2,2,2,2,2,5,8,128]{7,6,5,4,3,1,2,0:T(8,128)S(1)} %copy.8), channel_id=1, source_target_pairs={{0,2},{1,7},{2,0},{3,5},{4,6},{5,3},{6,4},{7,1},{8,10},{9,15},{10,... | collective-permute-start | bytes 1966088 | tf_op jit(solution)/shard_map/ppermute | solution.py:39
  37.8 13.8 %collective-permute-start.14 = (f32[2,2,2,2,6,8,128]{6,5,4,3,2,1,0:T(8,128)S(1)}, f32[2,2,2,2,6,8,128]{6,5,4,3,2,1,0:T(8,128)S(1)}, u32[]{:S(2)}, u32[]{:S(2)}) collective-permute-start(f32[2,2,2,2,6,8,128]{6,5,4,3,2,1,0:T(8,128)S(1)} %get-tuple-element.80), channel_id=1, source_target_pairs={{0,2},{1,7},{2,0},{3,5},{4,6},{5,3},{6,4},{7,1},{8,10},{9,15},{10,... | collective-permute-start | bytes 1179656 | tf_op jit(solution)/shard_map/ppermute | solution.py:39
  40.7 8.2 %collective-permute-start.16 = (f32[2,2,2,2,5,8,128]{6,5,4,3,2,1,0:T(8,128)S(1)}, f32[2,2,2,2,5,8,128]{6,5,4,3,2,1,0:T(8,128)S(1)}, u32[]{:S(2)}, u32[]{:S(2)}) collective-permute-start(f32[2,2,2,2,5,8,128]{6,5,4,3,2,1,0:T(8,128)S(1)} %get-tuple-element.65), channel_id=1, source_target_pairs={{0,8},{1,25},{2,10},{3,27},{4,12},{5,29},{6,14},{7,31},{8,0},{9,17... | collective-permute-start | bytes 983048 | tf_op jit(solution)/shard_map/ppermute | solution.py:39
  43.6 8.1 %collective-permute-start.15 = (f32[2,2,2,2,5,8,128]{6,5,4,3,2,1,0:T(8,128)S(1)}, f32[2,2,2,2,5,8,128]{6,5,4,3,2,1,0:T(8,128)S(1)}, u32[]{:S(2)}, u32[]{:S(2)}) collective-permute-start(f32[2,2,2,2,5,8,128]{6,5,4,3,2,1,0:T(8,128)S(1)} %get-tuple-element.74), channel_id=1, source_target_pairs={{0,32},{1,225},{2,34},{3,227},{4,36},{5,229},{6,38},{7,231},{8,40}... | collective-permute-start | bytes 983048 | tf_op jit(solution)/shard_map/ppermute | solution.py:37
  45.7 10.5 %collective-permute-start.4 = (f32[2,2,2,2,6,8,128]{6,5,4,3,2,1,0:T(8,128)S(1)}, f32[2,2,2,2,6,8,128]{6,5,4,3,2,1,0:T(8,128)S(1)}, u32[]{:S(2)}, u32[]{:S(2)}) collective-permute-start(f32[2,2,2,2,6,8,128]{6,5,4,3,2,1,0:T(8,128)S(1)} %get-tuple-element.84), channel_id=1, source_target_pairs={{0,2},{1,7},{2,0},{3,5},{4,6},{5,3},{6,4},{7,1},{8,10},{9,15},{10,... | collective-permute-start | bytes 1179656 | tf_op jit(solution)/shard_map/ppermute | solution.py:39
  48.5 7.2 %collective-permute-start.6 = (f32[2,2,2,2,5,8,128]{6,5,4,3,2,1,0:T(8,128)S(1)}, f32[2,2,2,2,5,8,128]{6,5,4,3,2,1,0:T(8,128)S(1)}, u32[]{:S(2)}, u32[]{:S(2)}) collective-permute-start(f32[2,2,2,2,5,8,128]{6,5,4,3,2,1,0:T(8,128)S(1)} %get-tuple-element.67), channel_id=1, source_target_pairs={{0,8},{1,25},{2,10},{3,27},{4,12},{5,29},{6,14},{7,31},{8,0},{9,17... | collective-permute-start | bytes 983048 | tf_op jit(solution)/shard_map/ppermute | solution.py:39
  48.9 7.2 %collective-permute-start.5 = (f32[2,2,2,2,5,8,128]{6,5,4,3,2,1,0:T(8,128)S(1)}, f32[2,2,2,2,5,8,128]{6,5,4,3,2,1,0:T(8,128)S(1)}, u32[]{:S(2)}, u32[]{:S(2)}) collective-permute-start(f32[2,2,2,2,5,8,128]{6,5,4,3,2,1,0:T(8,128)S(1)} %get-tuple-element.76), channel_id=1, source_target_pairs={{0,32},{1,225},{2,34},{3,227},{4,36},{5,229},{6,38},{7,231},{8,40}... | collective-permute-start | bytes 983048 | tf_op jit(solution)/shard_map/ppermute | solution.py:37
  51.7 9.9 %collective-permute-start.18 = (f32[2,2,2,5,8,128]{5,4,3,2,1,0:T(8,128)S(1)}, f32[2,2,2,5,8,128]{5,4,3,2,1,0:T(8,128)S(1)}, u32[]{:S(2)}, u32[]{:S(2)}) collective-permute-start(f32[2,2,2,5,8,128]{5,4,3,2,1,0:T(8,128)S(1)} %get-tuple-element.86), channel_id=1, source_target_pairs={{0,8},{1,25},{2,10},{3,27},{4,12},{5,29},{6,14},{7,31},{8,0},{9,17... | collective-permute-start | bytes 491528 | tf_op jit(solution)/shard_map/ppermute | solution.py:39
  54.5 7.2 %collective-permute-start.17 = (f32[2,2,2,6,8,128]{5,4,3,2,1,0:T(8,128)S(1)}, f32[2,2,2,6,8,128]{5,4,3,2,1,0:T(8,128)S(1)}, u32[]{:S(2)}, u32[]{:S(2)}) collective-permute-start(f32[2,2,2,6,8,128]{5,4,3,2,1,0:T(8,128)S(1)} %get-tuple-element.78), channel_id=1, source_target_pairs={{0,32},{1,225},{2,34},{3,227},{4,36},{5,229},{6,38},{7,231},{8,40}... | collective-permute-start | bytes 589832 | tf_op jit(solution)/shard_map/ppermute | solution.py:37
  55.8 6.0 %collective-permute-start.19 = (f32[2,2,2,5,8,128]{5,4,3,2,1,0:T(8,128)S(1)}, f32[2,2,2,5,8,128]{5,4,3,2,1,0:T(8,128)S(1)}, u32[]{:S(2)}, u32[]{:S(2)}) collective-permute-start(f32[2,2,2,5,8,128]{5,4,3,2,1,0:T(8,128)S(1)} %get-tuple-element.87), channel_id=1, source_target_pairs={{0,2},{1,7},{2,0},{3,5},{4,6},{5,3},{6,4},{7,1},{8,10},{9,15},{10,... | collective-permute-start | bytes 491528 | tf_op jit(solution)/shard_map/ppermute | solution.py:39
  56.2 6.2 %collective-permute-start.8 = (f32[2,2,2,5,8,128]{5,4,3,2,1,0:T(8,128)S(1)}, f32[2,2,2,5,8,128]{5,4,3,2,1,0:T(8,128)S(1)}, u32[]{:S(2)}, u32[]{:S(2)}) collective-permute-start(f32[2,2,2,5,8,128]{5,4,3,2,1,0:T(8,128)S(1)} %get-tuple-element.90), channel_id=1, source_target_pairs={{0,8},{1,25},{2,10},{3,27},{4,12},{5,29},{6,14},{7,31},{8,0},{9,17... | collective-permute-start | bytes 491528 | tf_op jit(solution)/shard_map/ppermute | solution.py:39
  58.8 11.4 %collective-permute-start.7 = (f32[2,2,2,6,8,128]{5,4,3,2,1,0:T(8,128)S(1)}, f32[2,2,2,6,8,128]{5,4,3,2,1,0:T(8,128)S(1)}, u32[]{:S(2)}, u32[]{:S(2)}) collective-permute-start(f32[2,2,2,6,8,128]{5,4,3,2,1,0:T(8,128)S(1)} %get-tuple-element.82), channel_id=1, source_target_pairs={{0,32},{1,225},{2,34},{3,227},{4,36},{5,229},{6,38},{7,231},{8,40}... | collective-permute-start | bytes 589832 | tf_op jit(solution)/shard_map/ppermute | solution.py:37
  61.6 8.6 %collective-permute-start.9 = (f32[2,2,2,5,8,128]{5,4,3,2,1,0:T(8,128)S(1)}, f32[2,2,2,5,8,128]{5,4,3,2,1,0:T(8,128)S(1)}, u32[]{:S(2)}, u32[]{:S(2)}) collective-permute-start(f32[2,2,2,5,8,128]{5,4,3,2,1,0:T(8,128)S(1)} %get-tuple-element.91), channel_id=1, source_target_pairs={{0,2},{1,7},{2,0},{3,5},{4,6},{5,3},{6,4},{7,1},{8,10},{9,15},{10,... | collective-permute-start | bytes 491528 | tf_op jit(solution)/shard_map/ppermute | solution.py:39
  61.9 8.6 %collective-permute-start.20 = (f32[2,2,16,8,128]{4,3,2,1,0:T(8,128)S(1)}, f32[2,2,16,8,128]{4,3,2,1,0:T(8,128)S(1)}, u32[]{:S(2)}, u32[]{:S(2)}) collective-permute-start(f32[2,2,16,8,128]{4,3,2,1,0:T(8,128)S(1)} %pad_maximum_fusion), channel_id=1, source_target_pairs={{0,30},{1,11},{2,28},{3,9},{4,26},{5,15},{6,24},{7,13},{8,22},{9,3... | collective-permute-start | bytes 786440 | tf_op jit(solution)/shard_map/ppermute | solution.py:39
  62.0 8.4 %collective-permute-start.21 = (f32[2,2,16,8,128]{4,3,2,1,0:T(8,128)S(1)}, f32[2,2,16,8,128]{4,3,2,1,0:T(8,128)S(1)}, u32[]{:S(2)}, u32[]{:S(2)}) collective-permute-start(f32[2,2,16,8,128]{4,3,2,1,0:T(8,128)S(1)} %pad_maximum_fusion.1), channel_id=1, source_target_pairs={{0,24},{1,9},{2,26},{3,11},{4,28},{5,13},{6,30},{7,15},{8,16},{9,1... | collective-permute-start | bytes 786440 | tf_op jit(solution)/shard_map/ppermute | solution.py:39
  70.3 10.4 %copy-start.3 = (f32[64]{0:T(128)S(1)}, f32[64]{0:T(128)}, u32[]{:S(2)}) copy-start(f32[64]{0:T(128)} %param.6) | copy-start | bytes 772
  70.3 5.3 %collective-permute-start.22 = (f32[2,2,16,8,128]{4,3,2,1,0:T(8,128)S(1)}, f32[2,2,16,8,128]{4,3,2,1,0:T(8,128)S(1)}, u32[]{:S(2)}, u32[]{:S(2)}) collective-permute-start(f32[2,2,16,8,128]{4,3,2,1,0:T(8,128)S(1)} %pad_maximum_fusion.2), channel_id=1, source_target_pairs={{0,6},{1,3},{2,4},{3,1},{4,2},{5,7},{6,0},{7,5},{8,14},{9,11},{10,... | collective-permute-start | bytes 786440 | tf_op jit(solution)/shard_map/ppermute | solution.py:39
  75.7 4.8 %collective-permute-start.23 = (f32[2,16,8,128]{3,2,1,0:T(8,128)S(1)}, f32[2,16,8,128]{3,2,1,0:T(8,128)S(1)}, u32[]{:S(2)}, u32[]{:S(2)}) collective-permute-start(f32[2,16,8,128]{3,2,1,0:T(8,128)S(1)} %slice_bitcast_fusion.14), channel_id=1, source_target_pairs={{0,64},{1,65},{2,66},{3,67},{4,68},{5,69},{6,70},{7,71},{8,72},{9,... | collective-permute-start | bytes 393224 | tf_op jit(solution)/shard_map/ppermute | solution.py:37
  80.5 5.9 %collective-permute-start.24 = (f32[16,8,128]{2,1,0:T(8,128)S(1)}, f32[16,8,128]{2,1,0:T(8,128)S(1)}, u32[]{:S(2)}, u32[]{:S(2)}) collective-permute-start(f32[16,8,128]{2,1,0:T(8,128)S(1)} %slice_bitcast_fusion.28), channel_id=1, source_target_pairs={{0,192},{1,193},{2,194},{3,195},{4,196},{5,197},{6,198},{7,199},{8... | collective-permute-start | bytes 196616 | tf_op jit(solution)/shard_map/ppermute | solution.py:37

commit v5 on v4

--- a/solution.py
+++ b/solution.py
@@ -17,7 +17,7 @@
 GRANTS = (52, 44, 20, 20)
 
 RING4 = ((1, 3), (3, 1))
-RING8 = (1, 2, 6)
+RING8 = (1, 2, 6, 4)
 Z_MASKS = [i * RING8[0] ^ j * RING8[1] ^ k * RING8[2] for i in (0, 1) for j in (0, 1) for k in (0, 1)]
 UNITS = ((0, 6), (6, 11), (11, 16))
 
@@ -252,8 +252,8 @@
 
     got = along("xy", 1, quarter(1, 1)), along("x", 1, quarter(1, 0)), along("y", 1, quarter(0, 1))
     value = quarter(0, 0) + got[0] + got[1] + got[2]
-    for step in (1, 2):
-        value = value[0] + along("z", step, value[1])
+    got = along("z", 3, value[1, 1]), along("z", 1, value[1, 0]), along("z", 2, value[0, 1])
+    value = value[0, 0] + got[0] + got[1] + got[2]
 
     tile, stats = pl.pallas_call(
         stats_kernel,

time: 118 us -> 113 us (0.958)
  waiting for transfers between devices: 33.2 us -> 25.6 us
  starting transfers between devices: 35.2 us -> 40.8 us
  blocking collectives: 28.5 us -> 26.3 us
    ppermute x8 -> x9, waiting for transfers between devices: 14.9 us -> 7.5 us  [along(): return lax.ppermute(value, ('row', 'col'), pairs)]
    ppermute x8 -> x9, starting transfers between devices: 12.5 us -> 18.1 us  [along(): return lax.ppermute(value, ('row', 'col'), pairs)]
    all_to_all x1, blocking collectives: 15.4 us -> 10.9 us  [on_device(): load = lax.all_to_all(load, 'row', 0, 0, tiled=True)]
    all_to_all x1, blocking collectives: 13.1 us -> 15.4 us  [on_device(): stats = lax.all_to_all(stats, 'col', 0, 0, tiled=True)]
  transfers between devices with their start and end apart: 25 -> 26, of which waited for: 11 -> 11; matrix products, arithmetic and copies ran while one was open for 1% -> 1% of each run, Pallas kernels for 9% -> 9%
where the time goes in v5:
time: 113 us
  starting transfers between devices  40.8 us (36%)
  blocking collectives  26.3 us (23%)
  waiting for transfers between devices  25.6 us (23%)
  Pallas kernels  17.1 us (15%)
  other arithmetic  1.75 us (2%)
    ppermute x15, starting transfers between devices, along(): lax.ppermute(value, 'col', [(i, i ^ RING4[i % 2][step] * unit) for i in r...  18.9 us
    ppermute x9, starting transfers between devices, along(): return lax.ppermute(value, ('row', 'col'), pairs)  18.1 us
    all_to_all x1, blocking collectives, on_device(): stats = lax.all_to_all(stats, 'col', 0, 0, tiled=True)  15.4 us
    ppermute x15, waiting for transfers between devices, along(): lax.ppermute(value, 'col', [(i, i ^ RING4[i % 2][step] * unit) for i in r...  15.1 us
    pallas_call x4, Pallas kernels, partial(): pl.pallas_call(functools.partial(partial_kernel, chunk, to_sibling), grid...  14.7 us
    all_to_all x1, blocking collectives, on_device(): load = lax.all_to_all(load, 'row', 0, 0, tiled=True)  10.9 us
    ppermute x9, waiting for transfers between devices, along(): return lax.ppermute(value, ('row', 'col'), pairs)  7.5 us
    ppermute x2, starting transfers between devices, swap_cores(): return lax.ppermute(value, 'col', [(i, i ^ 1) for i in range(32)])  3.82 us
  transfers between devices with their start and end apart: 26, of which 11 were waited for; matrix products, arithmetic and copies ran while one was open for 1% of the time, Pallas kernels for 9%

profile of v5, /device:TPU:1, one launch (start us, length us, event | category | flops | bytes accessed | tf_op | source)
XLA Modules:
  0.0 113.1 jit_solution(17043383548697425432)
XLA Ops:
  0.6 0.6 pad_add_fusion.pos
  1.2 4.2 %away1.1 = f32[2,4,8,16,8,128]{5,4,3,2,1,0:T(8,128)S(1)} custom-call(s32[2]{0:T(128)} %pad_add_fusion.pos, bf16[512,8192]{1,0:T(8,128)(2,1)} %refs_3_.7, bf16[512,8192]{1,0:T(8,128)(2,1)} %refs_3_.7, bf16[512,8192]{1,0:T(8,128)(2,1)} %refs_3_.7, bf16[512,8192]{1,0:T(8,128)(2,1)} %refs_3_.7, bf16[512,512]{1,0:T(8,128)(2,1)} %refs_4_.7), custom_call_target="tpu_custom_call" | custom-call | flops 1073741824 | bytes 7340032 | tf_op jit(solution)/shard_map/away1/pallas_call | solution.py:98
  5.4 3.3 %collective-permute-start.10 = (f32[2,4,8,16,8,128]{5,4,3,2,1,0:T(8,128)S(1)}, f32[2,4,8,16,8,128]{5,4,3,2,1,0:T(8,128)}, u32[]{:S(2)}, u32[]{:S(2)}) collective-permute-start(f32[2,4,8,16,8,128]{5,4,3,2,1,0:T(8,128)S(1)} %away1.1), channel_id=1, source_target_pairs={{0,1},{1,0},{2,3},{3,2},{4,5},{5,4},{6,7},{7,6},{8,9},{9,8},{10,11... | collective-permute-start | bytes 12582920 | tf_op jit(solution)/shard_map/ppermute | solution.py:26
  8.8 3.4 %away0.1 = f32[2,4,8,16,8,128]{5,4,3,2,1,0:T(8,128)S(1)} custom-call(s32[2]{0:T(128)S(1)} %copy-done.2, bf16[512,8192]{1,0:T(8,128)(2,1)} %refs_3_.7, bf16[512,8192]{1,0:T(8,128)(2,1)} %refs_3_.7, bf16[512,8192]{1,0:T(8,128)(2,1)} %refs_3_.7, bf16[512,8192]{1,0:T(8,128)(2,1)} %refs_3_.7, bf16[512,512]{1,0:T(8,128)(2,1)S(1)} %copy-done.1), custom_call_target="tpu_custom_call" | custom-call | flops 1073741824 | bytes 7340032 | tf_op jit(solution)/shard_map/away0/pallas_call | solution.py:98
  12.1 0.5 collective-permute-start
  12.6 3.0 %collective-permute-done.10.refs_5_ = f32[2,4,8,16,8,128]{5,4,3,2,1,0:T(8,128)} collective-permute-done((f32[2,4,8,16,8,128]{5,4,3,2,1,0:T(8,128)S(1)}, f32[2,4,8,16,8,128]{5,4,3,2,1,0:T(8,128)}, u32[]{:S(2)}, u32[]{:S(2)}) %collective-permute-start.10) | collective-permute-done | bytes 4194336 | tf_op jit(solution)/shard_map/ppermute | solution.py:26
  15.7 4.6 %near1.1 = (f32[2,4,8,6,8,128]{5,4,3,2,1,0:T(8,128)S(1)}, f32[2,2,8,5,8,128]{5,4,3,2,1,0:T(8,128)S(1)}, f32[2,2,8,5,8,128]{5,4,3,2,1,0:T(8,128)S(1)}, f32[2,4,8,5,8,128]{5,4,3,2,1,0:T(8,128)S(1)}) custom-call(s32[2]{0:T(128)S(1)} %copy-done.2, bf16[512,8192]{1,0:T(8,128)(2,1)S(1)} %bitcast.233, bf16[512,8192]{1,0:T(8,128)(2,1)S(1)} %bitcast.233, ...), custom_call_target="tpu_custom_call" | custom-call | flops 1073741824 | bytes 11534336 | tf_op jit(solution)/shard_map/near1/pallas_call | solution.py:98
  20.3 0.8 collective-permute-start.11
  21.2 5.7 %collective-permute-start.13 = (f32[2,2,2,2,2,5,8,128]{7,6,5,4,3,2,1,0:T(8,128)S(1)}, f32[2,2,2,2,2,5,8,128]{7,6,5,4,3,2,1,0:T(8,128)S(1)}, u32[]{:S(2)}, u32[]{:S(2)}) collective-permute-start(f32[2,2,2,2,2,5,8,128]{7,6,5,4,3,2,1,0:T(8,128)S(1)} %slice_bitcast_fusion), channel_id=1, source_target_pairs={{0,32},{1,225},{2,34},{3,227},{4,36},{5,229},{6,38},{7,231},{8,40}... | collective-permute-start | bytes 1966088 | tf_op jit(solution)/shard_map/ppermute | solution.py:37
  26.9 2.8 %collective-permute-start.12 = (f32[2,2,2,2,2,5,8,128]{7,6,5,4,3,1,2,0:T(8,128)S(1)}, f32[2,2,2,2,2,5,8,128]{7,6,5,4,3,1,2,0:T(8,128)S(1)}, u32[]{:S(2)}, u32[]{:S(2)}) collective-permute-start(f32[2,2,2,2,2,5,8,128]{7,6,5,4,3,1,2,0:T(8,128)S(1)} %copy.14), channel_id=1, source_target_pairs={{0,2},{1,7},{2,0},{3,5},{4,6},{5,3},{6,4},{7,1},{8,10},{9,15},{10,... | collective-permute-start | bytes 1966088 | tf_op jit(solution)/shard_map/ppermute | solution.py:39
  29.8 2.6 %near0.1 = (f32[2,4,8,6,8,128]{5,4,3,2,1,0:T(8,128)S(1)}, f32[2,2,8,5,8,128]{5,4,3,2,1,0:T(8,128)S(1)}, f32[2,2,8,5,8,128]{5,4,3,2,1,0:T(8,128)S(1)}, f32[2,4,8,5,8,128]{5,4,3,2,1,0:T(8,128)S(1)}) custom-call(s32[2]{0:T(128)S(1)} %copy-done.2, bf16[512,8192]{1,0:T(8,128)(2,1)S(1)} %bitcast.233, bf16[512,8192]{1,0:T(8,128)(2,1)S(1)} %bitcast.233, ...), custom_call_target="tpu_custom_call" | custom-call | flops 1073741824 | bytes 11534336 | tf_op jit(solution)/shard_map/near0/pallas_call | solution.py:98
  32.4 0.3 collective-permute-start.1
  32.9 0.1 collective-permute-start.3
  33.0 1.8 %collective-permute-done.13 = f32[2,2,2,2,2,5,8,128]{7,6,5,4,3,2,1,0:T(8,128)S(1)} collective-permute-done((f32[2,2,2,2,2,5,8,128]{7,6,5,4,3,2,1,0:T(8,128)S(1)}, f32[2,2,2,2,2,5,8,128]{7,6,5,4,3,2,1,0:T(8,128)S(1)}, u32[]{:S(2)}, u32[]{:S(2)}) %collective-permute-start.13) | collective-permute-done | bytes 655392 | tf_op jit(solution)/shard_map/ppermute | solution.py:37
  34.9 2.7 %collective-permute-start.2 = (f32[2,2,2,2,2,5,8,128]{7,6,5,4,3,1,2,0:T(8,128)S(1)}, f32[2,2,2,2,2,5,8,128]{7,6,5,4,3,1,2,0:T(8,128)S(1)}, u32[]{:S(2)}, u32[]{:S(2)}) collective-permute-start(f32[2,2,2,2,2,5,8,128]{7,6,5,4,3,1,2,0:T(8,128)S(1)} %copy.8), channel_id=1, source_target_pairs={{0,2},{1,7},{2,0},{3,5},{4,6},{5,3},{6,4},{7,1},{8,10},{9,15},{10,... | collective-permute-start | bytes 1966088 | tf_op jit(solution)/shard_map/ppermute | solution.py:39
  37.6 0.1 collective-permute-done.12
  37.7 0.1 bitcast_add_fusion.1
  37.8 2.8 %collective-permute-start.14 = (f32[2,2,2,2,6,8,128]{6,5,4,3,2,1,0:T(8,128)S(1)}, f32[2,2,2,2,6,8,128]{6,5,4,3,2,1,0:T(8,128)S(1)}, u32[]{:S(2)}, u32[]{:S(2)}) collective-permute-start(f32[2,2,2,2,6,8,128]{6,5,4,3,2,1,0:T(8,128)S(1)} %get-tuple-element.80), channel_id=1, source_target_pairs={{0,2},{1,7},{2,0},{3,5},{4,6},{5,3},{6,4},{7,1},{8,10},{9,15},{10,... | collective-permute-start | bytes 1179656 | tf_op jit(solution)/shard_map/ppermute | solution.py:39
  40.7 0.3 collective-permute-start.16
  41.0 2.6 %collective-permute-done.3 = f32[2,2,2,2,2,5,8,128]{7,6,5,4,3,2,1,0:T(8,128)S(1)} collective-permute-done((f32[2,2,2,2,2,5,8,128]{7,6,5,4,3,2,1,0:T(8,128)S(1)}, f32[2,2,2,2,2,5,8,128]{7,6,5,4,3,2,1,0:T(8,128)S(1)}, u32[]{:S(2)}, u32[]{:S(2)}) %collective-permute-start.3) | collective-permute-done | bytes 655392 | tf_op jit(solution)/shard_map/ppermute | solution.py:37
  43.6 0.9 collective-permute-start.15
  44.6 1.0 collective-permute-done.2
  45.6 0.1 bitcast_add_fusion.3
  45.7 2.8 %collective-permute-start.4 = (f32[2,2,2,2,6,8,128]{6,5,4,3,2,1,0:T(8,128)S(1)}, f32[2,2,2,2,6,8,128]{6,5,4,3,2,1,0:T(8,128)S(1)}, u32[]{:S(2)}, u32[]{:S(2)}) collective-permute-start(f32[2,2,2,2,6,8,128]{6,5,4,3,2,1,0:T(8,128)S(1)} %get-tuple-element.84), channel_id=1, source_target_pairs={{0,2},{1,7},{2,0},{3,5},{4,6},{5,3},{6,4},{7,1},{8,10},{9,15},{10,... | collective-permute-start | bytes 1179656 | tf_op jit(solution)/shard_map/ppermute | solution.py:39
  48.4 0.1 fusion.7
  48.5 0.3 collective-permute-start.6
  48.9 2.8 %collective-permute-start.5 = (f32[2,2,2,2,5,8,128]{6,5,4,3,2,1,0:T(8,128)S(1)}, f32[2,2,2,2,5,8,128]{6,5,4,3,2,1,0:T(8,128)S(1)}, u32[]{:S(2)}, u32[]{:S(2)}) collective-permute-start(f32[2,2,2,2,5,8,128]{6,5,4,3,2,1,0:T(8,128)S(1)} %get-tuple-element.76), channel_id=1, source_target_pairs={{0,32},{1,225},{2,34},{3,227},{4,36},{5,229},{6,38},{7,231},{8,40}... | collective-permute-start | bytes 983048 | tf_op jit(solution)/shard_map/ppermute | solution.py:37
  51.7 2.7 %collective-permute-start.18 = (f32[2,2,2,5,8,128]{5,4,3,2,1,0:T(8,128)S(1)}, f32[2,2,2,5,8,128]{5,4,3,2,1,0:T(8,128)S(1)}, u32[]{:S(2)}, u32[]{:S(2)}) collective-permute-start(f32[2,2,2,5,8,128]{5,4,3,2,1,0:T(8,128)S(1)} %get-tuple-element.86), channel_id=1, source_target_pairs={{0,8},{1,25},{2,10},{3,27},{4,12},{5,29},{6,14},{7,31},{8,0},{9,17... | collective-permute-start | bytes 491528 | tf_op jit(solution)/shard_map/ppermute | solution.py:39
  54.5 0.1 collective-permute-start.17
  54.7 1.1 collective-permute-done.6
  55.8 0.2 collective-permute-start.19
  55.9 0.2 collective-permute-done.5
  56.2 2.6 %collective-permute-start.8 = (f32[2,2,2,5,8,128]{5,4,3,2,1,0:T(8,128)S(1)}, f32[2,2,2,5,8,128]{5,4,3,2,1,0:T(8,128)S(1)}, u32[]{:S(2)}, u32[]{:S(2)}) collective-permute-start(f32[2,2,2,5,8,128]{5,4,3,2,1,0:T(8,128)S(1)} %get-tuple-element.90), channel_id=1, source_target_pairs={{0,8},{1,25},{2,10},{3,27},{4,12},{5,29},{6,14},{7,31},{8,0},{9,17... | collective-permute-start | bytes 491528 | tf_op jit(solution)/shard_map/ppermute | solution.py:39
  58.8 2.8 %collective-permute-start.7 = (f32[2,2,2,6,8,128]{5,4,3,2,1,0:T(8,128)S(1)}, f32[2,2,2,6,8,128]{5,4,3,2,1,0:T(8,128)S(1)}, u32[]{:S(2)}, u32[]{:S(2)}) collective-permute-start(f32[2,2,2,6,8,128]{5,4,3,2,1,0:T(8,128)S(1)} %get-tuple-element.82), channel_id=1, source_target_pairs={{0,32},{1,225},{2,34},{3,227},{4,36},{5,229},{6,38},{7,231},{8,40}... | collective-permute-start | bytes 589832 | tf_op jit(solution)/shard_map/ppermute | solution.py:37
  61.6 0.1 collective-permute-start.9
  62.0 0.4 collective-permute-start.21
  62.4 7.8 %collective-permute-done.9 = f32[2,2,2,5,8,128]{5,4,3,2,1,0:T(8,128)S(1)} collective-permute-done((f32[2,2,2,5,8,128]{5,4,3,2,1,0:T(8,128)S(1)}, f32[2,2,2,5,8,128]{5,4,3,2,1,0:T(8,128)S(1)}, u32[]{:S(2)}, u32[]{:S(2)}) %collective-permute-start.9) | collective-permute-done | bytes 163872 | tf_op jit(solution)/shard_map/ppermute | solution.py:39
  70.3 0.1 collective-permute-start.22
  70.6 5.0 %collective-permute-done.22 = f32[2,2,16,8,128]{4,3,2,1,0:T(8,128)S(1)} collective-permute-done((f32[2,2,16,8,128]{4,3,2,1,0:T(8,128)S(1)}, f32[2,2,16,8,128]{4,3,2,1,0:T(8,128)S(1)}, u32[]{:S(2)}, u32[]{:S(2)}) %collective-permute-start.22) | collective-permute-done | bytes 262176 | tf_op jit(solution)/shard_map/ppermute | solution.py:39
  75.7 0.1 collective-permute-start.23
  75.8 0.1 collective-permute-start.24
  75.9 5.5 %collective-permute-start.25 = (f32[16,8,128]{2,1,0:T(8,128)S(1)}, f32[16,8,128]{2,1,0:T(8,128)S(1)}, u32[]{:S(2)}, u32[]{:S(2)}) collective-permute-start(f32[16,8,128]{2,1,0:T(8,128)S(1)} %get-tuple-element.106), channel_id=1, source_target_pairs={{0,192},{1,193},{2,194},{3,195},{4,196},{5,197},{6,198},{7,199},{8... | collective-permute-start | bytes 196616 | tf_op jit(solution)/shard_map/ppermute | solution.py:37
  81.5 2.1 %collective-permute-done.23 = f32[16,8,128]{2,1,0:T(8,128)S(1)} collective-permute-done((f32[16,8,128]{2,1,0:T(8,128)S(1)}, f32[16,8,128]{2,1,0:T(8,128)S(1)}, u32[]{:S(2)}, u32[]{:S(2)}) %collective-permute-start.23) | collective-permute-done | bytes 65568 | tf_op jit(solution)/shard_map/ppermute | solution.py:37
  83.6 0.8 collective-permute-done.25
  84.4 0.8 stats.1
  85.2 15.4 %all_to_all.10.stats = f32[32,8,128]{2,1,0:T(8,128)S(1)} all-to-all(f32[32,8,128]{2,1,0:T(8,128)S(1)} %get-tuple-element.61), channel_id=1, replica_groups=mesh['row'=8,'col'=32] {'col'}, dimensions={0} | all-to-all | bytes 262144 | tf_op jit(solution)/shard_map/all_to_all | solution.py:270
  100.7 10.9 %all_to_all.11.load = f32[8,32,128]{2,1,0:T(8,128)S(1)} all-to-all(f32[8,32,128]{2,1,0:T(8,128)S(1)} %pack.1), channel_id=1, replica_groups=mesh['row'=8,'col'=32] {'row'}, dimensions={0} | all-to-all | bytes 262144 | tf_op jit(solution)/shard_map/all_to_all | solution.py:279
  111.6 1.5 %finish.1 = (f32[64,256]{1,0:T(8,128)}, f32[1,64]{1,0:T(1,128)}, f32[2,256]{1,0:T(2,128)}) custom-call(s32[2]{0:T(128)S(1)} %copy-done.2, f32[8,32,128]{2,1,0:T(8,128)S(1)} %all_to_all.11.load), custom_call_target="tpu_custom_call" | custom-call | tf_op jit(solution)/shard_map/finish/pallas_call | solution.py:281
  (60 shorter events, 1.7 us)
Async XLA Ops:
  0.6 69.8 %copy-start = (f32[2,256]{1,0:T(2,128)S(1)}, f32[2,256]{1,0:T(2,128)}, u32[]{:S(2)}) copy-start(f32[2,256]{1,0:T(2,128)} %param.7) | copy-start | bytes 6148
  1.2 7.5 %copy-start.1 = (bf16[512,512]{1,0:T(8,128)(2,1)S(1)}, bf16[512,512]{1,0:T(8,128)(2,1)}, u32[]{:S(2)}) copy-start(bf16[512,512]{1,0:T(8,128)(2,1)} %refs_4_.7) | copy-start | bytes 1572868
  1.2 7.5 %copy-start.2 = (s32[2]{0:T(128)S(1)}, s32[2]{0:T(128)}, u32[]{:S(2)}) copy-start(s32[2]{0:T(128)} %pad_add_fusion.pos) | copy-start | bytes 28
  1.2 14.4 %slice-start = ((s8[8388608]{0:T(1024)(128)(4,1)}), s8[4194304]{0:T(1024)(128)(4,1)S(1)}, s32[]{:S(2)}) async-start(s8[8388608]{0:T(1024)(128)(4,1)} %bitcast.232), calls=%async_computation.2 | async-start | bytes 8388608
  5.4 10.3 %slice-start.1 = ((s8[8388608]{0:T(1024)(128)(4,1)}), s8[4194304]{0:T(1024)(128)(4,1)S(1)}, s32[]{:S(2)}) async-start(s8[8388608]{0:T(1024)(128)(4,1)} %bitcast.232), calls=%async_computation.3 | async-start | bytes 8388608
  5.4 10.2 %collective-permute-start.10 = (f32[2,4,8,16,8,128]{5,4,3,2,1,0:T(8,128)S(1)}, f32[2,4,8,16,8,128]{5,4,3,2,1,0:T(8,128)}, u32[]{:S(2)}, u32[]{:S(2)}) collective-permute-start(f32[2,4,8,16,8,128]{5,4,3,2,1,0:T(8,128)S(1)} %away1.1), channel_id=1, source_target_pairs={{0,1},{1,0},{2,3},{3,2},{4,5},{5,4},{6,7},{7,6},{8,9},{9,8},{10,11... | collective-permute-start | bytes 12582920 | tf_op jit(solution)/shard_map/ppermute | solution.py:26
  12.1 17.6 %collective-permute-start = (f32[2,4,8,16,8,128]{5,4,3,2,1,0:T(8,128)S(1)}, f32[2,4,8,16,8,128]{5,4,3,2,1,0:T(8,128)S(1)}, u32[]{:S(2)}, u32[]{:S(2)}) collective-permute-start(f32[2,4,8,16,8,128]{5,4,3,2,1,0:T(8,128)S(1)} %away0.1), channel_id=1, source_target_pairs={{0,1},{1,0},{2,3},{3,2},{4,5},{5,4},{6,7},{7,6},{8,9},{9,8},{10,11... | collective-permute-start | bytes 12582920 | tf_op jit(solution)/shard_map/ppermute | solution.py:26
  20.3 17.4 %collective-permute-start.11 = (f32[2,2,2,2,2,6,8,128]{7,6,5,4,3,2,1,0:T(8,128)S(1)}, f32[2,2,2,2,2,6,8,128]{7,6,5,4,3,2,1,0:T(8,128)S(1)}, u32[]{:S(2)}, u32[]{:S(2)}) collective-permute-start(f32[2,2,2,2,2,6,8,128]{7,6,5,4,3,2,1,0:T(8,128)S(1)} %bitcast.248), channel_id=1, source_target_pairs={{0,8},{1,25},{2,10},{3,27},{4,12},{5,29},{6,14},{7,31},{8,0},{9,17... | collective-permute-start | bytes 2359304 | tf_op jit(solution)/shard_map/ppermute | solution.py:39
  21.2 13.6 %collective-permute-start.13 = (f32[2,2,2,2,2,5,8,128]{7,6,5,4,3,2,1,0:T(8,128)S(1)}, f32[2,2,2,2,2,5,8,128]{7,6,5,4,3,2,1,0:T(8,128)S(1)}, u32[]{:S(2)}, u32[]{:S(2)}) collective-permute-start(f32[2,2,2,2,2,5,8,128]{7,6,5,4,3,2,1,0:T(8,128)S(1)} %slice_bitcast_fusion), channel_id=1, source_target_pairs={{0,32},{1,225},{2,34},{3,227},{4,36},{5,229},{6,38},{7,231},{8,40}... | collective-permute-start | bytes 1966088 | tf_op jit(solution)/shard_map/ppermute | solution.py:37
  26.9 10.8 %collective-permute-start.12 = (f32[2,2,2,2,2,5,8,128]{7,6,5,4,3,1,2,0:T(8,128)S(1)}, f32[2,2,2,2,2,5,8,128]{7,6,5,4,3,1,2,0:T(8,128)S(1)}, u32[]{:S(2)}, u32[]{:S(2)}) collective-permute-start(f32[2,2,2,2,2,5,8,128]{7,6,5,4,3,1,2,0:T(8,128)S(1)} %copy.14), channel_id=1, source_target_pairs={{0,2},{1,7},{2,0},{3,5},{4,6},{5,3},{6,4},{7,1},{8,10},{9,15},{10,... | collective-permute-start | bytes 1966088 | tf_op jit(solution)/shard_map/ppermute | solution.py:39
  32.4 13.2 %collective-permute-start.1 = (f32[2,2,2,2,2,6,8,128]{7,6,5,4,3,2,1,0:T(8,128)S(1)}, f32[2,2,2,2,2,6,8,128]{7,6,5,4,3,2,1,0:T(8,128)S(1)}, u32[]{:S(2)}, u32[]{:S(2)}) collective-permute-start(f32[2,2,2,2,2,6,8,128]{7,6,5,4,3,2,1,0:T(8,128)S(1)} %bitcast.247), channel_id=1, source_target_pairs={{0,8},{1,25},{2,10},{3,27},{4,12},{5,29},{6,14},{7,31},{8,0},{9,17... | collective-permute-start | bytes 2359304 | tf_op jit(solution)/shard_map/ppermute | solution.py:39
  32.9 10.7 %collective-permute-start.3 = (f32[2,2,2,2,2,5,8,128]{7,6,5,4,3,2,1,0:T(8,128)S(1)}, f32[2,2,2,2,2,5,8,128]{7,6,5,4,3,2,1,0:T(8,128)S(1)}, u32[]{:S(2)}, u32[]{:S(2)}) collective-permute-start(f32[2,2,2,2,2,5,8,128]{7,6,5,4,3,2,1,0:T(8,128)S(1)} %slice_bitcast_fusion.1), channel_id=1, source_target_pairs={{0,32},{1,225},{2,34},{3,227},{4,36},{5,229},{6,38},{7,231},{8,40}... | collective-permute-start | bytes 1966088 | tf_op jit(solution)/shard_map/ppermute | solution.py:37
  34.9 10.7 %collective-permute-start.2 = (f32[2,2,2,2,2,5,8,128]{7,6,5,4,3,1,2,0:T(8,128)S(1)}, f32[2,2,2,2,2,5,8,128]{7,6,5,4,3,1,2,0:T(8,128)S(1)}, u32[]{:S(2)}, u32[]{:S(2)}) collective-permute-start(f32[2,2,2,2,2,5,8,128]{7,6,5,4,3,1,2,0:T(8,128)S(1)} %copy.8), channel_id=1, source_target_pairs={{0,2},{1,7},{2,0},{3,5},{4,6},{5,3},{6,4},{7,1},{8,10},{9,15},{10,... | collective-permute-start | bytes 1966088 | tf_op jit(solution)/shard_map/ppermute | solution.py:39
  37.8 13.8 %collective-permute-start.14 = (f32[2,2,2,2,6,8,128]{6,5,4,3,2,1,0:T(8,128)S(1)}, f32[2,2,2,2,6,8,128]{6,5,4,3,2,1,0:T(8,128)S(1)}, u32[]{:S(2)}, u32[]{:S(2)}) collective-permute-start(f32[2,2,2,2,6,8,128]{6,5,4,3,2,1,0:T(8,128)S(1)} %get-tuple-element.80), channel_id=1, source_target_pairs={{0,2},{1,7},{2,0},{3,5},{4,6},{5,3},{6,4},{7,1},{8,10},{9,15},{10,... | collective-permute-start | bytes 1179656 | tf_op jit(solution)/shard_map/ppermute | solution.py:39
  40.7 8.2 %collective-permute-start.16 = (f32[2,2,2,2,5,8,128]{6,5,4,3,2,1,0:T(8,128)S(1)}, f32[2,2,2,2,5,8,128]{6,5,4,3,2,1,0:T(8,128)S(1)}, u32[]{:S(2)}, u32[]{:S(2)}) collective-permute-start(f32[2,2,2,2,5,8,128]{6,5,4,3,2,1,0:T(8,128)S(1)} %get-tuple-element.65), channel_id=1, source_target_pairs={{0,8},{1,25},{2,10},{3,27},{4,12},{5,29},{6,14},{7,31},{8,0},{9,17... | collective-permute-start | bytes 983048 | tf_op jit(solution)/shard_map/ppermute | solution.py:39
  43.6 8.1 %collective-permute-start.15 = (f32[2,2,2,2,5,8,128]{6,5,4,3,2,1,0:T(8,128)S(1)}, f32[2,2,2,2,5,8,128]{6,5,4,3,2,1,0:T(8,128)S(1)}, u32[]{:S(2)}, u32[]{:S(2)}) collective-permute-start(f32[2,2,2,2,5,8,128]{6,5,4,3,2,1,0:T(8,128)S(1)} %get-tuple-element.74), channel_id=1, source_target_pairs={{0,32},{1,225},{2,34},{3,227},{4,36},{5,229},{6,38},{7,231},{8,40}... | collective-permute-start | bytes 983048 | tf_op jit(solution)/shard_map/ppermute | solution.py:37
  45.7 10.5 %collective-permute-start.4 = (f32[2,2,2,2,6,8,128]{6,5,4,3,2,1,0:T(8,128)S(1)}, f32[2,2,2,2,6,8,128]{6,5,4,3,2,1,0:T(8,128)S(1)}, u32[]{:S(2)}, u32[]{:S(2)}) collective-permute-start(f32[2,2,2,2,6,8,128]{6,5,4,3,2,1,0:T(8,128)S(1)} %get-tuple-element.84), channel_id=1, source_target_pairs={{0,2},{1,7},{2,0},{3,5},{4,6},{5,3},{6,4},{7,1},{8,10},{9,15},{10,... | collective-permute-start | bytes 1179656 | tf_op jit(solution)/shard_map/ppermute | solution.py:39
  48.5 7.2 %collective-permute-start.6 = (f32[2,2,2,2,5,8,128]{6,5,4,3,2,1,0:T(8,128)S(1)}, f32[2,2,2,2,5,8,128]{6,5,4,3,2,1,0:T(8,128)S(1)}, u32[]{:S(2)}, u32[]{:S(2)}) collective-permute-start(f32[2,2,2,2,5,8,128]{6,5,4,3,2,1,0:T(8,128)S(1)} %get-tuple-element.67), channel_id=1, source_target_pairs={{0,8},{1,25},{2,10},{3,27},{4,12},{5,29},{6,14},{7,31},{8,0},{9,17... | collective-permute-start | bytes 983048 | tf_op jit(solution)/shard_map/ppermute | solution.py:39
  48.9 7.2 %collective-permute-start.5 = (f32[2,2,2,2,5,8,128]{6,5,4,3,2,1,0:T(8,128)S(1)}, f32[2,2,2,2,5,8,128]{6,5,4,3,2,1,0:T(8,128)S(1)}, u32[]{:S(2)}, u32[]{:S(2)}) collective-permute-start(f32[2,2,2,2,5,8,128]{6,5,4,3,2,1,0:T(8,128)S(1)} %get-tuple-element.76), channel_id=1, source_target_pairs={{0,32},{1,225},{2,34},{3,227},{4,36},{5,229},{6,38},{7,231},{8,40}... | collective-permute-start | bytes 983048 | tf_op jit(solution)/shard_map/ppermute | solution.py:37
  51.7 9.9 %collective-permute-start.18 = (f32[2,2,2,5,8,128]{5,4,3,2,1,0:T(8,128)S(1)}, f32[2,2,2,5,8,128]{5,4,3,2,1,0:T(8,128)S(1)}, u32[]{:S(2)}, u32[]{:S(2)}) collective-permute-start(f32[2,2,2,5,8,128]{5,4,3,2,1,0:T(8,128)S(1)} %get-tuple-element.86), channel_id=1, source_target_pairs={{0,8},{1,25},{2,10},{3,27},{4,12},{5,29},{6,14},{7,31},{8,0},{9,17... | collective-permute-start | bytes 491528 | tf_op jit(solution)/shard_map/ppermute | solution.py:39
  54.5 7.2 %collective-permute-start.17 = (f32[2,2,2,6,8,128]{5,4,3,2,1,0:T(8,128)S(1)}, f32[2,2,2,6,8,128]{5,4,3,2,1,0:T(8,128)S(1)}, u32[]{:S(2)}, u32[]{:S(2)}) collective-permute-start(f32[2,2,2,6,8,128]{5,4,3,2,1,0:T(8,128)S(1)} %get-tuple-element.78), channel_id=1, source_target_pairs={{0,32},{1,225},{2,34},{3,227},{4,36},{5,229},{6,38},{7,231},{8,40}... | collective-permute-start | bytes 589832 | tf_op jit(solution)/shard_map/ppermute | solution.py:37
  55.8 6.0 %collective-permute-start.19 = (f32[2,2,2,5,8,128]{5,4,3,2,1,0:T(8,128)S(1)}, f32[2,2,2,5,8,128]{5,4,3,2,1,0:T(8,128)S(1)}, u32[]{:S(2)}, u32[]{:S(2)}) collective-permute-start(f32[2,2,2,5,8,128]{5,4,3,2,1,0:T(8,128)S(1)} %get-tuple-element.87), channel_id=1, source_target_pairs={{0,2},{1,7},{2,0},{3,5},{4,6},{5,3},{6,4},{7,1},{8,10},{9,15},{10,... | collective-permute-start | bytes 491528 | tf_op jit(solution)/shard_map/ppermute | solution.py:39
  56.2 6.2 %collective-permute-start.8 = (f32[2,2,2,5,8,128]{5,4,3,2,1,0:T(8,128)S(1)}, f32[2,2,2,5,8,128]{5,4,3,2,1,0:T(8,128)S(1)}, u32[]{:S(2)}, u32[]{:S(2)}) collective-permute-start(f32[2,2,2,5,8,128]{5,4,3,2,1,0:T(8,128)S(1)} %get-tuple-element.90), channel_id=1, source_target_pairs={{0,8},{1,25},{2,10},{3,27},{4,12},{5,29},{6,14},{7,31},{8,0},{9,17... | collective-permute-start | bytes 491528 | tf_op jit(solution)/shard_map/ppermute | solution.py:39
  58.8 11.4 %collective-permute-start.7 = (f32[2,2,2,6,8,128]{5,4,3,2,1,0:T(8,128)S(1)}, f32[2,2,2,6,8,128]{5,4,3,2,1,0:T(8,128)S(1)}, u32[]{:S(2)}, u32[]{:S(2)}) collective-permute-start(f32[2,2,2,6,8,128]{5,4,3,2,1,0:T(8,128)S(1)} %get-tuple-element.82), channel_id=1, source_target_pairs={{0,32},{1,225},{2,34},{3,227},{4,36},{5,229},{6,38},{7,231},{8,40}... | collective-permute-start | bytes 589832 | tf_op jit(solution)/shard_map/ppermute | solution.py:37
  61.6 8.6 %collective-permute-start.9 = (f32[2,2,2,5,8,128]{5,4,3,2,1,0:T(8,128)S(1)}, f32[2,2,2,5,8,128]{5,4,3,2,1,0:T(8,128)S(1)}, u32[]{:S(2)}, u32[]{:S(2)}) collective-permute-start(f32[2,2,2,5,8,128]{5,4,3,2,1,0:T(8,128)S(1)} %get-tuple-element.91), channel_id=1, source_target_pairs={{0,2},{1,7},{2,0},{3,5},{4,6},{5,3},{6,4},{7,1},{8,10},{9,15},{10,... | collective-permute-start | bytes 491528 | tf_op jit(solution)/shard_map/ppermute | solution.py:39
  61.9 8.8 %collective-permute-start.20 = (f32[2,2,16,8,128]{4,3,2,1,0:T(8,128)S(1)}, f32[2,2,16,8,128]{4,3,2,1,0:T(8,128)S(1)}, u32[]{:S(2)}, u32[]{:S(2)}) collective-permute-start(f32[2,2,16,8,128]{4,3,2,1,0:T(8,128)S(1)} %pad_maximum_fusion), channel_id=1, source_target_pairs={{0,30},{1,11},{2,28},{3,9},{4,26},{5,15},{6,24},{7,13},{8,22},{9,3... | collective-permute-start | bytes 786440 | tf_op jit(solution)/shard_map/ppermute | solution.py:39
  62.0 8.6 %collective-permute-start.21 = (f32[2,2,16,8,128]{4,3,2,1,0:T(8,128)S(1)}, f32[2,2,16,8,128]{4,3,2,1,0:T(8,128)S(1)}, u32[]{:S(2)}, u32[]{:S(2)}) collective-permute-start(f32[2,2,16,8,128]{4,3,2,1,0:T(8,128)S(1)} %pad_maximum_fusion.1), channel_id=1, source_target_pairs={{0,24},{1,9},{2,26},{3,11},{4,28},{5,13},{6,30},{7,15},{8,16},{9,1... | collective-permute-start | bytes 786440 | tf_op jit(solution)/shard_map/ppermute | solution.py:39
  70.2 11.2 %copy-start.3 = (f32[64]{0:T(128)S(1)}, f32[64]{0:T(128)}, u32[]{:S(2)}) copy-start(f32[64]{0:T(128)} %param.6) | copy-start | bytes 772
  70.3 5.3 %collective-permute-start.22 = (f32[2,2,16,8,128]{4,3,2,1,0:T(8,128)S(1)}, f32[2,2,16,8,128]{4,3,2,1,0:T(8,128)S(1)}, u32[]{:S(2)}, u32[]{:S(2)}) collective-permute-start(f32[2,2,16,8,128]{4,3,2,1,0:T(8,128)S(1)} %pad_maximum_fusion.2), channel_id=1, source_target_pairs={{0,6},{1,3},{2,4},{3,1},{4,2},{5,7},{6,0},{7,5},{8,14},{9,11},{10,... | collective-permute-start | bytes 786440 | tf_op jit(solution)/shard_map/ppermute | solution.py:39
  75.7 7.9 %collective-permute-start.23 = (f32[16,8,128]{2,1,0:T(8,128)S(1)}, f32[16,8,128]{2,1,0:T(8,128)S(1)}, u32[]{:S(2)}, u32[]{:S(2)}) collective-permute-start(f32[16,8,128]{2,1,0:T(8,128)S(1)} %get-tuple-element.105), channel_id=1, source_target_pairs={{0,128},{1,129},{2,130},{3,131},{4,132},{5,133},{6,134},{7,135},{8... | collective-permute-start | bytes 196616 | tf_op jit(solution)/shard_map/ppermute | solution.py:37
  75.8 7.8 %collective-permute-start.24 = (f32[16,8,128]{2,1,0:T(8,128)S(1)}, f32[16,8,128]{2,1,0:T(8,128)S(1)}, u32[]{:S(2)}, u32[]{:S(2)}) collective-permute-start(f32[16,8,128]{2,1,0:T(8,128)S(1)} %get-tuple-element.107), channel_id=1, source_target_pairs={{0,64},{1,65},{2,66},{3,67},{4,68},{5,69},{6,70},{7,71},{8,72},{9,... | collective-permute-start | bytes 196616 | tf_op jit(solution)/shard_map/ppermute | solution.py:37
  75.9 8.5 %collective-permute-start.25 = (f32[16,8,128]{2,1,0:T(8,128)S(1)}, f32[16,8,128]{2,1,0:T(8,128)S(1)}, u32[]{:S(2)}, u32[]{:S(2)}) collective-permute-start(f32[16,8,128]{2,1,0:T(8,128)S(1)} %get-tuple-element.106), channel_id=1, source_target_pairs={{0,192},{1,193},{2,194},{3,195},{4,196},{5,197},{6,198},{7,199},{8... | collective-permute-start | bytes 196616 | tf_op jit(solution)/shard_map/ppermute | solution.py:37

commit v6 on v5

--- a/solution.py
+++ b/solution.py
@@ -17,7 +17,7 @@
 GRANTS = (52, 44, 20, 20)
 
 RING4 = ((1, 3), (3, 1))
-RING8 = (1, 2, 6, 4)
+RING8 = (1, 2, 7, 5)
 Z_MASKS = [i * RING8[0] ^ j * RING8[1] ^ k * RING8[2] for i in (0, 1) for j in (0, 1) for k in (0, 1)]
 UNITS = ((0, 6), (6, 11), (11, 16))
 
@@ -39,9 +39,9 @@
     return lax.ppermute(value, "col", [(i, i ^ (RING4[i % 2][step] * unit)) for i in range(32)])
 
 
-def partial_kernel(chunk, to_sibling, pos, *refs):
+def partial_kernel(chunk, to_sibling, *refs):
     bit = 1 - pl.program_id(0)
-    z, core = pos[0], lax.rem(pos[1], 2)
+    z, core = lax.axis_index("row"), lax.rem(lax.axis_index("col"), 2)
     core = 1 - core if to_sibling else core
     xs, y = refs[:4], refs[4]
     if to_sibling:
@@ -52,7 +52,7 @@
     for place in range(8):
         mask = lax.rem(place + core, 8) ^ lax.rem(z + core, 8)
         high = lax.div(mask, 4)
-        slots.append(lax.rem(mask, 2) * 4 + (lax.rem(lax.div(mask, 2), 2) ^ high) * 2 + high)
+        slots.append((lax.rem(mask, 2) ^ high) * 4 + (lax.rem(lax.div(mask, 2), 2) ^ high) * 2 + high)
     for s in range(4):
         value = lax.dot_general(
             xs[s][...], y[...], (((0,), (0,)), ((), ())), preferred_element_type=jnp.float32
@@ -74,17 +74,18 @@
                     c[bit, s, slot, unit - UNITS[2][0]] = piece
 
 
-def partial(pos, x, y, chunk, grant, got=None):
+def partial(x, y, chunk, grant, got=None):
     to_sibling = got is None
     na, nb, nc = (to - start for start, to in UNITS)
 
     def block(s):
-        def index(step, pos):
-            core = lax.rem(pos[1], 2)
+        def index(step):
+            col = lax.axis_index("col")
+            core = lax.rem(col, 2)
             core = 1 - core if to_sibling else core
             first, second = 1 + 2 * core, 3 - 2 * core
-            xi = lax.div(pos[1], 8) ^ (first * (1 - step)) ^ (second * chunk)
-            yi = lax.rem(lax.div(pos[1], 2), 4) ^ (first * (s // 2)) ^ (second * (s % 2))
+            xi = lax.div(col, 8) ^ (first * (1 - step)) ^ (second * chunk)
+            yi = lax.rem(lax.div(col, 2), 4) ^ (first * (s // 2)) ^ (second * (s % 2))
             return (0, (xi * 4 + yi) * 2 + core)
 
         return pl.BlockSpec((512, 256), index)
@@ -97,25 +98,22 @@
     whole = pl.BlockSpec(memory_space=pltpu.VMEM)
     return pl.pallas_call(
         functools.partial(partial_kernel, chunk, to_sibling),
-        grid_spec=pltpu.PrefetchScalarGridSpec(
-            num_scalar_prefetch=1,
-            grid=(2,),
-            in_specs=[block(s) for s in range(4)]
-            + [pl.BlockSpec((512, 512), lambda step, pos: (0, 0))]
-            + ([] if to_sibling else [whole]),
-            out_specs=[whole] * len(shapes),
-        ),
+        grid=(2,),
+        in_specs=[block(s) for s in range(4)]
+        + [pl.BlockSpec((512, 512), lambda step: (0, 0))]
+        + ([] if to_sibling else [whole]),
+        out_specs=[whole] * len(shapes),
         out_shape=[pltpu.VMEM(s, jnp.float32) for s in shapes],
         compiler_params=pltpu.CompilerParams(vmem_limit_bytes=grant * MIB),
         cost_estimate=pl.CostEstimate(
             flops=2 * 512 * 512 * 2048, bytes_accessed=(7 if to_sibling else 11) * MIB, transcendentals=0
         ),
         name=("away" if to_sibling else "near") + str(chunk),
-    )(pos, x, x, x, x, y, *([] if to_sibling else [got]))
-
-
-def stats_kernel(pos, units, col_old, row_old, tile, stats):
-    z = pos[0]
+    )(x, x, x, x, y, *([] if to_sibling else [got]))
+
+
+def stats_kernel(units, col_old, row_old, tile, stats):
+    z = lax.axis_index("row")
     lane = lax.broadcasted_iota(jnp.int32, (8, 128), 1)
     sub = lax.broadcasted_iota(jnp.int32, (8, 128), 0)
     even = lane % 2 == 0
@@ -184,8 +182,8 @@
         load[to, 16:32] = tile[to, 16:32]
 
 
-def finish_kernel(pos, load, direction, row_new, col_new, scales, rows):
-    z = pos[0]
+def finish_kernel(load, direction, row_new, col_new, scales, rows):
+    z = lax.axis_index("row")
     lane = lax.broadcasted_iota(jnp.int32, (8, 128), 1)
     even = lane % 2 == 0
     upper = lane >= 64
@@ -218,16 +216,15 @@
 
 def on_device(activations, kv_grads, row_state, col_state):
     z = lax.axis_index("row").astype(jnp.int32)
-    pos = jnp.stack([z, lax.axis_index("col").astype(jnp.int32)])
     col_old = lax.dynamic_slice_in_dim(col_state, z * 32, 32, axis=1).T
     row_old = jnp.concatenate([row_state, row_state]).reshape(1, 128)
 
     x, y = activations, kv_grads
     na, nb, nc = (to - start for start, to in UNITS)
-    sent = [swap_cores(partial(pos, x, y, 1 - i, GRANTS[i])[0]) for i in (0, 1)]
+    sent = [swap_cores(partial(x, y, 1 - i, GRANTS[i])[0]) for i in (0, 1)]
     streams = [None, None]
     for i in (0, 1):
-        a, b_send, b_keep, c = partial(pos, x, y, 1 - i, GRANTS[2 + i], sent[i])
+        a, b_send, b_keep, c = partial(x, y, 1 - i, GRANTS[2 + i], sent[i])
         a = a.reshape(2, 2, 2, 2, 2, 2, na, 8, 128)
         b_send, b_keep = (v.reshape(2, 2, 2, 2, 2, nb, 8, 128) for v in (b_send, b_keep))
         c = c.reshape(2, 2, 2, 2, 2, 2, nc, 8, 128)
@@ -257,7 +254,7 @@
 
     tile, stats = pl.pallas_call(
         stats_kernel,
-        in_specs=[pl.BlockSpec(memory_space=pltpu.SMEM)] + [pl.BlockSpec(memory_space=pltpu.VMEM)] * 3,
+        in_specs=[pl.BlockSpec(memory_space=pltpu.VMEM)] * 3,
         out_specs=[pl.BlockSpec(memory_space=pltpu.VMEM)] * 2,
         out_shape=[
             pltpu.VMEM((8, 32, 128), jnp.float32),
@@ -265,7 +262,7 @@
         ],
         compiler_params=SMALL,
         name="stats",
-    )(pos, value, col_old, row_old)
+    )(value, col_old, row_old)
 
     stats = lax.all_to_all(stats, "col", 0, 0, tiled=True)
     load = pl.pallas_call(
@@ -280,7 +277,7 @@
 
     direction, row_new, col_new = pl.pallas_call(
         finish_kernel,
-        in_specs=[pl.BlockSpec(memory_space=pltpu.SMEM), pl.BlockSpec(memory_space=pltpu.VMEM)],
+        in_specs=[pl.BlockSpec(memory_space=pltpu.VMEM)],
         out_specs=[pl.BlockSpec(memory_space=pltpu.VMEM)] * 3,
         out_shape=[
             jax.ShapeDtypeStruct((64, 256), jnp.float32),
@@ -290,7 +287,7 @@
         scratch_shapes=[pltpu.VMEM((8, 128), jnp.float32)] * 2,
         compiler_params=SMALL,
         name="finish",
-    )(pos, load)
+    )(load)
     return (direction, row_new.reshape(64), col_new)
 
 

time: 113 us -> 109 us (0.965)
  Pallas kernels: 17.1 us -> 11.4 us
  waiting for transfers between devices: 25.6 us -> 23.5 us
  local copies, waits for them, and re-layouts: 0.61 us -> 2.59 us
  starting transfers between devices: 40.8 us -> 42.5 us
    pallas_call x4, Pallas kernels: 14.7 us -> 10.1 us  [partial(): pl.pallas_call(functools.partial(partial_kernel, chunk, to_sibling), grid...]
    ppermute x15, waiting for transfers between devices: 15.1 us -> 12.3 us  [along(): lax.ppermute(value, 'col', [(i, i ^ RING4[i % 2][step] * unit) for i in r...]
    unnamed x13, local copies, waits for them, and re-layouts: 0.12 us -> 2.09 us
    ppermute x9, starting transfers between devices: 18.1 us -> 19.9 us  [along(): return lax.ppermute(value, ('row', 'col'), pairs)]
    all_to_all x1, blocking collectives: 10.9 us -> 12.7 us  [on_device(): load = lax.all_to_all(load, 'row', 0, 0, tiled=True)]
    all_to_all x1, blocking collectives: 15.4 us -> 13.8 us  [on_device(): stats = lax.all_to_all(stats, 'col', 0, 0, tiled=True)]
  transfers between devices with their start and end apart: 26 -> 26, of which waited for: 11 -> 12; matrix products, arithmetic and copies ran while one was open for 1% -> 1% of each run, Pallas kernels for 9% -> 6%
where the time goes in v6:
time: 109 us; the launch traced here: 108 us
  starting transfers between devices  42.5 us (39%)
  blocking collectives  26.5 us (24%)
  waiting for transfers between devices  23.5 us (22%)
  Pallas kernels  11.4 us (10%)
  local copies, waits for them, and re-layouts  2.59 us (2%)
    ppermute x9, starting transfers between devices, along(): return lax.ppermute(value, ('row', 'col'), pairs)  19.9 us
    ppermute x15, starting transfers between devices, along(): lax.ppermute(value, 'col', [(i, i ^ RING4[i % 2][step] * unit) for i in r...  19 us
    all_to_all x1, blocking collectives, on_device(): stats = lax.all_to_all(stats, 'col', 0, 0, tiled=True)  13.8 us
    all_to_all x1, blocking collectives, on_device(): load = lax.all_to_all(load, 'row', 0, 0, tiled=True)  12.7 us
    ppermute x15, waiting for transfers between devices, along(): lax.ppermute(value, 'col', [(i, i ^ RING4[i % 2][step] * unit) for i in r...  12.3 us
    pallas_call x4, Pallas kernels, partial(): pl.pallas_call(functools.partial(partial_kernel, chunk, to_sibling), grid...  10.1 us
    ppermute x9, waiting for transfers between devices, along(): return lax.ppermute(value, ('row', 'col'), pairs)  7.25 us
    ppermute x2, waiting for transfers between devices, swap_cores(): return lax.ppermute(value, 'col', [(i, i ^ 1) for i in range(32)])  3.9 us
  transfers between devices with their start and end apart: 26, of which 12 were waited for; matrix products, arithmetic and copies ran while one was open for 1% of the time, Pallas kernels for 6%

profile of v6, /device:TPU:1, one launch (start us, length us, event | category | flops | bytes accessed | tf_op | source)
XLA Modules:
  0.0 108.4 jit_solution(2052251741903886198)
XLA Ops:
  0.7 3.2 %away1.1 = f32[2,4,8,16,8,128]{5,4,3,2,1,0:T(8,128)S(1)} custom-call(bf16[512,8192]{1,0:T(8,128)(2,1)} %refs_3_.7, bf16[512,8192]{1,0:T(8,128)(2,1)} %refs_3_.7, bf16[512,8192]{1,0:T(8,128)(2,1)} %refs_3_.7, bf16[512,8192]{1,0:T(8,128)(2,1)} %refs_3_.7, bf16[512,512]{1,0:T(8,128)(2,1)} %refs_4_.7), custom_call_target="tpu_custom_call" | custom-call | flops 1073741824 | bytes 7340032 | tf_op jit(solution)/shard_map/away1/pallas_call | solution.py:99
  3.9 2.0 %copy-done.2 = f32[2,4,8,16,8,128]{5,4,3,2,1,0:T(8,128)} copy-done((f32[2,4,8,16,8,128]{5,4,3,2,1,0:T(8,128)}, f32[2,4,8,16,8,128]{5,4,3,2,1,0:T(8,128)S(1)}, u32[]{:S(2)}) %copy-start.2) | copy-done | bytes 4194328
  5.8 3.2 %collective-permute-start.10 = (f32[2,4,8,16,8,128]{5,4,3,2,1,0:T(8,128)}, f32[2,4,8,16,8,128]{5,4,3,2,1,0:T(8,128)S(1)}, u32[]{:S(2)}, u32[]{:S(2)}) collective-permute-start(f32[2,4,8,16,8,128]{5,4,3,2,1,0:T(8,128)} %copy-done.2), channel_id=1, source_target_pairs={{0,1},{1,0},{2,3},{3,2},{4,5},{5,4},{6,7},{7,6},{8,9},{9,8},{10,11... | collective-permute-start | bytes 12582920 | tf_op jit(solution)/shard_map/ppermute | solution.py:26
  9.1 2.8 %away0.1 = f32[2,4,8,16,8,128]{5,4,3,2,1,0:T(8,128)S(1)} custom-call(bf16[512,8192]{1,0:T(8,128)(2,1)} %refs_3_.7, bf16[512,8192]{1,0:T(8,128)(2,1)} %refs_3_.7, bf16[512,8192]{1,0:T(8,128)(2,1)} %refs_3_.7, bf16[512,8192]{1,0:T(8,128)(2,1)} %refs_3_.7, bf16[512,512]{1,0:T(8,128)(2,1)S(1)} %copy-done.1), custom_call_target="tpu_custom_call" | custom-call | flops 1073741824 | bytes 7340032 | tf_op jit(solution)/shard_map/away0/pallas_call | solution.py:99
  11.9 0.3 collective-permute-start
  12.2 3.9 %collective-permute-done.10.refs_5_ = f32[2,4,8,16,8,128]{5,4,3,2,1,0:T(8,128)S(1)} collective-permute-done((f32[2,4,8,16,8,128]{5,4,3,2,1,0:T(8,128)}, f32[2,4,8,16,8,128]{5,4,3,2,1,0:T(8,128)S(1)}, u32[]{:S(2)}, u32[]{:S(2)}) %collective-permute-start.10) | collective-permute-done | bytes 4194336 | tf_op jit(solution)/shard_map/ppermute | solution.py:26
  16.1 2.1 %near1.1 = (f32[2,4,8,6,8,128]{5,4,3,2,1,0:T(8,128)S(1)}, f32[2,2,8,5,8,128]{5,4,3,2,1,0:T(8,128)S(1)}, f32[2,2,8,5,8,128]{5,4,3,2,1,0:T(8,128)S(1)}, f32[2,4,8,5,8,128]{5,4,3,2,1,0:T(8,128)S(1)}) custom-call(bf16[512,8192]{1,0:T(8,128)(2,1)S(1)} %bitcast.231, bf16[512,8192]{1,0:T(8,128)(2,1)S(1)} %bitcast.231, bf16[512,8192]{1,0:T(8,128)(2,1)S(1)} %bitcast.231, ...), custom_call_target="tpu_custom_call" | custom-call | flops 1073741824 | bytes 11534336 | tf_op jit(solution)/shard_map/near1/pallas_call | solution.py:99
  18.2 0.8 collective-permute-start.11
  19.1 5.7 %collective-permute-start.13 = (f32[2,2,2,2,2,5,8,128]{7,6,5,4,3,2,1,0:T(8,128)S(1)}, f32[2,2,2,2,2,5,8,128]{7,6,5,4,3,2,1,0:T(8,128)S(1)}, u32[]{:S(2)}, u32[]{:S(2)}) collective-permute-start(f32[2,2,2,2,2,5,8,128]{7,6,5,4,3,2,1,0:T(8,128)S(1)} %slice_bitcast_fusion), channel_id=1, source_target_pairs={{0,32},{1,225},{2,34},{3,227},{4,36},{5,229},{6,38},{7,231},{8,40}... | collective-permute-start | bytes 1966088 | tf_op jit(solution)/shard_map/ppermute | solution.py:37
  24.8 2.8 %collective-permute-start.12 = (f32[2,2,2,2,2,5,8,128]{7,6,5,4,3,1,2,0:T(8,128)S(1)}, f32[2,2,2,2,2,5,8,128]{7,6,5,4,3,1,2,0:T(8,128)S(1)}, u32[]{:S(2)}, u32[]{:S(2)}) collective-permute-start(f32[2,2,2,2,2,5,8,128]{7,6,5,4,3,1,2,0:T(8,128)S(1)} %copy.14), channel_id=1, source_target_pairs={{0,2},{1,7},{2,0},{3,5},{4,6},{5,3},{6,4},{7,1},{8,10},{9,15},{10,... | collective-permute-start | bytes 1966088 | tf_op jit(solution)/shard_map/ppermute | solution.py:39
  27.6 2.1 %near0.1 = (f32[2,4,8,6,8,128]{5,4,3,2,1,0:T(8,128)S(1)}, f32[2,2,8,5,8,128]{5,4,3,2,1,0:T(8,128)S(1)}, f32[2,2,8,5,8,128]{5,4,3,2,1,0:T(8,128)S(1)}, f32[2,4,8,5,8,128]{5,4,3,2,1,0:T(8,128)S(1)}) custom-call(bf16[512,8192]{1,0:T(8,128)(2,1)S(1)} %bitcast.231, bf16[512,8192]{1,0:T(8,128)(2,1)S(1)} %bitcast.231, bf16[512,8192]{1,0:T(8,128)(2,1)S(1)} %bitcast.231, ...), custom_call_target="tpu_custom_call" | custom-call | flops 1073741824 | bytes 11534336 | tf_op jit(solution)/shard_map/near0/pallas_call | solution.py:99
  29.8 0.3 collective-permute-start.1
  30.2 0.4 collective-permute-start.3
  30.7 2.0 %collective-permute-done.13 = f32[2,2,2,2,2,5,8,128]{7,6,5,4,3,2,1,0:T(8,128)S(1)} collective-permute-done((f32[2,2,2,2,2,5,8,128]{7,6,5,4,3,2,1,0:T(8,128)S(1)}, f32[2,2,2,2,2,5,8,128]{7,6,5,4,3,2,1,0:T(8,128)S(1)}, u32[]{:S(2)}, u32[]{:S(2)}) %collective-permute-start.13) | collective-permute-done | bytes 655392 | tf_op jit(solution)/shard_map/ppermute | solution.py:37
  32.7 2.7 %collective-permute-start.2 = (f32[2,2,2,2,2,5,8,128]{7,6,5,4,3,1,2,0:T(8,128)S(1)}, f32[2,2,2,2,2,5,8,128]{7,6,5,4,3,1,2,0:T(8,128)S(1)}, u32[]{:S(2)}, u32[]{:S(2)}) collective-permute-start(f32[2,2,2,2,2,5,8,128]{7,6,5,4,3,1,2,0:T(8,128)S(1)} %copy.8), channel_id=1, source_target_pairs={{0,2},{1,7},{2,0},{3,5},{4,6},{5,3},{6,4},{7,1},{8,10},{9,15},{10,... | collective-permute-start | bytes 1966088 | tf_op jit(solution)/shard_map/ppermute | solution.py:39
  35.5 0.1 collective-permute-done.12
  35.7 2.8 %collective-permute-start.14 = (f32[2,2,2,2,6,8,128]{6,5,4,3,2,1,0:T(8,128)S(1)}, f32[2,2,2,2,6,8,128]{6,5,4,3,2,1,0:T(8,128)S(1)}, u32[]{:S(2)}, u32[]{:S(2)}) collective-permute-start(f32[2,2,2,2,6,8,128]{6,5,4,3,2,1,0:T(8,128)S(1)} %get-tuple-element.80), channel_id=1, source_target_pairs={{0,2},{1,7},{2,0},{3,5},{4,6},{5,3},{6,4},{7,1},{8,10},{9,15},{10,... | collective-permute-start | bytes 1179656 | tf_op jit(solution)/shard_map/ppermute | solution.py:39
  38.5 0.3 collective-permute-start.16
  38.9 2.1 %collective-permute-done.3 = f32[2,2,2,2,2,5,8,128]{7,6,5,4,3,2,1,0:T(8,128)S(1)} collective-permute-done((f32[2,2,2,2,2,5,8,128]{7,6,5,4,3,2,1,0:T(8,128)S(1)}, f32[2,2,2,2,2,5,8,128]{7,6,5,4,3,2,1,0:T(8,128)S(1)}, u32[]{:S(2)}, u32[]{:S(2)}) %collective-permute-start.3) | collective-permute-done | bytes 655392 | tf_op jit(solution)/shard_map/ppermute | solution.py:37
  41.0 1.5 %collective-permute-start.15 = (f32[2,2,2,2,5,8,128]{6,5,4,3,2,1,0:T(8,128)S(1)}, f32[2,2,2,2,5,8,128]{6,5,4,3,2,1,0:T(8,128)S(1)}, u32[]{:S(2)}, u32[]{:S(2)}) collective-permute-start(f32[2,2,2,2,5,8,128]{6,5,4,3,2,1,0:T(8,128)S(1)} %get-tuple-element.74), channel_id=1, source_target_pairs={{0,32},{1,225},{2,34},{3,227},{4,36},{5,229},{6,38},{7,231},{8,40}... | collective-permute-start | bytes 983048 | tf_op jit(solution)/shard_map/ppermute | solution.py:37
  42.4 1.0 collective-permute-done.2
  43.5 2.8 %collective-permute-start.4 = (f32[2,2,2,2,6,8,128]{6,5,4,3,2,1,0:T(8,128)S(1)}, f32[2,2,2,2,6,8,128]{6,5,4,3,2,1,0:T(8,128)S(1)}, u32[]{:S(2)}, u32[]{:S(2)}) collective-permute-start(f32[2,2,2,2,6,8,128]{6,5,4,3,2,1,0:T(8,128)S(1)} %get-tuple-element.84), channel_id=1, source_target_pairs={{0,2},{1,7},{2,0},{3,5},{4,6},{5,3},{6,4},{7,1},{8,10},{9,15},{10,... | collective-permute-start | bytes 1179656 | tf_op jit(solution)/shard_map/ppermute | solution.py:39
  46.4 0.3 collective-permute-start.6
  46.8 2.8 %collective-permute-start.5 = (f32[2,2,2,2,5,8,128]{6,5,4,3,2,1,0:T(8,128)S(1)}, f32[2,2,2,2,5,8,128]{6,5,4,3,2,1,0:T(8,128)S(1)}, u32[]{:S(2)}, u32[]{:S(2)}) collective-permute-start(f32[2,2,2,2,5,8,128]{6,5,4,3,2,1,0:T(8,128)S(1)} %get-tuple-element.76), channel_id=1, source_target_pairs={{0,32},{1,225},{2,34},{3,227},{4,36},{5,229},{6,38},{7,231},{8,40}... | collective-permute-start | bytes 983048 | tf_op jit(solution)/shard_map/ppermute | solution.py:37
  49.6 1.1 %collective-permute-start.17 = (f32[2,2,2,6,8,128]{5,4,3,2,1,0:T(8,128)S(1)}, f32[2,2,2,6,8,128]{5,4,3,2,1,0:T(8,128)S(1)}, u32[]{:S(2)}, u32[]{:S(2)}) collective-permute-start(f32[2,2,2,6,8,128]{5,4,3,2,1,0:T(8,128)S(1)} %get-tuple-element.78), channel_id=1, source_target_pairs={{0,32},{1,225},{2,34},{3,227},{4,36},{5,229},{6,38},{7,231},{8,40}... | collective-permute-start | bytes 589832 | tf_op jit(solution)/shard_map/ppermute | solution.py:37
  50.7 2.8 %collective-permute-start.19 = (f32[2,2,2,5,8,128]{5,4,3,2,1,0:T(8,128)S(1)}, f32[2,2,2,5,8,128]{5,4,3,2,1,0:T(8,128)S(1)}, u32[]{:S(2)}, u32[]{:S(2)}) collective-permute-start(f32[2,2,2,5,8,128]{5,4,3,2,1,0:T(8,128)S(1)} %get-tuple-element.87), channel_id=1, source_target_pairs={{0,2},{1,7},{2,0},{3,5},{4,6},{5,3},{6,4},{7,1},{8,10},{9,15},{10,... | collective-permute-start | bytes 491528 | tf_op jit(solution)/shard_map/ppermute | solution.py:39
  53.5 0.1 collective-permute-done.6
  53.6 0.2 collective-permute-start.18
  53.8 0.2 collective-permute-done.5
  54.0 2.8 %collective-permute-start.7 = (f32[2,2,2,6,8,128]{5,4,3,2,1,0:T(8,128)S(1)}, f32[2,2,2,6,8,128]{5,4,3,2,1,0:T(8,128)S(1)}, u32[]{:S(2)}, u32[]{:S(2)}) collective-permute-start(f32[2,2,2,6,8,128]{5,4,3,2,1,0:T(8,128)S(1)} %get-tuple-element.82), channel_id=1, source_target_pairs={{0,32},{1,225},{2,34},{3,227},{4,36},{5,229},{6,38},{7,231},{8,40}... | collective-permute-start | bytes 589832 | tf_op jit(solution)/shard_map/ppermute | solution.py:37
  56.8 1.4 %collective-permute-start.9 = (f32[2,2,2,5,8,128]{5,4,3,2,1,0:T(8,128)S(1)}, f32[2,2,2,5,8,128]{5,4,3,2,1,0:T(8,128)S(1)}, u32[]{:S(2)}, u32[]{:S(2)}) collective-permute-start(f32[2,2,2,5,8,128]{5,4,3,2,1,0:T(8,128)S(1)} %get-tuple-element.91), channel_id=1, source_target_pairs={{0,2},{1,7},{2,0},{3,5},{4,6},{5,3},{6,4},{7,1},{8,10},{9,15},{10,... | collective-permute-start | bytes 491528 | tf_op jit(solution)/shard_map/ppermute | solution.py:39
  58.2 1.3 %collective-permute-start.8 = (f32[2,2,2,5,8,128]{5,4,3,2,1,0:T(8,128)S(1)}, f32[2,2,2,5,8,128]{5,4,3,2,1,0:T(8,128)S(1)}, u32[]{:S(2)}, u32[]{:S(2)}) collective-permute-start(f32[2,2,2,5,8,128]{5,4,3,2,1,0:T(8,128)S(1)} %get-tuple-element.90), channel_id=1, source_target_pairs={{0,8},{1,25},{2,10},{3,27},{4,12},{5,29},{6,14},{7,31},{8,0},{9,17... | collective-permute-start | bytes 491528 | tf_op jit(solution)/shard_map/ppermute | solution.py:39
  59.7 0.1 collective-permute-start.20
  59.8 0.5 collective-permute-start.21
  60.2 6.0 %collective-permute-done.9 = f32[2,2,2,5,8,128]{5,4,3,2,1,0:T(8,128)S(1)} collective-permute-done((f32[2,2,2,5,8,128]{5,4,3,2,1,0:T(8,128)S(1)}, f32[2,2,2,5,8,128]{5,4,3,2,1,0:T(8,128)S(1)}, u32[]{:S(2)}, u32[]{:S(2)}) %collective-permute-start.9) | collective-permute-done | bytes 163872 | tf_op jit(solution)/shard_map/ppermute | solution.py:39
  66.4 0.1 collective-permute-start.22
  66.6 0.1 copy.31
  66.7 0.3 collective-permute-done.21
  67.0 4.7 %collective-permute-done.22 = f32[2,2,16,8,128]{4,3,2,1,0:T(8,128)S(1)} collective-permute-done((f32[2,2,16,8,128]{4,3,2,1,0:T(8,128)S(1)}, f32[2,2,16,8,128]{4,3,2,1,0:T(8,128)S(1)}, u32[]{:S(2)}, u32[]{:S(2)}) %collective-permute-start.22) | collective-permute-done | bytes 262176 | tf_op jit(solution)/shard_map/ppermute | solution.py:39
  71.8 0.6 collective-permute-start.23
  72.4 5.1 %collective-permute-start.25 = (f32[16,8,128]{2,1,0:T(8,128)S(1)}, f32[16,8,128]{2,1,0:T(8,128)S(1)}, u32[]{:S(2)}, u32[]{:S(2)}) collective-permute-start(f32[16,8,128]{2,1,0:T(8,128)S(1)} %get-tuple-element.106), channel_id=1, source_target_pairs={{0,224},{1,161},{2,226},{3,163},{4,228},{5,165},{6,230},{7,167},{8... | collective-permute-start | bytes 196616 | tf_op jit(solution)/shard_map/ppermute | solution.py:37
  77.6 0.3 collective-permute-done.24
  77.9 2.6 %collective-permute-done.25 = f32[16,8,128]{2,1,0:T(8,128)S(1)} collective-permute-done((f32[16,8,128]{2,1,0:T(8,128)S(1)}, f32[16,8,128]{2,1,0:T(8,128)S(1)}, u32[]{:S(2)}, u32[]{:S(2)}) %collective-permute-start.25) | collective-permute-done | bytes 65568 | tf_op jit(solution)/shard_map/ppermute | solution.py:37
  80.6 0.3 stats.1
  80.9 13.8 %all_to_all.10.stats = f32[32,8,128]{2,1,0:T(8,128)S(1)} all-to-all(f32[32,8,128]{2,1,0:T(8,128)S(1)} %get-tuple-element.61), channel_id=1, replica_groups=mesh['row'=8,'col'=32] {'col'}, dimensions={0} | all-to-all | bytes 262144 | tf_op jit(solution)/shard_map/all_to_all | solution.py:267
  94.7 0.1 pack.1
  94.8 12.7 %all_to_all.11.load = f32[8,32,128]{2,1,0:T(8,128)S(1)} all-to-all(f32[8,32,128]{2,1,0:T(8,128)S(1)} %pack.1), channel_id=1, replica_groups=mesh['row'=8,'col'=32] {'row'}, dimensions={0} | all-to-all | bytes 262144 | tf_op jit(solution)/shard_map/all_to_all | solution.py:276
  107.5 0.9 finish.1
  (59 shorter events, 1.6 us)
Async XLA Ops:
  0.6 65.8 %copy-start = (f32[2,256]{1,0:T(2,128)S(1)}, f32[2,256]{1,0:T(2,128)}, u32[]{:S(2)}) copy-start(f32[2,256]{1,0:T(2,128)} %param.7) | copy-start | bytes 6148
  0.6 8.4 %copy-start.1 = (bf16[512,512]{1,0:T(8,128)(2,1)S(1)}, bf16[512,512]{1,0:T(8,128)(2,1)}, u32[]{:S(2)}) copy-start(bf16[512,512]{1,0:T(8,128)(2,1)} %refs_4_.7) | copy-start | bytes 1572868
  0.7 15.4 %slice-start = ((s8[8388608]{0:T(1024)(128)(4,1)}), s8[4194304]{0:T(1024)(128)(4,1)S(1)}, s32[]{:S(2)}) async-start(s8[8388608]{0:T(1024)(128)(4,1)} %bitcast.230), calls=%async_computation.2 | async-start | bytes 8388608
  3.9 2.0 %copy-start.2 = (f32[2,4,8,16,8,128]{5,4,3,2,1,0:T(8,128)}, f32[2,4,8,16,8,128]{5,4,3,2,1,0:T(8,128)S(1)}, u32[]{:S(2)}) copy-start(f32[2,4,8,16,8,128]{5,4,3,2,1,0:T(8,128)S(1)} %away1.1) | copy-start | bytes 12582916
  5.8 10.2 %slice-start.1 = ((s8[8388608]{0:T(1024)(128)(4,1)}), s8[4194304]{0:T(1024)(128)(4,1)S(1)}, s32[]{:S(2)}) async-start(s8[8388608]{0:T(1024)(128)(4,1)} %bitcast.230), calls=%async_computation.3 | async-start | bytes 8388608
  5.8 10.2 %collective-permute-start.10 = (f32[2,4,8,16,8,128]{5,4,3,2,1,0:T(8,128)}, f32[2,4,8,16,8,128]{5,4,3,2,1,0:T(8,128)S(1)}, u32[]{:S(2)}, u32[]{:S(2)}) collective-permute-start(f32[2,4,8,16,8,128]{5,4,3,2,1,0:T(8,128)} %copy-done.2), channel_id=1, source_target_pairs={{0,1},{1,0},{2,3},{3,2},{4,5},{5,4},{6,7},{7,6},{8,9},{9,8},{10,11... | collective-permute-start | bytes 12582920 | tf_op jit(solution)/shard_map/ppermute | solution.py:26
  11.9 15.8 %collective-permute-start = (f32[2,4,8,16,8,128]{5,4,3,2,1,0:T(8,128)S(1)}, f32[2,4,8,16,8,128]{5,4,3,2,1,0:T(8,128)S(1)}, u32[]{:S(2)}, u32[]{:S(2)}) collective-permute-start(f32[2,4,8,16,8,128]{5,4,3,2,1,0:T(8,128)S(1)} %away0.1), channel_id=1, source_target_pairs={{0,1},{1,0},{2,3},{3,2},{4,5},{5,4},{6,7},{7,6},{8,9},{9,8},{10,11... | collective-permute-start | bytes 12582920 | tf_op jit(solution)/shard_map/ppermute | solution.py:26
  18.2 17.4 %collective-permute-start.11 = (f32[2,2,2,2,2,6,8,128]{7,6,5,4,3,2,1,0:T(8,128)S(1)}, f32[2,2,2,2,2,6,8,128]{7,6,5,4,3,2,1,0:T(8,128)S(1)}, u32[]{:S(2)}, u32[]{:S(2)}) collective-permute-start(f32[2,2,2,2,2,6,8,128]{7,6,5,4,3,2,1,0:T(8,128)S(1)} %bitcast.246), channel_id=1, source_target_pairs={{0,8},{1,25},{2,10},{3,27},{4,12},{5,29},{6,14},{7,31},{8,0},{9,17... | collective-permute-start | bytes 2359304 | tf_op jit(solution)/shard_map/ppermute | solution.py:39
  19.1 13.6 %collective-permute-start.13 = (f32[2,2,2,2,2,5,8,128]{7,6,5,4,3,2,1,0:T(8,128)S(1)}, f32[2,2,2,2,2,5,8,128]{7,6,5,4,3,2,1,0:T(8,128)S(1)}, u32[]{:S(2)}, u32[]{:S(2)}) collective-permute-start(f32[2,2,2,2,2,5,8,128]{7,6,5,4,3,2,1,0:T(8,128)S(1)} %slice_bitcast_fusion), channel_id=1, source_target_pairs={{0,32},{1,225},{2,34},{3,227},{4,36},{5,229},{6,38},{7,231},{8,40}... | collective-permute-start | bytes 1966088 | tf_op jit(solution)/shard_map/ppermute | solution.py:37
  24.8 10.8 %collective-permute-start.12 = (f32[2,2,2,2,2,5,8,128]{7,6,5,4,3,1,2,0:T(8,128)S(1)}, f32[2,2,2,2,2,5,8,128]{7,6,5,4,3,1,2,0:T(8,128)S(1)}, u32[]{:S(2)}, u32[]{:S(2)}) collective-permute-start(f32[2,2,2,2,2,5,8,128]{7,6,5,4,3,1,2,0:T(8,128)S(1)} %copy.14), channel_id=1, source_target_pairs={{0,2},{1,7},{2,0},{3,5},{4,6},{5,3},{6,4},{7,1},{8,10},{9,15},{10,... | collective-permute-start | bytes 1966088 | tf_op jit(solution)/shard_map/ppermute | solution.py:39
  29.8 13.7 %collective-permute-start.1 = (f32[2,2,2,2,2,6,8,128]{7,6,5,4,3,2,1,0:T(8,128)S(1)}, f32[2,2,2,2,2,6,8,128]{7,6,5,4,3,2,1,0:T(8,128)S(1)}, u32[]{:S(2)}, u32[]{:S(2)}) collective-permute-start(f32[2,2,2,2,2,6,8,128]{7,6,5,4,3,2,1,0:T(8,128)S(1)} %bitcast.245), channel_id=1, source_target_pairs={{0,8},{1,25},{2,10},{3,27},{4,12},{5,29},{6,14},{7,31},{8,0},{9,17... | collective-permute-start | bytes 2359304 | tf_op jit(solution)/shard_map/ppermute | solution.py:39
  30.2 10.7 %collective-permute-start.3 = (f32[2,2,2,2,2,5,8,128]{7,6,5,4,3,2,1,0:T(8,128)S(1)}, f32[2,2,2,2,2,5,8,128]{7,6,5,4,3,2,1,0:T(8,128)S(1)}, u32[]{:S(2)}, u32[]{:S(2)}) collective-permute-start(f32[2,2,2,2,2,5,8,128]{7,6,5,4,3,2,1,0:T(8,128)S(1)} %slice_bitcast_fusion.1), channel_id=1, source_target_pairs={{0,32},{1,225},{2,34},{3,227},{4,36},{5,229},{6,38},{7,231},{8,40}... | collective-permute-start | bytes 1966088 | tf_op jit(solution)/shard_map/ppermute | solution.py:37
  32.7 10.7 %collective-permute-start.2 = (f32[2,2,2,2,2,5,8,128]{7,6,5,4,3,1,2,0:T(8,128)S(1)}, f32[2,2,2,2,2,5,8,128]{7,6,5,4,3,1,2,0:T(8,128)S(1)}, u32[]{:S(2)}, u32[]{:S(2)}) collective-permute-start(f32[2,2,2,2,2,5,8,128]{7,6,5,4,3,1,2,0:T(8,128)S(1)} %copy.8), channel_id=1, source_target_pairs={{0,2},{1,7},{2,0},{3,5},{4,6},{5,3},{6,4},{7,1},{8,10},{9,15},{10,... | collective-permute-start | bytes 1966088 | tf_op jit(solution)/shard_map/ppermute | solution.py:39
  35.7 13.8 %collective-permute-start.14 = (f32[2,2,2,2,6,8,128]{6,5,4,3,2,1,0:T(8,128)S(1)}, f32[2,2,2,2,6,8,128]{6,5,4,3,2,1,0:T(8,128)S(1)}, u32[]{:S(2)}, u32[]{:S(2)}) collective-permute-start(f32[2,2,2,2,6,8,128]{6,5,4,3,2,1,0:T(8,128)S(1)} %get-tuple-element.80), channel_id=1, source_target_pairs={{0,2},{1,7},{2,0},{3,5},{4,6},{5,3},{6,4},{7,1},{8,10},{9,15},{10,... | collective-permute-start | bytes 1179656 | tf_op jit(solution)/shard_map/ppermute | solution.py:39
  38.5 8.2 %collective-permute-start.16 = (f32[2,2,2,2,5,8,128]{6,5,4,3,2,1,0:T(8,128)S(1)}, f32[2,2,2,2,5,8,128]{6,5,4,3,2,1,0:T(8,128)S(1)}, u32[]{:S(2)}, u32[]{:S(2)}) collective-permute-start(f32[2,2,2,2,5,8,128]{6,5,4,3,2,1,0:T(8,128)S(1)} %get-tuple-element.65), channel_id=1, source_target_pairs={{0,8},{1,25},{2,10},{3,27},{4,12},{5,29},{6,14},{7,31},{8,0},{9,17... | collective-permute-start | bytes 983048 | tf_op jit(solution)/shard_map/ppermute | solution.py:39
  41.0 8.5 %collective-permute-start.15 = (f32[2,2,2,2,5,8,128]{6,5,4,3,2,1,0:T(8,128)S(1)}, f32[2,2,2,2,5,8,128]{6,5,4,3,2,1,0:T(8,128)S(1)}, u32[]{:S(2)}, u32[]{:S(2)}) collective-permute-start(f32[2,2,2,2,5,8,128]{6,5,4,3,2,1,0:T(8,128)S(1)} %get-tuple-element.74), channel_id=1, source_target_pairs={{0,32},{1,225},{2,34},{3,227},{4,36},{5,229},{6,38},{7,231},{8,40}... | collective-permute-start | bytes 983048 | tf_op jit(solution)/shard_map/ppermute | solution.py:37
  43.5 10.4 %collective-permute-start.4 = (f32[2,2,2,2,6,8,128]{6,5,4,3,2,1,0:T(8,128)S(1)}, f32[2,2,2,2,6,8,128]{6,5,4,3,2,1,0:T(8,128)S(1)}, u32[]{:S(2)}, u32[]{:S(2)}) collective-permute-start(f32[2,2,2,2,6,8,128]{6,5,4,3,2,1,0:T(8,128)S(1)} %get-tuple-element.84), channel_id=1, source_target_pairs={{0,2},{1,7},{2,0},{3,5},{4,6},{5,3},{6,4},{7,1},{8,10},{9,15},{10,... | collective-permute-start | bytes 1179656 | tf_op jit(solution)/shard_map/ppermute | solution.py:39
  46.4 7.2 %collective-permute-start.6 = (f32[2,2,2,2,5,8,128]{6,5,4,3,2,1,0:T(8,128)S(1)}, f32[2,2,2,2,5,8,128]{6,5,4,3,2,1,0:T(8,128)S(1)}, u32[]{:S(2)}, u32[]{:S(2)}) collective-permute-start(f32[2,2,2,2,5,8,128]{6,5,4,3,2,1,0:T(8,128)S(1)} %get-tuple-element.67), channel_id=1, source_target_pairs={{0,8},{1,25},{2,10},{3,27},{4,12},{5,29},{6,14},{7,31},{8,0},{9,17... | collective-permute-start | bytes 983048 | tf_op jit(solution)/shard_map/ppermute | solution.py:39
  46.8 7.2 %collective-permute-start.5 = (f32[2,2,2,2,5,8,128]{6,5,4,3,2,1,0:T(8,128)S(1)}, f32[2,2,2,2,5,8,128]{6,5,4,3,2,1,0:T(8,128)S(1)}, u32[]{:S(2)}, u32[]{:S(2)}) collective-permute-start(f32[2,2,2,2,5,8,128]{6,5,4,3,2,1,0:T(8,128)S(1)} %get-tuple-element.76), channel_id=1, source_target_pairs={{0,32},{1,225},{2,34},{3,227},{4,36},{5,229},{6,38},{7,231},{8,40}... | collective-permute-start | bytes 983048 | tf_op jit(solution)/shard_map/ppermute | solution.py:37
  49.6 10.0 %collective-permute-start.17 = (f32[2,2,2,6,8,128]{5,4,3,2,1,0:T(8,128)S(1)}, f32[2,2,2,6,8,128]{5,4,3,2,1,0:T(8,128)S(1)}, u32[]{:S(2)}, u32[]{:S(2)}) collective-permute-start(f32[2,2,2,6,8,128]{5,4,3,2,1,0:T(8,128)S(1)} %get-tuple-element.78), channel_id=1, source_target_pairs={{0,32},{1,225},{2,34},{3,227},{4,36},{5,229},{6,38},{7,231},{8,40}... | collective-permute-start | bytes 589832 | tf_op jit(solution)/shard_map/ppermute | solution.py:37
  50.7 7.5 %collective-permute-start.19 = (f32[2,2,2,5,8,128]{5,4,3,2,1,0:T(8,128)S(1)}, f32[2,2,2,5,8,128]{5,4,3,2,1,0:T(8,128)S(1)}, u32[]{:S(2)}, u32[]{:S(2)}) collective-permute-start(f32[2,2,2,5,8,128]{5,4,3,2,1,0:T(8,128)S(1)} %get-tuple-element.87), channel_id=1, source_target_pairs={{0,2},{1,7},{2,0},{3,5},{4,6},{5,3},{6,4},{7,1},{8,10},{9,15},{10,... | collective-permute-start | bytes 491528 | tf_op jit(solution)/shard_map/ppermute | solution.py:39
  53.6 5.9 %collective-permute-start.18 = (f32[2,2,2,5,8,128]{5,4,3,2,1,0:T(8,128)S(1)}, f32[2,2,2,5,8,128]{5,4,3,2,1,0:T(8,128)S(1)}, u32[]{:S(2)}, u32[]{:S(2)}) collective-permute-start(f32[2,2,2,5,8,128]{5,4,3,2,1,0:T(8,128)S(1)} %get-tuple-element.86), channel_id=1, source_target_pairs={{0,8},{1,25},{2,10},{3,27},{4,12},{5,29},{6,14},{7,31},{8,0},{9,17... | collective-permute-start | bytes 491528 | tf_op jit(solution)/shard_map/ppermute | solution.py:39
  54.0 12.2 %collective-permute-start.7 = (f32[2,2,2,6,8,128]{5,4,3,2,1,0:T(8,128)S(1)}, f32[2,2,2,6,8,128]{5,4,3,2,1,0:T(8,128)S(1)}, u32[]{:S(2)}, u32[]{:S(2)}) collective-permute-start(f32[2,2,2,6,8,128]{5,4,3,2,1,0:T(8,128)S(1)} %get-tuple-element.82), channel_id=1, source_target_pairs={{0,32},{1,225},{2,34},{3,227},{4,36},{5,229},{6,38},{7,231},{8,40}... | collective-permute-start | bytes 589832 | tf_op jit(solution)/shard_map/ppermute | solution.py:37
  56.8 9.4 %collective-permute-start.9 = (f32[2,2,2,5,8,128]{5,4,3,2,1,0:T(8,128)S(1)}, f32[2,2,2,5,8,128]{5,4,3,2,1,0:T(8,128)S(1)}, u32[]{:S(2)}, u32[]{:S(2)}) collective-permute-start(f32[2,2,2,5,8,128]{5,4,3,2,1,0:T(8,128)S(1)} %get-tuple-element.91), channel_id=1, source_target_pairs={{0,2},{1,7},{2,0},{3,5},{4,6},{5,3},{6,4},{7,1},{8,10},{9,15},{10,... | collective-permute-start | bytes 491528 | tf_op jit(solution)/shard_map/ppermute | solution.py:39
  58.2 8.0 %collective-permute-start.8 = (f32[2,2,2,5,8,128]{5,4,3,2,1,0:T(8,128)S(1)}, f32[2,2,2,5,8,128]{5,4,3,2,1,0:T(8,128)S(1)}, u32[]{:S(2)}, u32[]{:S(2)}) collective-permute-start(f32[2,2,2,5,8,128]{5,4,3,2,1,0:T(8,128)S(1)} %get-tuple-element.90), channel_id=1, source_target_pairs={{0,8},{1,25},{2,10},{3,27},{4,12},{5,29},{6,14},{7,31},{8,0},{9,17... | collective-permute-start | bytes 491528 | tf_op jit(solution)/shard_map/ppermute | solution.py:39
  59.7 7.0 %collective-permute-start.20 = (f32[2,2,16,8,128]{4,3,2,1,0:T(8,128)S(1)}, f32[2,2,16,8,128]{4,3,2,1,0:T(8,128)S(1)}, u32[]{:S(2)}, u32[]{:S(2)}) collective-permute-start(f32[2,2,16,8,128]{4,3,2,1,0:T(8,128)S(1)} %pad_maximum_fusion), channel_id=1, source_target_pairs={{0,30},{1,11},{2,28},{3,9},{4,26},{5,15},{6,24},{7,13},{8,22},{9,3... | collective-permute-start | bytes 786440 | tf_op jit(solution)/shard_map/ppermute | solution.py:39
  59.8 7.2 %collective-permute-start.21 = (f32[2,2,16,8,128]{4,3,2,1,0:T(8,128)S(1)}, f32[2,2,16,8,128]{4,3,2,1,0:T(8,128)S(1)}, u32[]{:S(2)}, u32[]{:S(2)}) collective-permute-start(f32[2,2,16,8,128]{4,3,2,1,0:T(8,128)S(1)} %pad_maximum_fusion.1), channel_id=1, source_target_pairs={{0,24},{1,9},{2,26},{3,11},{4,28},{5,13},{6,30},{7,15},{8,16},{9,1... | collective-permute-start | bytes 786440 | tf_op jit(solution)/shard_map/ppermute | solution.py:39
  66.3 11.2 %copy-start.3 = (f32[64]{0:T(128)S(1)}, f32[64]{0:T(128)}, u32[]{:S(2)}) copy-start(f32[64]{0:T(128)} %param.6) | copy-start | bytes 772
  66.4 5.3 %collective-permute-start.22 = (f32[2,2,16,8,128]{4,3,2,1,0:T(8,128)S(1)}, f32[2,2,16,8,128]{4,3,2,1,0:T(8,128)S(1)}, u32[]{:S(2)}, u32[]{:S(2)}) collective-permute-start(f32[2,2,16,8,128]{4,3,2,1,0:T(8,128)S(1)} %pad_maximum_fusion.2), channel_id=1, source_target_pairs={{0,6},{1,3},{2,4},{3,1},{4,2},{5,7},{6,0},{7,5},{8,14},{9,11},{10,... | collective-permute-start | bytes 786440 | tf_op jit(solution)/shard_map/ppermute | solution.py:39
  71.8 5.8 %collective-permute-start.23 = (f32[16,8,128]{2,1,0:T(8,128)S(1)}, f32[16,8,128]{2,1,0:T(8,128)S(1)}, u32[]{:S(2)}, u32[]{:S(2)}) collective-permute-start(f32[16,8,128]{2,1,0:T(8,128)S(1)} %get-tuple-element.105), channel_id=1, source_target_pairs={{0,160},{1,97},{2,162},{3,99},{4,164},{5,101},{6,166},{7,103},{8,1... | collective-permute-start | bytes 196616 | tf_op jit(solution)/shard_map/ppermute | solution.py:37
  72.4 5.5 %collective-permute-start.24 = (f32[16,8,128]{2,1,0:T(8,128)S(1)}, f32[16,8,128]{2,1,0:T(8,128)S(1)}, u32[]{:S(2)}, u32[]{:S(2)}) collective-permute-start(f32[16,8,128]{2,1,0:T(8,128)S(1)} %get-tuple-element.107), channel_id=1, source_target_pairs={{0,64},{1,65},{2,66},{3,67},{4,68},{5,69},{6,70},{7,71},{8,72},{9,... | collective-permute-start | bytes 196616 | tf_op jit(solution)/shard_map/ppermute | solution.py:37
  72.4 8.2 %collective-permute-start.25 = (f32[16,8,128]{2,1,0:T(8,128)S(1)}, f32[16,8,128]{2,1,0:T(8,128)S(1)}, u32[]{:S(2)}, u32[]{:S(2)}) collective-permute-start(f32[16,8,128]{2,1,0:T(8,128)S(1)} %get-tuple-element.106), channel_id=1, source_target_pairs={{0,224},{1,161},{2,226},{3,163},{4,228},{5,165},{6,230},{7,167},{8... | collective-permute-start | bytes 196616 | tf_op jit(solution)/shard_map/ppermute | solution.py:37
